TPU v7x, 256 devices: a whole 4x4x8 slice. The times are simulated.
256 devices in a mesh: dp: 4 (over y), fsdp: 64 (over x, z, core).
Axes of the slice: x: 4, y: 4, z: 8, core: 2. Of those that a mesh axis runs over, the one named last changes fastest.
Arguments:
- grads: bfloat16 [4, 256, 512, 512], P('dp', None, 'fsdp'), may hold values from -1.25 to 1.25
- stats_left: float32 [512, 512, 512], P(('dp', 'fsdp'))
- stats_right: float32 [512, 512, 512], P(('dp', 'fsdp'))
- precond_left: bfloat16 [512, 512, 512], P(('dp', 'fsdp'))
- precond_right: bfloat16 [512, 512, 512], P(('dp', 'fsdp'))
- owner_table: int32 [256], replicated, may hold values from 0 to 127, as said below
- block_counts: int32 [4, 64], P('dp', 'fsdp'), may hold values from 0 to 2, as said below
Outputs:
- new_left: float32 [512, 512, 512], P(('dp', 'fsdp'))
- new_right: float32 [512, 512, 512], P(('dp', 'fsdp'))
- update: bfloat16 [256, 512, 512], P(None, 'fsdp')
Inputs may be any that keep to these rules, and one draw needn't show every extreme that they name: `owner_table`: within each group of 64 consecutive blocks no two blocks share an entry; the slots that a group uses on one device are 0 to one less than that device's count; in each group max(1, 8) devices own 2 blocks each, and no other device owns more than 1. block_counts[d, o] is the number of blocks of group d whose entry names device o.
All inputs are finite; a program needn't handle non-finite values.
Results may differ from a plain program's by a relative error of at most 0.017.
Values may be sent and summed in bfloat16 or wider, within the bound.
No kernel may reach another device: no remote copies, remote signals or barrier semaphores. Data moves between devices by JAX's collectives and lax.ppermute only.
A program may use at most 64 MiB of HBM per device.

v0:
```python
import jax
import jax.numpy as jnp
from jax import lax
from jax.sharding import PartitionSpec as P

BETA = 0.9
EPS = 1e-06


def owner_statistics(blocks, stats_left, stats_right, live_slots):
    gram_left = jnp.einsum("sik,sjk->sij", blocks, blocks, preferred_element_type=jnp.float32)
    gram_right = jnp.einsum("ski,skj->sij", blocks, blocks, preferred_element_type=jnp.float32)
    keep = live_slots[:, None, None]
    new_left = jnp.where(keep, BETA * stats_left + (1.0 - BETA) * gram_left, stats_left)
    new_right = jnp.where(keep, BETA * stats_right + (1.0 - BETA) * gram_right, stats_right)
    return (new_left, new_right)


def precondition(blocks, precond_left, precond_right):
    left_part = jnp.einsum(
        "sik,skj->sij", precond_left, blocks, preferred_element_type=jnp.float32
    ).astype(jnp.bfloat16)
    direction = jnp.einsum(
        "sik,skj->sij", left_part, precond_right, preferred_element_type=jnp.float32
    )
    power = jnp.mean(direction * direction, axis=(1, 2), keepdims=True)
    return (direction * lax.rsqrt(power + EPS)).astype(jnp.bfloat16)


def return_rows(scaled, selector, fsdp_size, slot_count):
    pieces = lax.all_to_all(scaled[None], "fsdp", split_axis=2, concat_axis=0, tiled=True)
    flat_pieces = pieces.reshape(fsdp_size * slot_count, pieces.shape[2], pieces.shape[3])
    mine = jnp.einsum(
        "kj,jrc->krc", selector, flat_pieces, preferred_element_type=jnp.float32
    ).astype(jnp.bfloat16)
    return lax.all_gather(mine, "dp", axis=0, tiled=True)


def local(grads, stats_left, stats_right, precond_left, precond_right, owner_table, block_counts):
    fsdp_size = lax.axis_size("fsdp")
    replicas = lax.axis_size("dp")
    slot_count = stats_left.shape[0]
    all_blocks = grads.shape[1]
    row_count = grads.shape[2]
    width = grads.shape[3]
    group_blocks = all_blocks // replicas
    slot_ids = jnp.arange(fsdp_size * slot_count, dtype=jnp.int32)
    group_index = lax.axis_index("dp")
    group_table = lax.dynamic_slice_in_dim(owner_table, group_index * group_blocks, group_blocks)
    selector = (group_table[:, None] == slot_ids[None, :]).astype(jnp.bfloat16)
    live_slots = jnp.arange(slot_count, dtype=jnp.int32) < block_counts.reshape(())
    summed = lax.psum_scatter(
        grads[0].astype(jnp.float32).astype(jnp.bfloat16), "dp", scatter_dimension=0, tiled=True
    ).astype(jnp.float32)
    mean_grad = (summed * (1.0 / replicas)).astype(jnp.bfloat16)
    outgoing = jnp.einsum(
        "kj,krc->jrc", selector, mean_grad, preferred_element_type=jnp.float32
    ).astype(jnp.bfloat16)
    outgoing = outgoing.reshape(fsdp_size, slot_count, row_count, width)
    arrived = lax.all_to_all(outgoing, "fsdp", split_axis=0, concat_axis=2, tiled=True)
    blocks = arrived[0]
    new_left, new_right = owner_statistics(blocks, stats_left, stats_right, live_slots)
    update = return_rows(
        precondition(blocks, precond_left, precond_right), selector, fsdp_size, slot_count
    )
    return (new_left, new_right, update)


def solution(mesh):
    in_specs = (
        P("dp", None, "fsdp", None),
        P(("dp", "fsdp"), None, None),
        P(("dp", "fsdp"), None, None),
        P(("dp", "fsdp"), None, None),
        P(("dp", "fsdp"), None, None),
        P(),
        P("dp", "fsdp"),
    )
    out_specs = (
        P(("dp", "fsdp"), None, None),
        P(("dp", "fsdp"), None, None),
        P(None, "fsdp", None),
    )
    return jax.shard_map(local, mesh=mesh, in_specs=in_specs, out_specs=out_specs, check_vma=False)
```

profile of v0, /device:TPU:1, one launch (start us, length us, event | category | flops | bytes accessed | tf_op | source)
XLA Modules:
  0.0 173.4 jit_solution(606737208921192615)
XLA Ops:
  7.2 0.0 copy-start
  7.2 0.0 copy-start.3
  7.2 0.0 reduce-scatter.2.cloned.1.call-start
  7.2 0.7 reduce-scatter.2.cloned.1.call-update
  7.9 0.0 all-gather.2.cloned.1.call-start
  8.0 0.0 copy-done.3
  8.0 0.1 dynamic_slice.3
  8.1 38.6 %reduce-scatter.2.cloned.1.call-done = bf16[64,8,512]{2,1,0:T(8,128)(2,1)} async-done(((bf16[256,8,512]{2,1,0:T(8,128)(2,1)}), bf16[64,8,512]{2,1,0:T(8,128)(2,1)}) %reduce-scatter.2.cloned.1.call-update) | async-done | bytes 524304 | tf_op jit(solution)/shard_map/reduce_scatter | solution.py:52
  46.7 1.1 multiply_convert_fusion.1
  47.8 0.6 convolution_convert_fusion
  48.4 0.4 reshape.31
  48.8 1.1 copy.16
  50.0 0.0 copy-start.2
  50.0 39.1 %all_to_all.30 = bf16[64,2,8,512]{3,1,2,0:T(2,128)(2,1)S(1)} all-to-all(bf16[64,2,8,512]{3,1,2,0:T(2,128)(2,1)S(1)} %copy.16), channel_id=1, replica_groups=mesh['dp'=4,'fsdp'=64] {'fsdp'}, dimensions={0} | all-to-all | bytes 2097152 | tf_op jit(solution)/shard_map/all_to_all | solution.py:60
  89.1 0.0 copy-done
  89.1 0.0 copy-done.2
  89.1 2.6 %multiply_reduce_fusion = (f32[2]{0:T(128)S(1)}, f32[2,512,512]{2,1,0:T(8,128)}) fusion(bf16[2,512,512]{2,1,0:T(8,128)(2,1)S(1)} %copy-done, bf16[2,512,512]{2,1,0:T(8,128)(2,1)S(1)} %copy-done.2, bf16[1,2,64,8,512]{4,1,3,2,0:T(2,128)(2,1)S(1)} %bitcast.33), kind=kOutput, calls=%fused_computation.1 | convolution fusion | flops 1075314688 | bytes 5242888 | tf_op jit(solution)/shard_map/sik,skj->sij/dot_general | solution.py:23
  91.7 1.9 %fusion.1 = bf16[1,2,512,512]{3,2,1,0:T(8,128)(2,1)S(1)} fusion(f32[2,512,512]{2,1,0:T(8,128)} %get-tuple-element.10, f32[2]{0:T(128)S(1)} %add_rsqrt_fusion), kind=kLoop, calls=%fused_computation.8 | loop fusion | flops 1048576 | bytes 3145736 | tf_op jit(solution)/shard_map/broadcast_in_dim | solution.py:31
  93.6 1.1 copy.19
  94.7 34.5 %all_to_all.31 = bf16[1,2,512,512]{3,1,0,2:T(2,128)(2,1)S(1)} all-to-all(bf16[1,2,512,512]{3,1,0,2:T(2,128)(2,1)S(1)} %copy.19), channel_id=1, replica_groups=mesh['dp'=4,'fsdp'=64] {'fsdp'}, dimensions={2} | all-to-all | bytes 2097152 | tf_op jit(solution)/shard_map/all_to_all | solution.py:31
  129.2 1.8 %copy.41 = bf16[1,2,64,8,512]{4,1,2,3,0:T(2,128)(2,1)} copy(bf16[1,2,64,8,512]{4,1,3,2,0:T(2,128)(2,1)S(1)} %bitcast.36) | data formatting | bytes 2097152 | tf_op jit(solution)/shard_map/all_to_all | solution.py:31
  131.0 1.5 reshape.32
  132.5 1.1 convolution_convert_fusion.2
  133.6 0.0 all-gather.2.cloned.1.call-update
  134.3 0.0 copy-start.1
  134.3 3.9 %add_select_fusion = f32[2,512,512]{2,1,0:T(8,128)} fusion(f32[2,512,512]{2,1,0:T(8,128)} %param.9, pred[2]{0:T(512)(128)(4,1)S(1)} %iota_compare_fusion.1, bf16[1,2,64,8,512]{4,1,3,2,0:T(2,128)(2,1)S(1)} %bitcast.34), kind=kOutput, calls=%fused_computation.2 | convolution fusion | flops 538968064 | bytes 5242882 | tf_op jit(solution)/shard_map/ski,skj->sij/dot_general | solution.py:12
  138.3 0.0 copy-done.1
  138.3 2.3 %add_select_fusion.1 = f32[2,512,512]{2,1,0:T(8,128)} fusion(f32[2,512,512]{2,1,0:T(8,128)S(1)} %copy-done.1, pred[2]{0:T(512)(128)(4,1)S(1)} %iota_compare_fusion.1, bf16[1,2,64,8,512]{4,1,3,2,0:T(2,128)(2,1)S(1)} %bitcast.35), kind=kOutput, calls=%fused_computation.3 | convolution fusion | flops 538968064 | bytes 5242882 | tf_op jit(solution)/shard_map/sik,sjk->sij/dot_general | solution.py:11
  140.5 22.0 %all-gather.2.cloned.1.call-done = bf16[256,8,512]{2,0,1:T(8,128)(2,1)} async-done(((bf16[64,8,512]{2,0,1:T(8,128)(2,1)}), bf16[256,8,512]{2,0,1:T(8,128)(2,1)}) %all-gather.2.cloned.1.call-update) | async-done | bytes 2097168 | tf_op jit(solution)/shard_map/all_gather | solution.py:36
  162.5 4.1 %copy.21 = bf16[256,8,512]{2,1,0:T(8,128)(2,1)} copy(bf16[256,8,512]{2,0,1:T(8,128)(2,1)} %all-gather.2.cloned.1.call-done) | data formatting | bytes 4194304
  (2 shorter events, 0.0 us)
Async XLA Ops:
  7.2 81.9 %copy-start = (bf16[2,512,512]{2,1,0:T(8,128)(2,1)S(1)}, bf16[2,512,512]{2,1,0:T(8,128)(2,1)}, u32[]{:S(2)}) copy-start(bf16[2,512,512]{2,1,0:T(8,128)(2,1)} %param.11) | copy-start | bytes 3145732
  7.2 0.8 copy-start.3
  7.2 39.5 %reduce-scatter.2.cloned.1.call-start = ((), (), s32[]{:S(2)}) async-start(), calls=%async_computation.3 | async-start | bytes 2621440 | tf_op jit(solution)/shard_map/reduce_scatter | solution.py:52
  7.9 154.6 %all-gather.2.cloned.1.call-start = ((), (), s32[]{:S(2)}) async-start(), calls=%async_computation.4 | async-start | bytes 2621440 | tf_op jit(solution)/shard_map/all_gather | solution.py:36
  50.0 39.1 %copy-start.2 = (bf16[2,512,512]{2,1,0:T(8,128)(2,1)S(1)}, bf16[2,512,512]{2,1,0:T(8,128)(2,1)}, u32[]{:S(2)}) copy-start(bf16[2,512,512]{2,1,0:T(8,128)(2,1)} %param.10) | copy-start | bytes 3145732
  134.3 3.9 %copy-start.1 = (f32[2,512,512]{2,1,0:T(8,128)S(1)}, f32[2,512,512]{2,1,0:T(8,128)}, u32[]{:S(2)}) copy-start(f32[2,512,512]{2,1,0:T(8,128)} %param.8) | copy-start | bytes 6291460
Sparse Core Ops, SparseCore 0:
  10.6 36.0 reduce-scatter.1
  133.8 28.6 all-gather.1
where the time goes:
time: 174 us; the launch traced here: 173 us
  blocking collectives  73.6 us (42%)
  waiting for transfers between devices  61.3 us (35%)
  between operations  14.8 us (9%)
  matrix products  10.5 us (6%)
  local copies, waits for them, and re-layouts  10.1 us (6%)
  other arithmetic  3.05 us (2%)
    all_to_all x1, blocking collectives, local(): lax.all_to_all(outgoing, 'fsdp', split_axis=0, concat_axis=2, tiled=True)  39.1 us
    reduce_scatter x1, waiting for transfers between devices, local(): lax.psum_scatter(grads[0].astype(jnp.float32).astype(jnp.bfloat16), 'dp',...  38.6 us
    all_to_all x1, blocking collectives, return_rows(): lax.all_to_all(scaled[None], 'fsdp', split_axis=2, concat_axis=0, tiled=T...  34.5 us
    all_gather x1, waiting for transfers between devices, return_rows(): return lax.all_gather(mine, 'dp', axis=0, tiled=True)  22 us
    unnamed x9, local copies, waits for them, and re-layouts  4.1 us
    dot_general x1, matrix products, owner_statistics(): jnp.einsum('ski,skj->sij', blocks, blocks, preferred_element_type=jnp.flo...  3.92 us
  transfers between devices with their start and end apart: 2, of which 2 were waited for; matrix products, arithmetic and copies ran while one was open for 4% of the time, Pallas kernels for 0%

commit v1 on v0

v1 whole, which is shorter than its diff:
```python
import jax
import jax.numpy as jnp
from jax import lax
from jax.experimental import pallas as pl
from jax.experimental.pallas import tpu as pltpu
from jax.sharding import PartitionSpec as P

BETA = 0.9
EPS = 1e-06
BF16 = jnp.bfloat16
F32 = jnp.float32
SECOND = 8
LIST = 16

VMEM = pl.BlockSpec(memory_space=pltpu.VMEM)
SMEM = pl.BlockSpec(memory_space=pltpu.SMEM)
PARAMS = pltpu.CompilerParams(vmem_limit_bytes=32 * 1024 * 1024)


def shape(*dims, dtype=BF16):
    return jax.ShapeDtypeStruct(dims, dtype)


def call(kernel, outs, scalars, arrays, name, out_specs=None):
    return pl.pallas_call(
        kernel,
        out_shape=outs,
        in_specs=[SMEM] * len(scalars) + [VMEM] * len(arrays),
        out_specs=[VMEM] * len(outs) if out_specs is None else out_specs,
        compiler_params=PARAMS,
        name=name,
    )(*scalars, *arrays)


def split_lists(table, place, grads, replicas, group):
    rows, width = grads.shape[1:]

    def kernel(table_ref, place_ref, grads_ref, first_ref, second_ref, *outs):
        for g in range(replicas):
            in_first = jnp.int32(0)
            in_second = jnp.int32(0)
            for b in range(group):
                odd = table_ref[g * group + b] & 1
                first_ref[g * group + in_first] = b
                second_ref[g * LIST + in_second] = b
                in_first = in_first + (1 - odd)
                in_second = in_second + odd
        for k in range(replicas):
            g = lax.rem(place_ref[0] + k, replicas)
            for i in range(SECOND):
                outs[k][i] = grads_ref[g * group + second_ref[g * LIST + i]]

    outs = [shape(replicas * group, dtype=jnp.int32), shape(replicas * LIST, dtype=jnp.int32)]
    outs += [shape(SECOND, rows, width)] * replicas
    return call(
        kernel, outs, [table, place], [grads], "split", [SMEM, SMEM] + [VMEM] * replicas
    )


def sort_first(first, place, grads, replicas, group):
    rows, width = grads.shape[1:]
    count = group - SECOND

    def kernel(first_ref, place_ref, grads_ref, *outs):
        for k in range(replicas):
            g = lax.rem(place_ref[0] + k, replicas)

            def step(j, _, k=k, g=g):
                outs[k][j] = grads_ref[g * group + first_ref[g * group + j]]
                return 0

            lax.fori_loop(0, count, step, 0, unroll=8)

    return call(
        kernel, [shape(count, rows, width)] * replicas, [first, place], [grads], "sort_first"
    )


def place_mean(table, blocks, stride, count, place, terms, devices, group, name):
    rows, width = terms[0].shape[1:]
    scale = 1.0 / len(terms)

    def kernel(table_ref, blocks_ref, place_ref, *refs):
        out = refs[-1]
        out[...] = jnp.zeros(out.shape, BF16)
        g = place_ref[0]

        def step(j, _):
            owner = table_ref[g * group + blocks_ref[g * stride + j]] >> 1
            total = refs[0][j].astype(F32)
            for term in refs[1:-1]:
                total = total + term[j].astype(F32)
            out[owner] = (total * scale).astype(BF16)
            return 0

        lax.fori_loop(0, count, step, 0, unroll=8)

    return call(kernel, [shape(devices, rows, width)], [table, blocks, place], terms, name)[0]


def precondition(grad, left, right, slot, name):
    size = grad.shape[0]

    def kernel(grad_ref, left_ref, right_ref, out_ref):
        part = jnp.dot(left_ref[0], grad_ref[...], preferred_element_type=F32).astype(BF16)
        direction = jnp.dot(part, right_ref[0], preferred_element_type=F32)
        power = jnp.sum(direction * direction) * (1.0 / (size * size))
        out_ref[...] = (direction * lax.rsqrt(power + EPS)).astype(BF16)

    whole = pl.BlockSpec((size, size), lambda i: (0, 0))
    one = pl.BlockSpec((1, size, size), lambda i: (slot, 0, 0))
    return pl.pallas_call(
        kernel,
        out_shape=shape(size, size),
        grid=(1,),
        in_specs=[whole, one, one],
        out_specs=whole,
        compiler_params=PARAMS,
        name=name,
    )(grad, left, right)


def pick_rows(table, blocks, stride, count, place, pieces, group, name):
    rows, width = pieces.shape[1:]

    def kernel(table_ref, blocks_ref, place_ref, pieces_ref, out):
        g = place_ref[0]

        def step(j, _):
            out[j] = pieces_ref[table_ref[g * group + blocks_ref[g * stride + j]] >> 1]
            return 0

        lax.fori_loop(0, count, step, 0, unroll=8)

    return call(kernel, [shape(count, rows, width)], [table, blocks, place], [pieces], name)[0]


def assemble(first, second, place, firsts, seconds, group):
    replicas = len(firsts)
    rows, width = firsts[0].shape[1:]
    count = group - SECOND

    def kernel(place_ref, first_ref, second_ref, *refs):
        out = refs[-1]
        for k in range(replicas):

            @pl.when(pl.program_id(0) == k)
            def _(k=k):
                g = lax.rem(place_ref[0] + (replicas - k), replicas)

                def step(j, _):
                    out[first_ref[g * group + j]] = refs[k][j]
                    return 0

                lax.fori_loop(0, count, step, 0, unroll=8)
                for i in range(SECOND):
                    out[second_ref[g * LIST + i]] = refs[replicas + k][i]

    whole = lambda count: pl.BlockSpec((count, rows, width), lambda i, *_: (0, 0, 0))
    return pl.pallas_call(
        kernel,
        out_shape=shape(replicas * group, rows, width),
        grid_spec=pltpu.PrefetchScalarGridSpec(
            num_scalar_prefetch=3,
            grid=(replicas,),
            in_specs=[whole(count)] * replicas + [whole(SECOND)] * replicas,
            out_specs=pl.BlockSpec(
                (group, rows, width),
                lambda i, place_ref, *_: (lax.rem(place_ref[0] + (replicas - i), replicas), 0, 0),
            ),
        ),
        compiler_params=PARAMS,
        name="assemble",
    )(place, first, second, *firsts, *seconds)


def shifted(arrays, replicas):
    return [arrays[0]] + [
        lax.ppermute(arrays[k], "dp", [(i, (i + k) % replicas) for i in range(replicas)])
        for k in range(1, replicas)
    ]


def new_statistics(counts, grad_first, grad_second, stats_left, stats_right, parts=2):
    size = stats_left.shape[1]
    tile = size // parts

    def kernel(counts_ref, first_ref, second_ref, left_ref, right_ref, new_left_ref, new_right_ref):
        t = pl.program_id(1)
        for slot, grad_ref in enumerate((first_ref, second_ref)):

            @pl.when(pl.program_id(0) == slot)
            def _(slot=slot, grad_ref=grad_ref):
                live = counts_ref[0] > slot
                for p in range(parts):

                    @pl.when(t == p)
                    def _(p=p):
                        grad = grad_ref[...]
                        span = slice(p * tile, (p + 1) * tile)
                        gram_left = lax.dot_general(
                            grad[span], grad, (((1,), (1,)), ((), ())), preferred_element_type=F32
                        )
                        gram_right = lax.dot_general(
                            grad[:, span], grad, (((0,), (0,)), ((), ())), preferred_element_type=F32
                        )
                        old_left, old_right = left_ref[0], right_ref[0]
                        new_left_ref[0] = jnp.where(
                            live, BETA * old_left + (1.0 - BETA) * gram_left, old_left
                        )
                        new_right_ref[0] = jnp.where(
                            live, BETA * old_right + (1.0 - BETA) * gram_right, old_right
                        )

    whole = pl.BlockSpec((size, size), lambda s, t: (0, 0))
    part = pl.BlockSpec((1, tile, size), lambda s, t: (s, t, 0))
    return pl.pallas_call(
        kernel,
        out_shape=[shape(*stats_left.shape, dtype=F32)] * 2,
        grid=(2, parts),
        in_specs=[SMEM, whole, whole, part, part],
        out_specs=[part, part],
        compiler_params=PARAMS,
        cost_estimate=pl.CostEstimate(
            flops=8 * size**3, bytes_accessed=16 * 2 * size * size, transcendentals=0
        ),
        name="statistics",
    )(counts, grad_first, grad_second, stats_left, stats_right)


def local(grads, stats_left, stats_right, precond_left, precond_right, owner_table, block_counts):
    devices = lax.axis_size("fsdp")
    replicas = lax.axis_size("dp")
    blocks, rows, width = grads.shape[1:]
    size = stats_left.shape[1]
    group = blocks // replicas
    count = group - SECOND
    place = lax.axis_index("dp").astype(jnp.int32).reshape(1)
    mine = grads[0]

    first, second, *second_terms = split_lists(owner_table, place, mine, replicas, group)
    second_terms = shifted(second_terms, replicas)
    first_terms = shifted(sort_first(first, place, mine, replicas, group), replicas)
    second_out = place_mean(
        owner_table, second, LIST, SECOND, place, second_terms, devices, group, "mean_second"
    )
    second_in = lax.all_to_all(second_out, "fsdp", 0, 0, tiled=True)
    first_out = place_mean(
        owner_table, first, group, count, place, first_terms, devices, group, "mean_first"
    )
    first_in = lax.all_to_all(first_out, "fsdp", 0, 0, tiled=True)

    grad_first = first_in.reshape(size, size)
    grad_second = second_in.reshape(size, size)
    scaled_second = precondition(grad_second, precond_left, precond_right, 1, "direction_second")
    scaled_first = precondition(grad_first, precond_left, precond_right, 0, "direction_first")

    first_back = lax.all_to_all(
        scaled_first.reshape(devices, rows, width), "fsdp", 0, 0, tiled=True
    )
    first_rows = pick_rows(
        owner_table, first, group, count, place, first_back, group, "pick_first"
    )
    first_all = shifted([first_rows] * replicas, replicas)
    scaled_second, first_rows = lax.optimization_barrier((scaled_second, first_rows))
    second_back = lax.all_to_all(
        scaled_second.reshape(devices, rows, width), "fsdp", 0, 0, tiled=True
    )
    second_rows = pick_rows(
        owner_table, second, LIST, SECOND, place, second_back, group, "pick_second"
    )
    second_all = shifted([second_rows] * replicas, replicas)
    update = assemble(first, second, place, first_all, second_all, group)

    new_left, new_right = new_statistics(
        block_counts.reshape(1), grad_first, grad_second, stats_left, stats_right
    )
    return (new_left, new_right, update)


def solution(mesh):
    in_specs = (
        P("dp", None, "fsdp", None),
        P(("dp", "fsdp"), None, None),
        P(("dp", "fsdp"), None, None),
        P(("dp", "fsdp"), None, None),
        P(("dp", "fsdp"), None, None),
        P(),
        P("dp", "fsdp"),
    )
    out_specs = (
        P(("dp", "fsdp"), None, None),
        P(("dp", "fsdp"), None, None),
        P(None, "fsdp", None),
    )
    return jax.shard_map(local, mesh=mesh, in_specs=in_specs, out_specs=out_specs, check_vma=False)
```

time: 174 us -> 153 us (0.88); the launches traced: 173 us -> 150 us
  blocking collectives: 73.6 us -> 0 us
  starting transfers between devices: 0.08 us -> 49 us
  Pallas kernels: 0 us -> 17.2 us
  waiting for transfers between devices: 61.3 us -> 75.1 us
  between operations: 14.8 us -> 1.47 us
  matrix products: 10.5 us -> 0 us
  local copies, waits for them, and re-layouts: 10.1 us -> 7 us
  other arithmetic: 3.05 us -> 0 us
    all_to_all x2 -> x0, blocking collectives: 73.6 us -> none  [the longest x1 39.1 us: local(): lax.all_to_all(outgoing, 'fsdp', split_axis=0, concat_axis=2, tiled=True)]
    all_to_all x0 -> x4, waiting for transfers between devices: none -> 52.8 us  [the longest x1 15.4 us: local(): second_in = lax.all_to_all(second_out, 'fsdp', 0, 0, tiled=True)]
    reduce_scatter x1 -> x0, waiting for transfers between devices: 38.6 us -> none  [local(): lax.psum_scatter(grads[0].astype(jnp.float32).astype(jnp.bfloat16), 'dp',...]
    all_to_all x0 -> x4, starting transfers between devices: none -> 32.2 us  [the longest x1 13 us: local(): first_in = lax.all_to_all(first_out, 'fsdp', 0, 0, tiled=True)]
    ppermute x0 -> x12, waiting for transfers between devices: none -> 22.3 us  [shifted(): lax.ppermute(arrays[k], 'dp', [(i, (i + k) % replicas) for i in range(rep...]
    all_gather x1 -> x0, waiting for transfers between devices: 22 us -> none  [return_rows(): return lax.all_gather(mine, 'dp', axis=0, tiled=True)]
    pallas_call x0 -> x10, Pallas kernels: none -> 17.2 us  [the longest x6 7.65 us: call(): pl.pallas_call(kernel, out_shape=outs, in_specs=[SMEM] * len(scalars) + [...]
    ppermute x0 -> x12, starting transfers between devices: none -> 16.8 us  [shifted(): lax.ppermute(arrays[k], 'dp', [(i, (i + k) % replicas) for i in range(rep...]
  transfers between devices with their start and end apart: 2 -> 16, of which waited for: 2 -> 11; matrix products, arithmetic and copies ran while one was open for 4% -> 0% of each run, Pallas kernels for 0% -> 5%
where the time goes in v1:
time: 153 us; the launch traced here: 150 us
  waiting for transfers between devices  75.1 us (49%)
  starting transfers between devices  49 us (32%)
  Pallas kernels  17.2 us (11%)
  local copies, waits for them, and re-layouts  7 us (5%)
    ppermute x12, waiting for transfers between devices, shifted(): lax.ppermute(arrays[k], 'dp', [(i, (i + k) % replicas) for i in range(rep...  22.3 us
    ppermute x12, starting transfers between devices, shifted(): lax.ppermute(arrays[k], 'dp', [(i, (i + k) % replicas) for i in range(rep...  16.8 us
    all_to_all x1, waiting for transfers between devices, local(): second_in = lax.all_to_all(second_out, 'fsdp', 0, 0, tiled=True)  15.4 us
    all_to_all x1, waiting for transfers between devices, local(): lax.all_to_all(scaled_first.reshape(devices, rows, width), 'fsdp', 0, 0,...  15.3 us
    all_to_all x1, waiting for transfers between devices, local(): lax.all_to_all(scaled_second.reshape(devices, rows, width), 'fsdp', 0, 0,...  13.4 us
    all_to_all x1, starting transfers between devices, local(): first_in = lax.all_to_all(first_out, 'fsdp', 0, 0, tiled=True)  13 us
    all_to_all x1, waiting for transfers between devices, local(): first_in = lax.all_to_all(first_out, 'fsdp', 0, 0, tiled=True)  8.73 us
    pallas_call x6, Pallas kernels, call(): pl.pallas_call(kernel, out_shape=outs, in_specs=[SMEM] * len(scalars) + [...  7.65 us
  transfers between devices with their start and end apart: 16, of which 11 were waited for; matrix products, arithmetic and copies ran while one was open for 0% of the time, Pallas kernels for 5%

profile of v1, /device:TPU:1, one launch (start us, length us, event | category | flops | bytes accessed | tf_op | source)
XLA Modules:
  0.0 149.8 jit_solution(18342104634134330882)
XLA Ops:
  0.6 1.6 %copy-done = bf16[1,256,8,512]{3,2,1,0:T(8,128)(2,1)S(1)} copy-done((bf16[1,256,8,512]{3,2,1,0:T(8,128)(2,1)S(1)}, bf16[1,256,8,512]{3,2,1,0:T(8,128)(2,1)}, u32[]{:S(2)}) %copy-start) | copy-done | bytes 2097176
  2.2 0.7 copy-done.11
  2.9 2.0 %split.1 = (s32[256]{0:T(256)S(1)}, s32[64]{0:T(128)S(1)}, bf16[8,8,512]{2,1,0:T(8,128)(2,1)S(1)}, bf16[8,8,512]{2,1,0:T(8,128)(2,1)S(1)}, bf16[8,8,512]{2,1,0:T...) custom-call(s32[256]{0:T(256)S(1)} %copy-done.11, s32[1]{0:T(128)} %bitcast.1.place_ref, bf16[256,8,512]{2,1,0:T(8,128)(2,1)S(1)} %bitcast.8), custom_call_target="tpu_custom_call" | custom-call | tf_op jit(solution)/shard_map/split/pallas_call | solution.py:25
  5.0 1.0 sort_first.1
  6.0 0.0 copy-start.12
  6.0 2.2 %collective-permute-start = (bf16[56,8,512]{2,1,0:T(8,128)(2,1)S(1)}, bf16[56,8,512]{2,1,0:T(8,128)(2,1)S(1)}, u32[]{:S(2)}, u32[]{:S(2)}) collective-permute-start(bf16[56,8,512]{2,1,0:T(8,128)(2,1)S(1)} %get-tuple-element.18), channel_id=1, source_target_pairs={{0,64},{64,128},{128,192},{192,0},{1,65},{65,129},{129,193},{193,1... | collective-permute-start | bytes 1376264 | tf_op jit(solution)/shard_map/ppermute | solution.py:179
  8.2 2.6 %collective-permute-start.1 = (bf16[56,8,512]{2,1,0:T(8,128)(2,1)S(1)}, bf16[56,8,512]{2,1,0:T(8,128)(2,1)S(1)}, u32[]{:S(2)}, u32[]{:S(2)}) collective-permute-start(bf16[56,8,512]{2,1,0:T(8,128)(2,1)S(1)} %get-tuple-element.19), channel_id=1, source_target_pairs={{0,128},{64,192},{128,0},{192,64},{1,129},{65,193},{129,1},{193,65... | collective-permute-start | bytes 1376264 | tf_op jit(solution)/shard_map/ppermute | solution.py:179
  10.8 1.1 collective-permute-start.2
  11.9 6.0 %collective-permute-done.refs_1_ = bf16[56,8,512]{2,1,0:T(8,128)(2,1)S(1)} collective-permute-done((bf16[56,8,512]{2,1,0:T(8,128)(2,1)S(1)}, bf16[56,8,512]{2,1,0:T(8,128)(2,1)S(1)}, u32[]{:S(2)}, u32[]{:S(2)}) %collective-permute-start) | collective-permute-done | bytes 458784 | tf_op jit(solution)/shard_map/ppermute | solution.py:179
  17.9 12.7 %collective-permute-done.1.refs_2_ = bf16[56,8,512]{2,1,0:T(8,128)(2,1)S(1)} collective-permute-done((bf16[56,8,512]{2,1,0:T(8,128)(2,1)S(1)}, bf16[56,8,512]{2,1,0:T(8,128)(2,1)S(1)}, u32[]{:S(2)}, u32[]{:S(2)}) %collective-permute-start.1) | collective-permute-done | bytes 458784 | tf_op jit(solution)/shard_map/ppermute | solution.py:179
  30.6 1.7 %mean_first.1 = bf16[64,8,512]{2,1,0:T(8,128)(2,1)} custom-call(s32[256]{0:T(256)S(1)} %copy-done.11, s32[256]{0:T(256)S(1)} %get-tuple-element.16.first_ref.blocks_ref, s32[1]{0:T(128)} %bitcast.1.place_ref, bf16[56,8,512]{2,1,0:T(8,128)(2,1)S(1)} %get-tuple-element.17.refs_0_, bf16[56,8,512]{2,1,0:T(8,128)(2,1)S(1)} %collective-permute-done.refs_1_, ...), custom_call_target="tpu_custom_call" | custom-call | tf_op jit(solution)/shard_map/mean_first/pallas_call | solution.py:25
  32.3 13.0 %all-to-all-start = ((bf16[64,8,512]{2,1,0:T(8,128)(2,1)}), bf16[64,8,512]{2,1,0:T(8,128)(2,1)S(1)}, u32[]{:S(2)}, u32[]{:S(2)}) async-start(bf16[64,8,512]{2,1,0:T(8,128)(2,1)} %mean_first.1), calls=%async_computation | async-start | bytes 1048576 | tf_op jit(solution)/shard_map/all_to_all | solution.py:251
  45.3 1.0 collective-permute-start.3
  46.4 2.1 %collective-permute-start.4 = (bf16[8,8,512]{2,1,0:T(8,128)(2,1)S(1)}, bf16[8,8,512]{2,1,0:T(8,128)(2,1)S(1)}, u32[]{:S(2)}, u32[]{:S(2)}) collective-permute-start(bf16[8,8,512]{2,1,0:T(8,128)(2,1)S(1)} %get-tuple-element.24), channel_id=1, source_target_pairs={{0,128},{64,192},{128,0},{192,64},{1,129},{65,193},{129,1},{193,65... | collective-permute-start | bytes 196616 | tf_op jit(solution)/shard_map/ppermute | solution.py:179
  48.5 1.3 collective-permute-start.5
  49.8 0.3 collective-permute-done.3.refs_1_
  50.0 1.9 %collective-permute-done.4.refs_2_ = bf16[8,8,512]{2,1,0:T(8,128)(2,1)S(1)} collective-permute-done((bf16[8,8,512]{2,1,0:T(8,128)(2,1)S(1)}, bf16[8,8,512]{2,1,0:T(8,128)(2,1)S(1)}, u32[]{:S(2)}, u32[]{:S(2)}) %collective-permute-start.4) | collective-permute-done | bytes 65568 | tf_op jit(solution)/shard_map/ppermute | solution.py:179
  51.9 0.6 collective-permute-done.5.refs_3_
  52.5 0.6 mean_second.1
  53.1 0.8 copy-done.6
  53.9 8.7 %all-to-all-done = bf16[64,8,512]{2,1,0:T(8,128)(2,1)S(1)} async-done(((bf16[64,8,512]{2,1,0:T(8,128)(2,1)}), bf16[64,8,512]{2,1,0:T(8,128)(2,1)S(1)}, u32[]{:S(2)}, u32[]{:S(2)}) %all-to-all-start) | async-done | bytes 524320 | tf_op jit(solution)/shard_map/all_to_all | solution.py:251
  62.6 6.3 %all-to-all-start.1 = ((bf16[64,8,512]{2,1,0:T(8,128)(2,1)}), bf16[64,8,512]{2,1,0:T(8,128)(2,1)S(1)}, u32[]{:S(2)}, u32[]{:S(2)}) async-start(bf16[64,8,512]{2,1,0:T(8,128)(2,1)} %copy-done.6), calls=%async_computation.1 | async-start | bytes 1048576 | tf_op jit(solution)/shard_map/all_to_all | solution.py:247
  68.9 1.1 direction_first.1
  70.1 0.0 copy-start.8
  70.1 0.8 copy-done.8
  70.9 15.4 %all-to-all-done.1 = bf16[64,8,512]{2,1,0:T(8,128)(2,1)S(1)} async-done(((bf16[64,8,512]{2,1,0:T(8,128)(2,1)}), bf16[64,8,512]{2,1,0:T(8,128)(2,1)S(1)}, u32[]{:S(2)}, u32[]{:S(2)}) %all-to-all-start.1) | async-done | bytes 524320 | tf_op jit(solution)/shard_map/all_to_all | solution.py:247
  86.3 6.5 %all-to-all-start.2 = ((bf16[64,8,512]{2,1,0:T(8,128)(2,1)}), bf16[64,8,512]{2,1,0:T(8,128)(2,1)}, u32[]{:S(2)}, u32[]{:S(2)}) async-start(bf16[64,8,512]{2,1,0:T(8,128)(2,1)} %bitcast.15), calls=%async_computation.2 | async-start | bytes 1048576 | tf_op jit(solution)/shard_map/all_to_all | solution.py:258
  92.7 1.1 direction_second.1
  93.8 0.0 copy-start.7
  93.9 0.8 copy-done.7
  94.6 15.3 %all-to-all-done.2.pieces_ref = bf16[64,8,512]{2,1,0:T(8,128)(2,1)} async-done(((bf16[64,8,512]{2,1,0:T(8,128)(2,1)}), bf16[64,8,512]{2,1,0:T(8,128)(2,1)}, u32[]{:S(2)}, u32[]{:S(2)}) %all-to-all-start.2) | async-done | bytes 524320 | tf_op jit(solution)/shard_map/all_to_all | solution.py:258
  110.0 1.2 pick_first.1.refs_0_
  111.2 0.0 copy-start.9
  111.2 0.8 copy-done.9
  112.0 6.5 %all-to-all-start.3 = ((bf16[64,8,512]{2,1,0:T(8,128)(2,1)}), bf16[64,8,512]{2,1,0:T(8,128)(2,1)}, u32[]{:S(2)}, u32[]{:S(2)}) async-start(bf16[64,8,512]{2,1,0:T(8,128)(2,1)} %bitcast.14), calls=%async_computation.3 | async-start | bytes 1048576 | tf_op jit(solution)/shard_map/all_to_all | solution.py:266
  118.4 2.0 %collective-permute-start.8 = (bf16[56,8,512]{2,1,0:T(8,128)(2,1)}, bf16[56,8,512]{2,1,0:T(8,128)(2,1)}, u32[]{:S(2)}, u32[]{:S(2)}) collective-permute-start(bf16[56,8,512]{2,1,0:T(8,128)(2,1)} %copy-done.9), channel_id=1, source_target_pairs={{0,192},{64,0},{128,64},{192,128},{1,193},{65,1},{129,65},{193,129... | collective-permute-start | bytes 1376264 | tf_op jit(solution)/shard_map/ppermute | solution.py:179
  120.4 0.9 collective-permute-start.7
  121.3 0.4 collective-permute-start.6
  122.3 13.4 %all-to-all-done.3.pieces_ref = bf16[64,8,512]{2,1,0:T(8,128)(2,1)} async-done(((bf16[64,8,512]{2,1,0:T(8,128)(2,1)}), bf16[64,8,512]{2,1,0:T(8,128)(2,1)}, u32[]{:S(2)}, u32[]{:S(2)}) %all-to-all-start.3) | async-done | bytes 524320 | tf_op jit(solution)/shard_map/all_to_all | solution.py:266
  135.7 1.1 pick_second.1.refs_4_
  136.8 2.0 %collective-permute-start.11 = (bf16[8,8,512]{2,1,0:T(8,128)(2,1)S(1)}, bf16[8,8,512]{2,1,0:T(8,128)(2,1)S(1)}, u32[]{:S(2)}, u32[]{:S(2)}) collective-permute-start(bf16[8,8,512]{2,1,0:T(8,128)(2,1)S(1)} %pick_second.1.refs_4_), channel_id=1, source_target_pairs={{0,192},{64,0},{128,64},{192,128},{1,193},{65,1},{129,65},{193,129... | collective-permute-start | bytes 196616 | tf_op jit(solution)/shard_map/ppermute | solution.py:179
  138.7 0.9 collective-permute-start.10
  139.6 0.4 collective-permute-start.9
  140.0 1.6 %copy-done.5 = f32[2,512,512]{2,1,0:T(8,128)S(1)} copy-done((f32[2,512,512]{2,1,0:T(8,128)S(1)}, f32[2,512,512]{2,1,0:T(8,128)}, u32[]{:S(2)}) %copy-start.5) | copy-done | bytes 2097176
  141.6 3.5 %statistics.1 = (f32[2,512,512]{2,1,0:T(8,128)}, f32[2,512,512]{2,1,0:T(8,128)}) custom-call(s32[1]{0:T(128)} %bitcast.7.counts_ref, bf16[512,512]{1,0:T(8,128)(2,1)S(1)} %bitcast.11, bf16[512,512]{1,0:T(8,128)(2,1)S(1)} %bitcast.13, f32[2,512,512]{2,1,0:T(8,128)S(1)} %copy-done.4, f32[2,512,512]{2,1,0:T(8,128)S(1)} %copy-done.5), custom_call_target="tpu_custom_call" | custom-call | flops 1073741824 | bytes 8388608 | tf_op jit(solution)/shard_map/statistics/pallas_call | solution.py:217
  145.1 0.1 collective-permute-done.6.refs_1_
  145.2 0.7 collective-permute-done.9.refs_5_
  145.9 3.9 %assemble.1 = bf16[256,8,512]{2,1,0:T(8,128)(2,1)} custom-call(s32[1]{0:T(128)} %bitcast.1.place_ref, s32[256]{0:T(256)S(1)} %get-tuple-element.16.first_ref.blocks_ref, s32[64]{0:T(128)S(1)} %get-tuple-element.21.blocks_ref.second_ref, bf16[56,8,512]{2,1,0:T(8,128)(2,1)S(1)} %copy-done.10, bf16[56,8,512]{2,1,0:T(8,128)(2,1)} %collective-permute-done.6.refs_1_, ...), custom_call_target="tpu_custom_call" | custom-call | tf_op jit(solution)/shard_map/assemble/pallas_call | solution.py:160
  (20 shorter events, 0.0 us)
Async XLA Ops:
  0.6 1.6 %copy-start = (bf16[1,256,8,512]{3,2,1,0:T(8,128)(2,1)S(1)}, bf16[1,256,8,512]{3,2,1,0:T(8,128)(2,1)}, u32[]{:S(2)}) copy-start(bf16[1,256,8,512]{3,2,1,0:T(8,128)(2,1)} %param.7) | copy-start | bytes 6291460
  2.2 0.7 copy-start.11
  2.9 2.0 %copy-start.1 = (bf16[1,256,8,512]{3,2,1,0:T(8,128)(2,1)S(1)}, bf16[1,256,8,512]{3,2,1,0:T(8,128)(2,1)}, u32[]{:S(2)}) copy-start(bf16[1,256,8,512]{3,2,1,0:T(8,128)(2,1)} %param.7) | copy-start | bytes 6291460
  6.0 46.5 %copy-start.12 = (s32[256]{0:T(256)S(1)}, s32[256]{0:T(256)}, u32[]{:S(2)}) copy-start(s32[256]{0:T(256)} %table_ref.9) | copy-start | bytes 3076
  6.0 11.8 %collective-permute-start = (bf16[56,8,512]{2,1,0:T(8,128)(2,1)S(1)}, bf16[56,8,512]{2,1,0:T(8,128)(2,1)S(1)}, u32[]{:S(2)}, u32[]{:S(2)}) collective-permute-start(bf16[56,8,512]{2,1,0:T(8,128)(2,1)S(1)} %get-tuple-element.18), channel_id=1, source_target_pairs={{0,64},{64,128},{128,192},{192,0},{1,65},{65,129},{129,193},{193,1... | collective-permute-start | bytes 1376264 | tf_op jit(solution)/shard_map/ppermute | solution.py:179
  8.2 22.4 %collective-permute-start.1 = (bf16[56,8,512]{2,1,0:T(8,128)(2,1)S(1)}, bf16[56,8,512]{2,1,0:T(8,128)(2,1)S(1)}, u32[]{:S(2)}, u32[]{:S(2)}) collective-permute-start(bf16[56,8,512]{2,1,0:T(8,128)(2,1)S(1)} %get-tuple-element.19), channel_id=1, source_target_pairs={{0,128},{64,192},{128,0},{192,64},{1,129},{65,193},{129,1},{193,65... | collective-permute-start | bytes 1376264 | tf_op jit(solution)/shard_map/ppermute | solution.py:179
  10.8 19.8 %collective-permute-start.2 = (bf16[56,8,512]{2,1,0:T(8,128)(2,1)S(1)}, bf16[56,8,512]{2,1,0:T(8,128)(2,1)S(1)}, u32[]{:S(2)}, u32[]{:S(2)}) collective-permute-start(bf16[56,8,512]{2,1,0:T(8,128)(2,1)S(1)} %get-tuple-element.20), channel_id=1, source_target_pairs={{0,192},{64,0},{128,64},{192,128},{1,193},{65,1},{129,65},{193,129... | collective-permute-start | bytes 1376264 | tf_op jit(solution)/shard_map/ppermute | solution.py:179
  30.6 38.3 %copy-start.2 = (bf16[2,512,512]{2,1,0:T(8,128)(2,1)S(1)}, bf16[2,512,512]{2,1,0:T(8,128)(2,1)}, u32[]{:S(2)}) copy-start(bf16[2,512,512]{2,1,0:T(8,128)(2,1)} %left_ref.5) | copy-start | bytes 3145732
  30.6 38.3 %copy-start.3 = (bf16[2,512,512]{2,1,0:T(8,128)(2,1)S(1)}, bf16[2,512,512]{2,1,0:T(8,128)(2,1)}, u32[]{:S(2)}) copy-start(bf16[2,512,512]{2,1,0:T(8,128)(2,1)} %right_ref.5) | copy-start | bytes 3145732
  32.3 30.4 %all-to-all-start = ((bf16[64,8,512]{2,1,0:T(8,128)(2,1)}), bf16[64,8,512]{2,1,0:T(8,128)(2,1)S(1)}, u32[]{:S(2)}, u32[]{:S(2)}) async-start(bf16[64,8,512]{2,1,0:T(8,128)(2,1)} %mean_first.1), calls=%async_computation | async-start | bytes 1048576 | tf_op jit(solution)/shard_map/all_to_all | solution.py:251
  45.3 4.7 %collective-permute-start.3 = (bf16[8,8,512]{2,1,0:T(8,128)(2,1)S(1)}, bf16[8,8,512]{2,1,0:T(8,128)(2,1)S(1)}, u32[]{:S(2)}, u32[]{:S(2)}) collective-permute-start(bf16[8,8,512]{2,1,0:T(8,128)(2,1)S(1)} %get-tuple-element.23), channel_id=1, source_target_pairs={{0,64},{64,128},{128,192},{192,0},{1,65},{65,129},{129,193},{193,1... | collective-permute-start | bytes 196616 | tf_op jit(solution)/shard_map/ppermute | solution.py:179
  46.4 5.6 %collective-permute-start.4 = (bf16[8,8,512]{2,1,0:T(8,128)(2,1)S(1)}, bf16[8,8,512]{2,1,0:T(8,128)(2,1)S(1)}, u32[]{:S(2)}, u32[]{:S(2)}) collective-permute-start(bf16[8,8,512]{2,1,0:T(8,128)(2,1)S(1)} %get-tuple-element.24), channel_id=1, source_target_pairs={{0,128},{64,192},{128,0},{192,64},{1,129},{65,193},{129,1},{193,65... | collective-permute-start | bytes 196616 | tf_op jit(solution)/shard_map/ppermute | solution.py:179
  48.5 4.0 %collective-permute-start.5 = (bf16[8,8,512]{2,1,0:T(8,128)(2,1)S(1)}, bf16[8,8,512]{2,1,0:T(8,128)(2,1)S(1)}, u32[]{:S(2)}, u32[]{:S(2)}) collective-permute-start(bf16[8,8,512]{2,1,0:T(8,128)(2,1)S(1)} %get-tuple-element.25), channel_id=1, source_target_pairs={{0,192},{64,0},{128,64},{192,128},{1,193},{65,1},{129,65},{193,129... | collective-permute-start | bytes 196616 | tf_op jit(solution)/shard_map/ppermute | solution.py:179
  53.1 0.8 copy-start.6
  62.6 23.6 %all-to-all-start.1 = ((bf16[64,8,512]{2,1,0:T(8,128)(2,1)}), bf16[64,8,512]{2,1,0:T(8,128)(2,1)S(1)}, u32[]{:S(2)}, u32[]{:S(2)}) async-start(bf16[64,8,512]{2,1,0:T(8,128)(2,1)} %copy-done.6), calls=%async_computation.1 | async-start | bytes 1048576 | tf_op jit(solution)/shard_map/all_to_all | solution.py:247
  70.1 0.8 copy-start.8
  86.3 23.7 %all-to-all-start.2 = ((bf16[64,8,512]{2,1,0:T(8,128)(2,1)}), bf16[64,8,512]{2,1,0:T(8,128)(2,1)}, u32[]{:S(2)}, u32[]{:S(2)}) async-start(bf16[64,8,512]{2,1,0:T(8,128)(2,1)} %bitcast.15), calls=%async_computation.2 | async-start | bytes 1048576 | tf_op jit(solution)/shard_map/all_to_all | solution.py:258
  93.8 0.8 copy-start.7
  94.6 45.4 %copy-start.4 = (f32[2,512,512]{2,1,0:T(8,128)S(1)}, f32[2,512,512]{2,1,0:T(8,128)}, u32[]{:S(2)}) copy-start(f32[2,512,512]{2,1,0:T(8,128)} %left_ref.3) | copy-start | bytes 6291460
  111.2 0.8 copy-start.9
  112.0 23.7 %all-to-all-start.3 = ((bf16[64,8,512]{2,1,0:T(8,128)(2,1)}), bf16[64,8,512]{2,1,0:T(8,128)(2,1)}, u32[]{:S(2)}, u32[]{:S(2)}) async-start(bf16[64,8,512]{2,1,0:T(8,128)(2,1)} %bitcast.14), calls=%async_computation.3 | async-start | bytes 1048576 | tf_op jit(solution)/shard_map/all_to_all | solution.py:266
  118.4 21.1 %collective-permute-start.8 = (bf16[56,8,512]{2,1,0:T(8,128)(2,1)}, bf16[56,8,512]{2,1,0:T(8,128)(2,1)}, u32[]{:S(2)}, u32[]{:S(2)}) collective-permute-start(bf16[56,8,512]{2,1,0:T(8,128)(2,1)} %copy-done.9), channel_id=1, source_target_pairs={{0,192},{64,0},{128,64},{192,128},{1,193},{65,1},{129,65},{193,129... | collective-permute-start | bytes 1376264 | tf_op jit(solution)/shard_map/ppermute | solution.py:179
  120.4 24.7 %collective-permute-start.7 = (bf16[56,8,512]{2,1,0:T(8,128)(2,1)}, bf16[56,8,512]{2,1,0:T(8,128)(2,1)}, u32[]{:S(2)}, u32[]{:S(2)}) collective-permute-start(bf16[56,8,512]{2,1,0:T(8,128)(2,1)} %copy-done.9), channel_id=1, source_target_pairs={{0,128},{64,192},{128,0},{192,64},{1,129},{65,193},{129,1},{193,65... | collective-permute-start | bytes 1376264 | tf_op jit(solution)/shard_map/ppermute | solution.py:179
  121.3 23.9 %collective-permute-start.6 = (bf16[56,8,512]{2,1,0:T(8,128)(2,1)}, bf16[56,8,512]{2,1,0:T(8,128)(2,1)}, u32[]{:S(2)}, u32[]{:S(2)}) collective-permute-start(bf16[56,8,512]{2,1,0:T(8,128)(2,1)} %copy-done.9), channel_id=1, source_target_pairs={{0,64},{64,128},{128,192},{192,0},{1,65},{65,129},{129,193},{193,1... | collective-permute-start | bytes 1376264 | tf_op jit(solution)/shard_map/ppermute | solution.py:179
  136.8 8.4 %collective-permute-start.11 = (bf16[8,8,512]{2,1,0:T(8,128)(2,1)S(1)}, bf16[8,8,512]{2,1,0:T(8,128)(2,1)S(1)}, u32[]{:S(2)}, u32[]{:S(2)}) collective-permute-start(bf16[8,8,512]{2,1,0:T(8,128)(2,1)S(1)} %pick_second.1.refs_4_), channel_id=1, source_target_pairs={{0,192},{64,0},{128,64},{192,128},{1,193},{65,1},{129,65},{193,129... | collective-permute-start | bytes 196616 | tf_op jit(solution)/shard_map/ppermute | solution.py:179
  138.7 6.5 %collective-permute-start.10 = (bf16[8,8,512]{2,1,0:T(8,128)(2,1)S(1)}, bf16[8,8,512]{2,1,0:T(8,128)(2,1)S(1)}, u32[]{:S(2)}, u32[]{:S(2)}) collective-permute-start(bf16[8,8,512]{2,1,0:T(8,128)(2,1)S(1)} %pick_second.1.refs_4_), channel_id=1, source_target_pairs={{0,128},{64,192},{128,0},{192,64},{1,129},{65,193},{129,1},{193,65... | collective-permute-start | bytes 196616 | tf_op jit(solution)/shard_map/ppermute | solution.py:179
  139.6 6.4 %collective-permute-start.9 = (bf16[8,8,512]{2,1,0:T(8,128)(2,1)S(1)}, bf16[8,8,512]{2,1,0:T(8,128)(2,1)S(1)}, u32[]{:S(2)}, u32[]{:S(2)}) collective-permute-start(bf16[8,8,512]{2,1,0:T(8,128)(2,1)S(1)} %pick_second.1.refs_4_), channel_id=1, source_target_pairs={{0,64},{64,128},{128,192},{192,0},{1,65},{65,129},{129,193},{193,1... | collective-permute-start | bytes 196616 | tf_op jit(solution)/shard_map/ppermute | solution.py:179
  140.0 1.6 %copy-start.5 = (f32[2,512,512]{2,1,0:T(8,128)S(1)}, f32[2,512,512]{2,1,0:T(8,128)}, u32[]{:S(2)}) copy-start(f32[2,512,512]{2,1,0:T(8,128)} %right_ref.3) | copy-start | bytes 6291460
  141.6 4.4 %copy-start.10 = (bf16[56,8,512]{2,1,0:T(8,128)(2,1)S(1)}, bf16[56,8,512]{2,1,0:T(8,128)(2,1)}, u32[]{:S(2)}) copy-start(bf16[56,8,512]{2,1,0:T(8,128)(2,1)} %copy-done.9) | copy-start | bytes 1376260

commit v2 on v0

v2 whole, which is shorter than its diff:
```python
import jax
import jax.numpy as jnp
from jax import lax
from jax.experimental import pallas as pl
from jax.experimental.pallas import tpu as pltpu
from jax.sharding import PartitionSpec as P

BETA = 0.9
EPS = 1e-06
BF16 = jnp.bfloat16
F32 = jnp.float32

NEXT = [(i, i ^ 1) for i in range(4)]
LAST = [(i, 3 - i) for i in range(4)]

VMEM = pl.BlockSpec(memory_space=pltpu.VMEM)
SMEM = pl.BlockSpec(memory_space=pltpu.SMEM)
HBM = pl.BlockSpec(memory_space=pltpu.HBM)
PARAMS = pltpu.CompilerParams(vmem_limit_bytes=32 * 1024 * 1024)


def shape(*dims, dtype=BF16):
    return jax.ShapeDtypeStruct(dims, dtype)


def call(kernel, outs, in_specs, args, name, scratch=(), out_specs=None):
    return pl.pallas_call(
        kernel,
        out_shape=outs,
        in_specs=in_specs,
        out_specs=[VMEM] * len(outs) if out_specs is None else out_specs,
        scratch_shapes=scratch,
        compiler_params=PARAMS,
        name=name,
    )(*args)


def around():
    me = lax.axis_index("dp")
    return me, me ^ 1, 3 - me, me ^ 2


def first_sends(grads, group):
    rows, width = grads.shape[1:]
    half = width // 2

    def kernel(grads_ref, to_next, to_last, sems):
        _, after, before, opposite = around()
        copies = []
        for out, column, near in ((to_next, 0, after), (to_last, half, before)):
            for at, g in enumerate((near, opposite)):
                source = grads_ref.at[pl.ds(g * group, group), :, pl.ds(column, half)]
                target = out.at[pl.ds(at * group, group)]
                copies.append(pltpu.make_async_copy(source, target, sems.at[len(copies)]))
        for copy in copies:
            copy.start()
        for copy in copies:
            copy.wait()

    outs = [shape(2 * group, rows, half)] * 2
    return call(kernel, outs, [HBM], [grads], "sends", [pltpu.SemaphoreType.DMA((4,))])


def partial_sums(grads, from_next, from_last, group):
    rows, width = grads.shape[1:]
    half = width // 2

    def kernel(grads_ref, from_next_ref, from_last_ref, left, right):
        _, after, before, _ = around()

        def step(j, _):
            kept = grads_ref[before * group + j][:, :half].astype(F32)
            left[j] = (kept + from_next_ref[group + j].astype(F32)).astype(BF16)
            kept = grads_ref[after * group + j][:, half:].astype(F32)
            right[j] = (kept + from_last_ref[group + j].astype(F32)).astype(BF16)
            return 0

        lax.fori_loop(0, group, step, 0, unroll=8)

    outs = [shape(group, rows, half)] * 2
    return call(kernel, outs, [VMEM] * 3, [grads, from_next, from_last], "partial")


def place_mean(table, grads, step_one, step_two, devices, slots, group, replicas):
    rows, width = grads.shape[1:]
    half = width // 2
    scale = 1.0 / replicas

    def kernel(table_ref, grads_ref, *refs):
        out = refs[-1]
        out[...] = jnp.zeros(out.shape, BF16)
        me = lax.axis_index("dp")

        def step(j, _):
            entry = table_ref[me * group + j]
            owner = entry // slots
            column = (entry - owner * slots) * width
            own = grads_ref[me * group + j].astype(F32)
            for c in range(2):
                total = own[:, c * half : (c + 1) * half]
                total = total + refs[c][j].astype(F32) + refs[2 + c][j].astype(F32)
                span = pl.ds(pl.multiple_of(column + c * half, half), half)
                out[owner, :, span] = (total * scale).astype(BF16)
            return 0

        lax.fori_loop(0, group, step, 0, unroll=8)

    outs = [shape(devices, rows, slots * width)]
    args = [table, grads, *step_one, *step_two]
    return call(kernel, outs, [SMEM] + [VMEM] * 5, args, "mean")[0]


def precondition(grads, left, right):
    slots, size = left.shape[:2]

    def kernel(grads_ref, left_ref, right_ref, out_ref):
        for s in range(slots):
            span = slice(s * size, (s + 1) * size)
            part = jnp.dot(
                left_ref[s], grads_ref[:, span], preferred_element_type=F32
            ).astype(BF16)
            direction = jnp.dot(part, right_ref[s], preferred_element_type=F32)
            power = jnp.sum(direction * direction) * (1.0 / (size * size))
            out_ref[:, span] = (direction * lax.rsqrt(power + EPS)).astype(BF16)

    outs = [shape(size, slots * size)]
    return call(kernel, outs, [VMEM] * 3, [grads, left, right], "direction")[0]


def pick_rows(table, pieces, slots, group):
    rows, width = pieces.shape[1], pieces.shape[2] // slots

    def kernel(table_ref, pieces_ref, out):
        me = lax.axis_index("dp")

        def step(j, _):
            entry = table_ref[me * group + j]
            owner = entry // slots
            column = pl.multiple_of((entry - owner * slots) * width, width)
            out[j] = pieces_ref[owner, :, pl.ds(column, width)]
            return 0

        lax.fori_loop(0, group, step, 0, unroll=8)

    return call(kernel, [shape(group, rows, width)], [SMEM, VMEM], [table, pieces], "pick")[0]


def assemble(mine, at_next, at_last, across, replicas):
    group, rows, width = mine.shape

    def kernel(mine_ref, next_ref, last_ref, low_ref, high_ref, out, sems):
        me, after, before, opposite = around()
        parts = (
            (mine_ref, me * group),
            (next_ref, after * group),
            (last_ref, before * group),
            (low_ref, opposite * group),
            (high_ref, opposite * group + group // 2),
        )
        copies = [
            pltpu.make_async_copy(ref, out.at[pl.ds(start, ref.shape[0])], sems.at[i])
            for i, (ref, start) in enumerate(parts)
        ]
        for copy in copies:
            copy.start()
        for copy in copies:
            copy.wait()

    args = [mine, at_next, at_last, *across]
    outs = [shape(replicas * group, rows, width)]
    scratch = [pltpu.SemaphoreType.DMA((5,))]
    return call(kernel, outs, [VMEM] * 5, args, "assemble", scratch, [HBM])[0]


def new_statistics(counts, grads, stats_left, stats_right, parts=2):
    slots, size = stats_left.shape[:2]
    tile = size // parts

    def kernel(counts_ref, grads_ref, left_ref, right_ref, new_left_ref, new_right_ref):
        live = counts_ref[0] > pl.program_id(0)
        for p in range(parts):

            @pl.when(pl.program_id(1) == p)
            def _(p=p):
                grad = grads_ref[...]
                span = slice(p * tile, (p + 1) * tile)
                gram_left = lax.dot_general(
                    grad[span], grad, (((1,), (1,)), ((), ())), preferred_element_type=F32
                )
                gram_right = lax.dot_general(
                    grad[:, span], grad, (((0,), (0,)), ((), ())), preferred_element_type=F32
                )
                old_left, old_right = left_ref[0], right_ref[0]
                new_left_ref[0] = jnp.where(
                    live, BETA * old_left + (1.0 - BETA) * gram_left, old_left
                )
                new_right_ref[0] = jnp.where(
                    live, BETA * old_right + (1.0 - BETA) * gram_right, old_right
                )

    block = pl.BlockSpec((size, size), lambda s, t: (0, s))
    part = pl.BlockSpec((1, tile, size), lambda s, t: (s, t, 0))
    return pl.pallas_call(
        kernel,
        out_shape=[shape(*stats_left.shape, dtype=F32)] * 2,
        grid=(slots, parts),
        in_specs=[SMEM, block, part, part],
        out_specs=[part, part],
        compiler_params=PARAMS,
        cost_estimate=pl.CostEstimate(
            flops=8 * size**3, bytes_accessed=16 * 2 * size * size, transcendentals=0
        ),
        name="statistics",
    )(counts, grads, stats_left, stats_right)


def local(grads, stats_left, stats_right, precond_left, precond_right, owner_table, block_counts):
    devices = lax.axis_size("fsdp")
    replicas = lax.axis_size("dp")
    blocks, rows, width = grads.shape[1:]
    slots, size = stats_left.shape[:2]
    group = blocks // replicas
    mine = grads[0]
    send = lambda pieces, pairs: lax.ppermute(pieces, "dp", pairs)
    exchange = lambda pieces: lax.all_to_all(pieces, "fsdp", 0, 0, tiled=True)

    to_next, to_last = first_sends(mine, group)
    step_one = [send(to_next, NEXT), send(to_last, LAST)]
    left, right = partial_sums(mine, *step_one, group)
    step_two = [send(left, LAST), send(right, NEXT)]
    outgoing = place_mean(
        owner_table, mine, step_one, step_two, devices, slots, group, replicas
    )
    owned = exchange(outgoing).reshape(size, slots * width)

    scaled = precondition(owned, precond_left, precond_right)
    returned = exchange(scaled.reshape(devices, rows, slots * width))
    picked = pick_rows(owner_table, returned, slots, group)
    at_next, at_last = send(picked, NEXT), send(picked, LAST)
    across = [send(at_last[: group // 2], NEXT), send(at_next[group // 2 :], LAST)]
    update = assemble(picked, at_next, at_last, across, replicas)
    new_left, new_right = new_statistics(
        block_counts.reshape(1), owned, stats_left, stats_right
    )
    return (new_left, new_right, update)


def solution(mesh):
    in_specs = (
        P("dp", None, "fsdp", None),
        P(("dp", "fsdp"), None, None),
        P(("dp", "fsdp"), None, None),
        P(("dp", "fsdp"), None, None),
        P(("dp", "fsdp"), None, None),
        P(),
        P("dp", "fsdp"),
    )
    out_specs = (
        P(("dp", "fsdp"), None, None),
        P(("dp", "fsdp"), None, None),
        P(None, "fsdp", None),
    )
    return jax.shard_map(local, mesh=mesh, in_specs=in_specs, out_specs=out_specs, check_vma=False)
```

time: 174 us -> 133 us (0.76)
  waiting for transfers between devices: 61.3 us -> 33.3 us
  between operations: 14.8 us -> 1.42 us
  matrix products: 10.5 us -> 0 us
  Pallas kernels: 0 us -> 9.24 us
  starting transfers between devices: 0.08 us -> 9.09 us
  local copies, waits for them, and re-layouts: 10.1 us -> 1.65 us
  blocking collectives: 73.6 us -> 77.8 us
  other arithmetic: 3.05 us -> 0 us
    reduce_scatter x1 -> x0, waiting for transfers between devices: 38.6 us -> none  [local(): lax.psum_scatter(grads[0].astype(jnp.float32).astype(jnp.bfloat16), 'dp',...]
    ppermute x0 -> x8, waiting for transfers between devices: none -> 33.3 us  [local(): send = lambda pieces, pairs: lax.ppermute(pieces, 'dp', pairs)]
    all_gather x1 -> x0, waiting for transfers between devices: 22 us -> none  [return_rows(): return lax.all_gather(mine, 'dp', axis=0, tiled=True)]
    dot_general x5 -> x0, matrix products: 10.5 us -> none  [the longest x1 3.92 us: owner_statistics(): jnp.einsum('ski,skj->sij', blocks, blocks, preferred_element_type=jnp.flo...]
    pallas_call x0 -> x7, Pallas kernels: none -> 9.24 us  [the longest x6 5.65 us: call(): pl.pallas_call(kernel, out_shape=outs, in_specs=in_specs, out_specs=[VMEM...]
    ppermute x0 -> x8, starting transfers between devices: none -> 9.09 us  [local(): send = lambda pieces, pairs: lax.ppermute(pieces, 'dp', pairs)]
    all_to_all x2, blocking collectives: 73.6 us -> 77.8 us  [local(): exchange = lambda pieces: lax.all_to_all(pieces, 'fsdp', 0, 0, tiled=True)]
    reshape x3 -> x0, local copies, waits for them, and re-layouts: 3.05 us -> none  [the longest x2 1.58 us: local(): outgoing = outgoing.reshape(fsdp_size, slot_count, row_count, width)]
  transfers between devices with their start and end apart: 2 -> 8, of which waited for: 2 -> 7; matrix products, arithmetic and copies ran while one was open for 4% -> 0% of each run, Pallas kernels for 0% -> 3%
where the time goes in v2:
time: 133 us
  blocking collectives  77.8 us (58%)
  waiting for transfers between devices  33.3 us (25%)
  Pallas kernels  9.24 us (7%)
  starting transfers between devices  9.09 us (7%)
  local copies, waits for them, and re-layouts  1.65 us (1%)
  between operations  1.42 us (1%)
    all_to_all x2, blocking collectives, local(): exchange = lambda pieces: lax.all_to_all(pieces, 'fsdp', 0, 0, tiled=True)  77.8 us
    ppermute x8, waiting for transfers between devices, local(): send = lambda pieces, pairs: lax.ppermute(pieces, 'dp', pairs)  33.3 us
    ppermute x8, starting transfers between devices, local(): send = lambda pieces, pairs: lax.ppermute(pieces, 'dp', pairs)  9.09 us
    pallas_call x6, Pallas kernels, call(): pl.pallas_call(kernel, out_shape=outs, in_specs=in_specs, out_specs=[VMEM...  5.65 us
    pallas_call x1, Pallas kernels, new_statistics(): pl.pallas_call(kernel, out_shape=[shape(*stats_left.shape, dtype=F32)] *...  3.59 us
  transfers between devices with their start and end apart: 8, of which 7 were waited for; matrix products, arithmetic and copies ran while one was open for 0% of the time, Pallas kernels for 3%

profile of v2, /device:TPU:1, one launch (start us, length us, event | category | flops | bytes accessed | tf_op | source)
XLA Modules:
  0.0 132.6 jit_solution(1835656856628842237)
XLA Ops:
  0.6 0.0 copy-start
  0.6 1.6 %copy-done = bf16[1,256,8,512]{3,2,1,0:T(8,128)(2,1)S(1)} copy-done((bf16[1,256,8,512]{3,2,1,0:T(8,128)(2,1)S(1)}, bf16[1,256,8,512]{3,2,1,0:T(8,128)(2,1)}, u32[]{:S(2)}) %copy-start) | copy-done | bytes 2097176
  2.2 0.1 sends.1
  2.3 0.0 copy-start.5
  2.4 2.2 %collective-permute-start = (bf16[128,8,256]{2,1,0:T(8,128)(2,1)S(1)}, bf16[128,8,256]{2,1,0:T(8,128)(2,1)S(1)}, u32[]{:S(2)}, u32[]{:S(2)}) collective-permute-start(bf16[128,8,256]{2,1,0:T(8,128)(2,1)S(1)} %get-tuple-element.9), channel_id=1, source_target_pairs={{0,64},{64,0},{128,192},{192,128},{1,65},{65,1},{129,193},{193,129... | collective-permute-start | bytes 1572872 | tf_op jit(solution)/shard_map/ppermute | solution.py:224
  4.6 1.9 %collective-permute-start.1 = (bf16[128,8,256]{2,1,0:T(8,128)(2,1)S(1)}, bf16[128,8,256]{2,1,0:T(8,128)(2,1)S(1)}, u32[]{:S(2)}, u32[]{:S(2)}) collective-permute-start(bf16[128,8,256]{2,1,0:T(8,128)(2,1)S(1)} %get-tuple-element.10), channel_id=1, source_target_pairs={{0,192},{64,128},{128,64},{192,0},{1,193},{65,129},{129,65},{193,1... | collective-permute-start | bytes 1572872 | tf_op jit(solution)/shard_map/ppermute | solution.py:224
  6.5 8.5 %collective-permute-done.from_next_ref.refs_0_ = bf16[128,8,256]{2,1,0:T(8,128)(2,1)S(1)} collective-permute-done((bf16[128,8,256]{2,1,0:T(8,128)(2,1)S(1)}, bf16[128,8,256]{2,1,0:T(8,128)(2,1)S(1)}, u32[]{:S(2)}, u32[]{:S(2)}) %collective-permute-start) | collective-permute-done | bytes 524320 | tf_op jit(solution)/shard_map/ppermute | solution.py:224
  15.0 3.0 %collective-permute-done.1.from_last_ref.refs_1_ = bf16[128,8,256]{2,1,0:T(8,128)(2,1)S(1)} collective-permute-done((bf16[128,8,256]{2,1,0:T(8,128)(2,1)S(1)}, bf16[128,8,256]{2,1,0:T(8,128)(2,1)S(1)}, u32[]{:S(2)}, u32[]{:S(2)}) %collective-permute-start.1) | collective-permute-done | bytes 524320 | tf_op jit(solution)/shard_map/ppermute | solution.py:224
  18.0 0.2 partial.1
  18.1 2.3 %collective-permute-start.2 = (bf16[64,8,256]{2,1,0:T(8,128)(2,1)S(1)}, bf16[64,8,256]{2,1,0:T(8,128)(2,1)S(1)}, u32[]{:S(2)}, u32[]{:S(2)}) collective-permute-start(bf16[64,8,256]{2,1,0:T(8,128)(2,1)S(1)} %get-tuple-element.11), channel_id=1, source_target_pairs={{0,192},{64,128},{128,64},{192,0},{1,193},{65,129},{129,65},{193,1... | collective-permute-start | bytes 786440 | tf_op jit(solution)/shard_map/ppermute | solution.py:224
  20.4 0.0 collective-permute-start.3
  20.4 4.7 %collective-permute-done.2.refs_2_ = bf16[64,8,256]{2,1,0:T(8,128)(2,1)S(1)} collective-permute-done((bf16[64,8,256]{2,1,0:T(8,128)(2,1)S(1)}, bf16[64,8,256]{2,1,0:T(8,128)(2,1)S(1)}, u32[]{:S(2)}, u32[]{:S(2)}) %collective-permute-start.2) | collective-permute-done | bytes 262176 | tf_op jit(solution)/shard_map/ppermute | solution.py:224
  25.1 1.0 collective-permute-done.3.refs_3_
  26.1 0.0 copy-done.5
  26.1 1.3 mean.1
  27.3 0.0 copy-start.3
  27.3 0.0 copy-start.4
  27.3 43.0 %all_to_all.10 = bf16[64,8,1024]{2,1,0:T(8,128)(2,1)S(1)} all-to-all(bf16[64,8,1024]{2,1,0:T(8,128)(2,1)S(1)} %mean.1), channel_id=1, replica_groups=mesh['dp'=4,'fsdp'=64] {'fsdp'}, dimensions={0} | all-to-all | bytes 2097152 | tf_op jit(solution)/shard_map/all_to_all | solution.py:225
  70.4 0.0 copy-done.3
  70.4 0.0 copy-done.4
  70.4 1.7 %direction.1 = bf16[512,1024]{1,0:T(8,128)(2,1)S(1)} custom-call(bf16[512,1024]{1,0:T(8,128)(2,1)S(1)} %bitcast.8, bf16[2,512,512]{2,1,0:T(8,128)(2,1)S(1)} %copy-done.3, bf16[2,512,512]{2,1,0:T(8,128)(2,1)S(1)} %copy-done.4), custom_call_target="tpu_custom_call" | custom-call | tf_op jit(solution)/shard_map/direction/pallas_call | solution.py:27
  72.1 0.0 copy-start.1
  72.1 0.0 copy-start.2
  72.1 34.8 %all_to_all.11.pieces_ref = bf16[64,8,1024]{2,1,0:T(8,128)(2,1)S(1)} all-to-all(bf16[64,8,1024]{2,1,0:T(8,128)(2,1)S(1)} %bitcast.10), channel_id=1, replica_groups=mesh['dp'=4,'fsdp'=64] {'fsdp'}, dimensions={0} | all-to-all | bytes 2097152 | tf_op jit(solution)/shard_map/all_to_all | solution.py:225
  107.0 1.1 pick.1.mine_ref
  108.0 1.3 collective-permute-start.5
  109.3 0.0 collective-permute-start.4
  109.3 13.5 %collective-permute-done.5.last_ref = bf16[64,8,512]{2,1,0:T(8,128)(2,1)S(1)} collective-permute-done((bf16[64,8,512]{2,1,0:T(8,128)(2,1)S(1)}, bf16[64,8,512]{2,1,0:T(8,128)(2,1)S(1)}, u32[]{:S(2)}, u32[]{:S(2)}) %collective-permute-start.5) | collective-permute-done | bytes 524320 | tf_op jit(solution)/shard_map/ppermute | solution.py:224
  122.8 0.1 collective-permute-start.6
  122.9 0.0 collective-permute-done.4.next_ref
  123.0 1.3 collective-permute-start.7
  124.9 0.0 copy-done.1
  124.9 0.0 copy-done.2
  124.9 3.6 %statistics.1 = (f32[2,512,512]{2,1,0:T(8,128)}, f32[2,512,512]{2,1,0:T(8,128)}) custom-call(s32[1]{0:T(128)} %bitcast.4.counts_ref, bf16[512,1024]{1,0:T(8,128)(2,1)S(1)} %bitcast.9, f32[2,512,512]{2,1,0:T(8,128)S(1)} %copy-done.1, f32[2,512,512]{2,1,0:T(8,128)S(1)} %copy-done.2), custom_call_target="tpu_custom_call" | custom-call | flops 1073741824 | bytes 8388608 | tf_op jit(solution)/shard_map/statistics/pallas_call | solution.py:203
  128.5 1.3 %collective-permute-done.6.low_ref = bf16[32,8,512]{2,1,0:T(8,128)(2,1)S(1)} collective-permute-done((bf16[32,8,512]{2,1,0:T(8,128)(2,1)S(1)}, bf16[32,8,512]{2,1,0:T(8,128)(2,1)S(1)}, u32[]{:S(2)}, u32[]{:S(2)}) %collective-permute-start.6) | collective-permute-done | bytes 262176 | tf_op jit(solution)/shard_map/ppermute | solution.py:224
  129.9 1.3 %collective-permute-done.7.high_ref = bf16[32,8,512]{2,1,0:T(8,128)(2,1)S(1)} collective-permute-done((bf16[32,8,512]{2,1,0:T(8,128)(2,1)S(1)}, bf16[32,8,512]{2,1,0:T(8,128)(2,1)S(1)}, u32[]{:S(2)}, u32[]{:S(2)}) %collective-permute-start.7) | collective-permute-done | bytes 262176 | tf_op jit(solution)/shard_map/ppermute | solution.py:224
  131.2 1.3 %assemble.1 = bf16[256,8,512]{2,1,0:T(8,128)(2,1)} custom-call(bf16[64,8,512]{2,1,0:T(8,128)(2,1)S(1)} %pick.1.mine_ref, bf16[64,8,512]{2,1,0:T(8,128)(2,1)S(1)} %collective-permute-done.4.next_ref, bf16[64,8,512]{2,1,0:T(8,128)(2,1)S(1)} %collective-permute-done.5.last_ref, bf16[32,8,512]{2,1,0:T(8,128)(2,1)S(1)} %collective-permute-done.6.low_ref, ...), custom_call_target="tpu_custom_call" | custom-call | tf_op jit(solution)/shard_map/assemble/pallas_call | solution.py:27
  (2 shorter events, 0.0 us)
Async XLA Ops:
  0.6 1.6 %copy-start = (bf16[1,256,8,512]{3,2,1,0:T(8,128)(2,1)S(1)}, bf16[1,256,8,512]{3,2,1,0:T(8,128)(2,1)}, u32[]{:S(2)}) copy-start(bf16[1,256,8,512]{3,2,1,0:T(8,128)(2,1)} %param.7) | copy-start | bytes 6291460
  2.3 23.7 %copy-start.5 = (s32[256]{0:T(256)S(1)}, s32[256]{0:T(256)}, u32[]{:S(2)}) copy-start(s32[256]{0:T(256)} %table_ref.3) | copy-start | bytes 3076
  2.4 12.6 %collective-permute-start = (bf16[128,8,256]{2,1,0:T(8,128)(2,1)S(1)}, bf16[128,8,256]{2,1,0:T(8,128)(2,1)S(1)}, u32[]{:S(2)}, u32[]{:S(2)}) collective-permute-start(bf16[128,8,256]{2,1,0:T(8,128)(2,1)S(1)} %get-tuple-element.9), channel_id=1, source_target_pairs={{0,64},{64,0},{128,192},{192,128},{1,65},{65,1},{129,193},{193,129... | collective-permute-start | bytes 1572872 | tf_op jit(solution)/shard_map/ppermute | solution.py:224
  4.6 13.4 %collective-permute-start.1 = (bf16[128,8,256]{2,1,0:T(8,128)(2,1)S(1)}, bf16[128,8,256]{2,1,0:T(8,128)(2,1)S(1)}, u32[]{:S(2)}, u32[]{:S(2)}) collective-permute-start(bf16[128,8,256]{2,1,0:T(8,128)(2,1)S(1)} %get-tuple-element.10), channel_id=1, source_target_pairs={{0,192},{64,128},{128,64},{192,0},{1,193},{65,129},{129,65},{193,1... | collective-permute-start | bytes 1572872 | tf_op jit(solution)/shard_map/ppermute | solution.py:224
  18.1 7.0 %collective-permute-start.2 = (bf16[64,8,256]{2,1,0:T(8,128)(2,1)S(1)}, bf16[64,8,256]{2,1,0:T(8,128)(2,1)S(1)}, u32[]{:S(2)}, u32[]{:S(2)}) collective-permute-start(bf16[64,8,256]{2,1,0:T(8,128)(2,1)S(1)} %get-tuple-element.11), channel_id=1, source_target_pairs={{0,192},{64,128},{128,64},{192,0},{1,193},{65,129},{129,65},{193,1... | collective-permute-start | bytes 786440 | tf_op jit(solution)/shard_map/ppermute | solution.py:224
  20.4 5.7 %collective-permute-start.3 = (bf16[64,8,256]{2,1,0:T(8,128)(2,1)S(1)}, bf16[64,8,256]{2,1,0:T(8,128)(2,1)S(1)}, u32[]{:S(2)}, u32[]{:S(2)}) collective-permute-start(bf16[64,8,256]{2,1,0:T(8,128)(2,1)S(1)} %get-tuple-element.12), channel_id=1, source_target_pairs={{0,64},{64,0},{128,192},{192,128},{1,65},{65,1},{129,193},{193,129... | collective-permute-start | bytes 786440 | tf_op jit(solution)/shard_map/ppermute | solution.py:224
  27.3 43.1 %copy-start.3 = (bf16[2,512,512]{2,1,0:T(8,128)(2,1)S(1)}, bf16[2,512,512]{2,1,0:T(8,128)(2,1)}, u32[]{:S(2)}) copy-start(bf16[2,512,512]{2,1,0:T(8,128)(2,1)} %left_ref.3) | copy-start | bytes 3145732
  27.3 43.1 %copy-start.4 = (bf16[2,512,512]{2,1,0:T(8,128)(2,1)S(1)}, bf16[2,512,512]{2,1,0:T(8,128)(2,1)}, u32[]{:S(2)}) copy-start(bf16[2,512,512]{2,1,0:T(8,128)(2,1)} %right_ref.3) | copy-start | bytes 3145732
  72.1 52.8 %copy-start.1 = (f32[2,512,512]{2,1,0:T(8,128)S(1)}, f32[2,512,512]{2,1,0:T(8,128)}, u32[]{:S(2)}) copy-start(f32[2,512,512]{2,1,0:T(8,128)} %left_ref.2) | copy-start | bytes 6291460
  72.1 52.8 %copy-start.2 = (f32[2,512,512]{2,1,0:T(8,128)S(1)}, f32[2,512,512]{2,1,0:T(8,128)}, u32[]{:S(2)}) copy-start(f32[2,512,512]{2,1,0:T(8,128)} %right_ref.2) | copy-start | bytes 6291460
  108.0 14.8 %collective-permute-start.5 = (bf16[64,8,512]{2,1,0:T(8,128)(2,1)S(1)}, bf16[64,8,512]{2,1,0:T(8,128)(2,1)S(1)}, u32[]{:S(2)}, u32[]{:S(2)}) collective-permute-start(bf16[64,8,512]{2,1,0:T(8,128)(2,1)S(1)} %pick.1.mine_ref), channel_id=1, source_target_pairs={{0,192},{64,128},{128,64},{192,0},{1,193},{65,129},{129,65},{193,1... | collective-permute-start | bytes 1572872 | tf_op jit(solution)/shard_map/ppermute | solution.py:224
  109.3 13.6 %collective-permute-start.4 = (bf16[64,8,512]{2,1,0:T(8,128)(2,1)S(1)}, bf16[64,8,512]{2,1,0:T(8,128)(2,1)S(1)}, u32[]{:S(2)}, u32[]{:S(2)}) collective-permute-start(bf16[64,8,512]{2,1,0:T(8,128)(2,1)S(1)} %pick.1.mine_ref), channel_id=1, source_target_pairs={{0,64},{64,0},{128,192},{192,128},{1,65},{65,1},{129,193},{193,129... | collective-permute-start | bytes 1572872 | tf_op jit(solution)/shard_map/ppermute | solution.py:224
  122.8 7.0 %collective-permute-start.6 = (bf16[32,8,512]{2,1,0:T(8,128)(2,1)S(1)}, bf16[32,8,512]{2,1,0:T(8,128)(2,1)S(1)}, u32[]{:S(2)}, u32[]{:S(2)}) collective-permute-start(bf16[32,8,512]{2,1,0:T(8,128)(2,1)S(1)} %slice.8), channel_id=1, source_target_pairs={{0,64},{64,0},{128,192},{192,128},{1,65},{65,1},{129,193},{193,129... | collective-permute-start | bytes 786440 | tf_op jit(solution)/shard_map/ppermute | solution.py:224
  123.0 8.3 %collective-permute-start.7 = (bf16[32,8,512]{2,1,0:T(8,128)(2,1)S(1)}, bf16[32,8,512]{2,1,0:T(8,128)(2,1)S(1)}, u32[]{:S(2)}, u32[]{:S(2)}) collective-permute-start(bf16[32,8,512]{2,1,0:T(8,128)(2,1)S(1)} %slice.9), channel_id=1, source_target_pairs={{0,192},{64,128},{128,64},{192,0},{1,193},{65,129},{129,65},{193,1... | collective-permute-start | bytes 786440 | tf_op jit(solution)/shard_map/ppermute | solution.py:224

commit v3 on v2

v3 whole, which is shorter than its diff:
```python
import jax
import jax.numpy as jnp
from jax import lax
from jax.experimental import pallas as pl
from jax.experimental.pallas import tpu as pltpu
from jax.sharding import PartitionSpec as P

BETA = 0.9
EPS = 1e-06
BF16 = jnp.bfloat16
F32 = jnp.float32

NEXT = [(i, i ^ 1) for i in range(4)]
LAST = [(i, 3 - i) for i in range(4)]
OPPOSITE = [(i, i ^ 2) for i in range(4)]
SECOND = 8
LIST = 16

VMEM = pl.BlockSpec(memory_space=pltpu.VMEM)
SMEM = pl.BlockSpec(memory_space=pltpu.SMEM)
HBM = pl.BlockSpec(memory_space=pltpu.HBM)
PARAMS = pltpu.CompilerParams(vmem_limit_bytes=16 * 1024 * 1024)


def shape(*dims, dtype=BF16):
    return jax.ShapeDtypeStruct(dims, dtype)


def call(kernel, outs, in_specs, args, name, scratch=(), out_specs=None):
    return pl.pallas_call(
        kernel,
        out_shape=outs,
        in_specs=in_specs,
        out_specs=[VMEM] * len(outs) if out_specs is None else out_specs,
        scratch_shapes=scratch,
        compiler_params=PARAMS,
        name=name,
    )(*args)


def around():
    me = lax.axis_index("dp")
    return me, me ^ 1, 3 - me, me ^ 2


def copy_all(pairs, sems):
    copies = [
        pltpu.make_async_copy(source, target, sems.at[i])
        for i, (source, target) in enumerate(pairs)
    ]
    for copy in copies:
        copy.start()
    for copy in copies:
        copy.wait()


def first_sends(grads, group):
    rows, width = grads.shape[1:]
    half = width // 2

    def kernel(grads_ref, far_next, far_last, near_next, near_last, sems):
        _, after, before, opposite = around()
        part = lambda g, column: grads_ref.at[pl.ds(g * group, group), :, pl.ds(column, half)]
        pairs = [
            (part(opposite, 0), far_next),
            (part(opposite, half), far_last),
            (part(after, 0), near_next),
            (part(before, half), near_last),
        ]
        copy_all(pairs, sems)

    outs = [shape(group, rows, half)] * 4
    scratch = [pltpu.SemaphoreType.DMA((4,))]
    return call(kernel, outs, [HBM], [grads], "sends", scratch)


def kept(grads, group):
    rows, width = grads.shape[1:]
    half = width // 2

    def kernel(grads_ref, own, left, right, sems):
        me, after, before, _ = around()
        part = lambda g, column: grads_ref.at[pl.ds(g * group, group), :, pl.ds(column, half)]
        pairs = [
            (grads_ref.at[pl.ds(me * group, group)], own),
            (part(before, 0), left),
            (part(after, half), right),
        ]
        copy_all(pairs, sems)

    outs = [shape(group, rows, width)] + [shape(group, rows, half)] * 2
    scratch = [pltpu.SemaphoreType.DMA((3,))]
    return call(kernel, outs, [HBM], [grads], "kept", scratch)


def partial_sums(kept_halves, arrived):
    dims = arrived[0].shape

    def kernel(left_kept, right_kept, left_got, right_got, left, right):
        def step(j, _):
            left[j] = (left_kept[j].astype(F32) + left_got[j].astype(F32)).astype(BF16)
            right[j] = (right_kept[j].astype(F32) + right_got[j].astype(F32)).astype(BF16)
            return 0

        lax.fori_loop(0, dims[0], step, 0, unroll=8)

    return call(kernel, [shape(*dims)] * 2, [VMEM] * 4, [*kept_halves, *arrived], "partial")


def place_mean(table, own, near, passed, devices, replicas):
    group, rows, width = own.shape
    half = width // 2
    scale = 1.0 / replicas

    def kernel(table_ref, own_ref, *refs):
        first, second = refs[-2:]
        first[...] = jnp.zeros(first.shape, BF16)
        second[...] = jnp.zeros(second.shape, BF16)
        me = lax.axis_index("dp")

        def step(j, _):
            entry = table_ref[me * group + j]
            own = own_ref[j].astype(F32)
            halves = []
            for c in range(2):
                total = own[:, c * half : (c + 1) * half]
                total = total + refs[c][j].astype(F32) + refs[2 + c][j].astype(F32)
                halves.append((total * scale).astype(BF16))
            for slot, out in enumerate((first, second)):

                @pl.when((entry & 1) == slot)
                def _(out=out):
                    for c in range(2):
                        out[entry >> 1, :, c * half : (c + 1) * half] = halves[c]

            return 0

        lax.fori_loop(0, group, step, 0, unroll=8)

    outs = [shape(devices, rows, width)] * 2
    args = [table, own, *near, *passed]
    return call(kernel, outs, [SMEM] + [VMEM] * 5, args, "mean")


def scaled_update(grad, left, right):
    part = jnp.dot(left, grad, preferred_element_type=F32).astype(BF16)
    direction = jnp.dot(part, right, preferred_element_type=F32)
    power = jnp.sum(direction * direction) * (1.0 / (direction.shape[0] * direction.shape[1]))
    return (direction * lax.rsqrt(power + EPS)).astype(BF16)


def direction_first(grad, left, right, passenger):
    size = grad.shape[0]

    def kernel(grad_ref, left_ref, right_ref, passenger_ref, out):
        out[:, size:] = passenger_ref[...]
        out[:, :size] = scaled_update(grad_ref[...], left_ref[0], right_ref[0])

    whole = pl.BlockSpec((size, size), lambda i: (0, 0))
    slot = pl.BlockSpec((1, size, size), lambda i: (0, 0, 0))
    return pl.pallas_call(
        kernel,
        out_shape=shape(size, 2 * size),
        grid=(1,),
        in_specs=[whole, slot, slot, whole],
        out_specs=pl.BlockSpec((size, 2 * size), lambda i: (0, 0)),
        compiler_params=PARAMS,
        name="direction_first",
    )(grad, left, right, passenger)


def direction_second(mixed, left, right):
    size = mixed.shape[0]

    def kernel(grad_ref, left_ref, right_ref, out):
        out[...] = scaled_update(grad_ref[...], left_ref[0], right_ref[0])

    slot = pl.BlockSpec((1, size, size), lambda i: (1, 0, 0))
    return pl.pallas_call(
        kernel,
        out_shape=shape(size, size),
        grid=(1,),
        in_specs=[pl.BlockSpec((size, size), lambda i: (0, 1)), slot, slot],
        out_specs=pl.BlockSpec((size, size), lambda i: (0, 0)),
        compiler_params=PARAMS,
        name="direction_second",
    )(mixed, left, right)


def pick_first(table, pieces, group):
    rows, width = pieces.shape[1], pieces.shape[2] // 2
    half = group // 2

    def kernel(table_ref, pieces_ref, low, high):
        me = lax.axis_index("dp")

        def step(j, _):
            low[j] = pieces_ref[table_ref[me * group + j] >> 1]
            high[j] = pieces_ref[table_ref[me * group + half + j] >> 1]
            return 0

        lax.fori_loop(0, half, step, 0, unroll=8)

    return pl.pallas_call(
        kernel,
        out_shape=[shape(half, rows, width)] * 2,
        grid=(1,),
        in_specs=[SMEM, pl.BlockSpec((pieces.shape[0], rows, width), lambda i: (0, 0, 0))],
        out_specs=[pl.BlockSpec((half, rows, width), lambda i: (0, 0, 0))] * 2,
        compiler_params=PARAMS,
        name="pick_first",
    )(table, pieces)


def pick_second(table, pieces, group):
    rows, width = pieces.shape[1:]

    def kernel(table_ref, pieces_ref, out, room):
        me = lax.axis_index("dp")
        count = jnp.int32(0)
        for j in range(group):
            entry = table_ref[me * group + j]
            room[count] = pieces_ref[entry >> 1]
            count = count + (entry & 1)
        for i in range(SECOND):
            out[i] = room[i]

    outs = [shape(SECOND, rows, width)]
    scratch = [pltpu.VMEM((SECOND + 1, rows, width), BF16)]
    return call(kernel, outs, [SMEM, VMEM], [table, pieces], "pick_second", scratch)[0]


def second_places(table, group, replicas):
    def kernel(table_ref, at):
        for g in range(replicas):
            count = jnp.int32(0)
            for j in range(group):
                at[g * LIST + count] = g * group + j
                count = count + (table_ref[g * group + j] & 1)

    outs = [shape(replicas * LIST, dtype=jnp.int32)]
    return call(kernel, outs, [SMEM], [table], "second_places", out_specs=[SMEM])[0]


def lay_near(near, group, replicas):
    rows, width = near[0].shape[1:]

    def kernel(*refs):
        sources, (out, sems) = refs[:-2], refs[-2:]
        starts = [g * group + i * (group // 2) for g in around()[:3] for i in range(2)]
        pairs = [
            (source, out.at[pl.ds(start, group // 2)])
            for source, start in zip(sources, starts)
        ]
        copy_all(pairs, sems)

    outs = [shape(replicas * group, rows, width)]
    scratch = [pltpu.SemaphoreType.DMA((len(near),))]
    return call(kernel, outs, [VMEM] * len(near), near, "lay_near", scratch, [HBM])[0]


def lay_rest(update, at, across, seconds, group):
    replicas = len(seconds)

    def kernel(at_ref, _, low, high, *refs):
        sources, (out, sems, second_sems) = refs[:replicas], refs[replicas:]
        groups = around()
        start = groups[-1] * group
        copies = [
            pltpu.make_async_copy(ref, out.at[pl.ds(start + i * (group // 2), group // 2)], sems.at[i])
            for i, ref in enumerate((low, high))
        ]
        for copy in copies:
            copy.start()
        for k, g in enumerate(groups):
            if k == replicas - 1:
                for copy in copies:
                    copy.wait()
            for i in range(SECOND):
                pltpu.make_async_copy(
                    sources[k].at[i], out.at[at_ref[g * LIST + i]], second_sems.at[k]
                ).start()
        for k in range(replicas):
            pltpu.make_async_copy(
                sources[k], out.at[pl.ds(0, SECOND)], second_sems.at[k]
            ).wait()

    return pl.pallas_call(
        kernel,
        out_shape=shape(*update.shape),
        in_specs=[SMEM, HBM] + [VMEM] * (2 + replicas),
        out_specs=HBM,
        scratch_shapes=[pltpu.SemaphoreType.DMA((2,)), pltpu.SemaphoreType.DMA((replicas,))],
        input_output_aliases={1: 0},
        compiler_params=PARAMS,
        name="lay_rest",
    )(at, update, *across, *seconds)


def new_statistics(counts, grad, mixed, stats_left, stats_right, parts=2):
    slots, size = stats_left.shape[:2]
    tile = size // parts

    def kernel(counts_ref, first, second, left_ref, right_ref, new_left_ref, new_right_ref):
        live = counts_ref[0] > pl.program_id(0)
        for s, p in [(s, p) for s in range(slots) for p in range(parts)]:

            @pl.when((pl.program_id(0) == s) & (pl.program_id(1) == p))
            def _(s=s, p=p):
                grad = (first, second)[s][...]
                span = slice(p * tile, (p + 1) * tile)
                gram_left = lax.dot_general(
                    grad[span], grad, (((1,), (1,)), ((), ())), preferred_element_type=F32
                )
                gram_right = lax.dot_general(
                    grad[:, span], grad, (((0,), (0,)), ((), ())), preferred_element_type=F32
                )
                old_left, old_right = left_ref[0], right_ref[0]
                new_left_ref[0] = jnp.where(
                    live, BETA * old_left + (1.0 - BETA) * gram_left, old_left
                )
                new_right_ref[0] = jnp.where(
                    live, BETA * old_right + (1.0 - BETA) * gram_right, old_right
                )

    block = lambda column: pl.BlockSpec((size, size), lambda s, t: (0, column))
    part = pl.BlockSpec((1, tile, size), lambda s, t: (s, t, 0))
    return pl.pallas_call(
        kernel,
        out_shape=[shape(*stats_left.shape, dtype=F32)] * 2,
        grid=(slots, parts),
        in_specs=[SMEM, block(0), block(1), part, part],
        out_specs=[part, part],
        compiler_params=PARAMS,
        cost_estimate=pl.CostEstimate(
            flops=8 * size**3, bytes_accessed=16 * 2 * size * size, transcendentals=0
        ),
        name="statistics",
    )(counts, grad, mixed, stats_left, stats_right)


def local(grads, stats_left, stats_right, precond_left, precond_right, owner_table, block_counts):
    devices = lax.axis_size("fsdp")
    replicas = lax.axis_size("dp")
    blocks, rows, width = grads.shape[1:]
    slots, size = stats_left.shape[:2]
    group = blocks // replicas
    mine = grads[0]
    send = lambda pieces, pairs: lax.ppermute(pieces, "dp", pairs)
    exchange = lambda pieces: lax.all_to_all(pieces, "fsdp", 0, 0, tiled=True)

    far_next, far_last, near_next, near_last = first_sends(mine, group)
    own, *kept_halves = kept(mine, group)
    arrived = [send(far_next, NEXT), send(far_last, LAST)]
    near = [send(near_next, NEXT), send(near_last, LAST)]
    at = second_places(owner_table, group, replicas)
    kept_halves, at = lax.optimization_barrier((kept_halves, at))
    left, right = partial_sums(kept_halves, arrived)
    passed = [send(left, LAST), send(right, NEXT)]
    first_out, second_out = place_mean(owner_table, own, near, passed, devices, replicas)
    grad_first = exchange(first_out).reshape(size, width)
    outgoing = direction_first(
        grad_first, precond_left, precond_right, second_out.reshape(size, width)
    )
    mixed = exchange(outgoing.reshape(devices, rows, 2 * width))
    mixed_rows = mixed.reshape(size, 2 * width)
    scaled_second = direction_second(mixed_rows, precond_left, precond_right)
    second_back = exchange(scaled_second.reshape(devices, rows, width))

    low, high = pick_first(owner_table, mixed, group)
    last_low, next_high = send(low, LAST), send(high, NEXT)
    next_low, last_high = send(low, NEXT), send(high, LAST)
    grad_first, _ = lax.optimization_barrier((grad_first, low))
    stats = new_statistics(
        block_counts.reshape(1), grad_first, mixed_rows, stats_left, stats_right
    )
    last_low, next_high, stats = lax.optimization_barrier((last_low, next_high, stats))
    across = [send(last_low, NEXT), send(next_high, LAST)]
    second_rows = pick_second(owner_table, second_back, group)
    seconds = [second_rows] + [send(second_rows, p) for p in (NEXT, LAST, OPPOSITE)]
    update = lay_near([low, high, next_low, next_high, last_low, last_high], group, replicas)
    update = lay_rest(update, at, across, seconds, group)
    return (*stats, update)


def solution(mesh):
    in_specs = (
        P("dp", None, "fsdp", None),
        P(("dp", "fsdp"), None, None),
        P(("dp", "fsdp"), None, None),
        P(("dp", "fsdp"), None, None),
        P(("dp", "fsdp"), None, None),
        P(),
        P("dp", "fsdp"),
    )
    out_specs = (
        P(("dp", "fsdp"), None, None),
        P(("dp", "fsdp"), None, None),
        P(None, "fsdp", None),
    )
    return jax.shard_map(local, mesh=mesh, in_specs=in_specs, out_specs=out_specs, check_vma=False)
```

time: 133 us -> 127 us (0.955)
  waiting for transfers between devices: 33.3 us -> 16.7 us
  starting transfers between devices: 9.09 us -> 22.1 us
  blocking collectives: 77.8 us -> 65.4 us
  Pallas kernels: 9.24 us -> 15.6 us
  local copies, waits for them, and re-layouts: 1.65 us -> 4.78 us
    ppermute x8 -> x15, waiting for transfers between devices: 33.3 us -> 13.2 us  [local(): send = lambda pieces, pairs: lax.ppermute(pieces, 'dp', pairs)]
    all_to_all x2, blocking collectives: 77.8 us -> 65.4 us  [local(): exchange = lambda pieces: lax.all_to_all(pieces, 'fsdp', 0, 0, tiled=True)]
    ppermute x8 -> x15, starting transfers between devices: 9.09 us -> 15.9 us  [local(): send = lambda pieces, pairs: lax.ppermute(pieces, 'dp', pairs)]
    all_to_all x0 -> x1, starting transfers between devices: none -> 6.2 us  [local(): exchange = lambda pieces: lax.all_to_all(pieces, 'fsdp', 0, 0, tiled=True)]
    pallas_call x0 -> x4, Pallas kernels: none -> 5.7 us  [the longest x1 2.02 us: lay_rest(): pl.pallas_call(kernel, out_shape=shape(*update.shape), in_specs=[SMEM, HB...]
    all_to_all x0 -> x1, waiting for transfers between devices: none -> 3.48 us  [local(): exchange = lambda pieces: lax.all_to_all(pieces, 'fsdp', 0, 0, tiled=True)]
    unnamed x12, local copies, waits for them, and re-layouts: 1.62 us -> 4.78 us
    pallas_call x6 -> x7, Pallas kernels: 5.65 us -> 6.37 us  [call(): pl.pallas_call(kernel, out_shape=outs, in_specs=in_specs, out_specs=[VMEM...]
  transfers between devices with their start and end apart: 8 -> 16, of which waited for: 7 -> 7; matrix products, arithmetic and copies ran while one was open for 0% -> 0% of each run, Pallas kernels for 3% -> 7%
where the time goes in v3:
time: 127 us; the launch traced here: 126 us
  blocking collectives  65.4 us (51%)
  starting transfers between devices  22.1 us (17%)
  waiting for transfers between devices  16.7 us (13%)
  Pallas kernels  15.6 us (12%)
  local copies, waits for them, and re-layouts  4.78 us (4%)
  between operations  1.6 us (1%)
    all_to_all x2, blocking collectives, local(): exchange = lambda pieces: lax.all_to_all(pieces, 'fsdp', 0, 0, tiled=True)  65.4 us
    ppermute x15, starting transfers between devices, local(): send = lambda pieces, pairs: lax.ppermute(pieces, 'dp', pairs)  15.9 us
    ppermute x15, waiting for transfers between devices, local(): send = lambda pieces, pairs: lax.ppermute(pieces, 'dp', pairs)  13.2 us
    pallas_call x7, Pallas kernels, call(): pl.pallas_call(kernel, out_shape=outs, in_specs=in_specs, out_specs=[VMEM...  6.37 us
    all_to_all x1, starting transfers between devices, local(): exchange = lambda pieces: lax.all_to_all(pieces, 'fsdp', 0, 0, tiled=True)  6.2 us
    unnamed x12, local copies, waits for them, and re-layouts  4.78 us
    pallas_call x1, Pallas kernels, new_statistics(): pl.pallas_call(kernel, out_shape=[shape(*stats_left.shape, dtype=F32)] *...  3.51 us
    all_to_all x1, waiting for transfers between devices, local(): exchange = lambda pieces: lax.all_to_all(pieces, 'fsdp', 0, 0, tiled=True)  3.48 us
  transfers between devices with their start and end apart: 16, of which 7 were waited for; matrix products, arithmetic and copies ran while one was open for 0% of the time, Pallas kernels for 7%

profile of v3, /device:TPU:1, one launch (start us, length us, event | category | flops | bytes accessed | tf_op | source)
XLA Modules:
  0.0 126.2 jit_solution(17393120870670032814)
XLA Ops:
  0.6 1.6 %copy-done = bf16[1,256,8,512]{3,2,1,0:T(8,128)(2,1)S(1)} copy-done((bf16[1,256,8,512]{3,2,1,0:T(8,128)(2,1)S(1)}, bf16[1,256,8,512]{3,2,1,0:T(8,128)(2,1)}, u32[]{:S(2)}) %copy-start) | copy-done | bytes 2097176
  2.2 0.1 sends.1
  2.3 2.2 %collective-permute-start.2 = (bf16[64,8,256]{2,1,0:T(8,128)(2,1)S(1)}, bf16[64,8,256]{2,1,0:T(8,128)(2,1)S(1)}, u32[]{:S(2)}, u32[]{:S(2)}) collective-permute-start(bf16[64,8,256]{2,1,0:T(8,128)(2,1)S(1)} %get-tuple-element.33), channel_id=1, source_target_pairs={{0,64},{64,0},{128,192},{192,128},{1,65},{65,1},{129,193},{193,129... | collective-permute-start | bytes 786440 | tf_op jit(solution)/shard_map/ppermute | solution.py:349
  4.6 1.9 %collective-permute-start.3 = (bf16[64,8,256]{2,1,0:T(8,128)(2,1)S(1)}, bf16[64,8,256]{2,1,0:T(8,128)(2,1)S(1)}, u32[]{:S(2)}, u32[]{:S(2)}) collective-permute-start(bf16[64,8,256]{2,1,0:T(8,128)(2,1)S(1)} %get-tuple-element.34), channel_id=1, source_target_pairs={{0,192},{64,128},{128,64},{192,0},{1,193},{65,129},{129,65},{193,1... | collective-permute-start | bytes 786440 | tf_op jit(solution)/shard_map/ppermute | solution.py:349
  6.5 0.4 collective-permute-start
  6.9 0.6 collective-permute-start.1
  7.5 0.1 kept.1
  7.6 0.0 copy-start.1
  7.6 0.0 copy-start.2
  7.6 1.6 %second_places.1.at_ref = s32[64]{0:T(128)S(1)} custom-call(s32[256]{0:T(256)S(1)} %copy-done.5), custom_call_target="tpu_custom_call" | custom-call | tf_op jit(solution)/shard_map/second_places/pallas_call | solution.py:30
  9.2 0.1 collective-permute-done.2.left_got
  9.3 3.0 %collective-permute-done.3.right_got = bf16[64,8,256]{2,1,0:T(8,128)(2,1)S(1)} collective-permute-done((bf16[64,8,256]{2,1,0:T(8,128)(2,1)S(1)}, bf16[64,8,256]{2,1,0:T(8,128)(2,1)S(1)}, u32[]{:S(2)}, u32[]{:S(2)}) %collective-permute-start.3) | collective-permute-done | bytes 262176 | tf_op jit(solution)/shard_map/ppermute | solution.py:349
  12.4 0.1 partial.1
  12.5 2.3 %collective-permute-start.4 = (bf16[64,8,256]{2,1,0:T(8,128)(2,1)S(1)}, bf16[64,8,256]{2,1,0:T(8,128)(2,1)S(1)}, u32[]{:S(2)}, u32[]{:S(2)}) collective-permute-start(bf16[64,8,256]{2,1,0:T(8,128)(2,1)S(1)} %get-tuple-element.35), channel_id=1, source_target_pairs={{0,192},{64,128},{128,64},{192,0},{1,193},{65,129},{129,65},{193,1... | collective-permute-start | bytes 786440 | tf_op jit(solution)/shard_map/ppermute | solution.py:349
  14.8 0.0 collective-permute-start.5
  14.8 0.2 collective-permute-done.refs_0_
  15.0 3.0 %collective-permute-done.1.refs_1_ = bf16[64,8,256]{2,1,0:T(8,128)(2,1)S(1)} collective-permute-done((bf16[64,8,256]{2,1,0:T(8,128)(2,1)S(1)}, bf16[64,8,256]{2,1,0:T(8,128)(2,1)S(1)}, u32[]{:S(2)}, u32[]{:S(2)}) %collective-permute-start.1) | collective-permute-done | bytes 262176 | tf_op jit(solution)/shard_map/ppermute | solution.py:349
  18.0 5.6 %collective-permute-done.4.refs_2_ = bf16[64,8,256]{2,1,0:T(8,128)(2,1)S(1)} collective-permute-done((bf16[64,8,256]{2,1,0:T(8,128)(2,1)S(1)}, bf16[64,8,256]{2,1,0:T(8,128)(2,1)S(1)}, u32[]{:S(2)}, u32[]{:S(2)}) %collective-permute-start.4) | collective-permute-done | bytes 262176 | tf_op jit(solution)/shard_map/ppermute | solution.py:349
  23.6 0.0 collective-permute-done.5.refs_3_
  23.6 1.6 %mean.1 = (bf16[64,8,512]{2,1,0:T(8,128)(2,1)S(1)}, bf16[64,8,512]{2,1,0:T(8,128)(2,1)S(1)}) custom-call(s32[256]{0:T(256)S(1)} %copy-done.5, bf16[64,8,512]{2,1,0:T(8,128)(2,1)S(1)} %get-tuple-element.26.own_ref, bf16[64,8,256]{2,1,0:T(8,128)(2,1)S(1)} %collective-permute-done.refs_0_, bf16[64,8,256]{2,1,0:T(8,128)(2,1)S(1)} %collective-permute-done.1.refs_1_, ...), custom_call_target="tpu_custom_call" | custom-call | tf_op jit(solution)/shard_map/mean/pallas_call | solution.py:30
  25.2 30.7 %all_to_all.15 = bf16[64,8,512]{2,1,0:T(8,128)(2,1)S(1)} all-to-all(bf16[64,8,512]{2,1,0:T(8,128)(2,1)S(1)} %get-tuple-element.37), channel_id=1, replica_groups=mesh['dp'=4,'fsdp'=64] {'fsdp'}, dimensions={0} | all-to-all | bytes 1048576 | tf_op jit(solution)/shard_map/all_to_all | solution.py:350
  55.9 1.1 direction_first.1
  57.0 34.6 %all_to_all.16.pieces_ref = bf16[64,8,1024]{2,1,0:T(8,128)(2,1)S(1)} all-to-all(bf16[64,8,1024]{2,1,0:T(8,128)(2,1)S(1)} %bitcast.14), channel_id=1, replica_groups=mesh['dp'=4,'fsdp'=64] {'fsdp'}, dimensions={0} | all-to-all | bytes 2097152 | tf_op jit(solution)/shard_map/all_to_all | solution.py:350
  91.7 1.9 %direction_second.1 = bf16[512,512]{1,0:T(8,128)(2,1)} custom-call(bf16[512,1024]{1,0:T(8,128)(2,1)S(1)} %bitcast.8, bf16[2,512,512]{2,1,0:T(8,128)(2,1)S(1)} %copy-done.1, bf16[2,512,512]{2,1,0:T(8,128)(2,1)S(1)} %copy-done.2), custom_call_target="tpu_custom_call" | custom-call | tf_op jit(solution)/shard_map/direction_second/pallas_call | solution.py:179
  93.6 6.2 %all-to-all-start.2 = ((bf16[64,8,512]{2,1,0:T(8,128)(2,1)}), bf16[64,8,512]{2,1,0:T(8,128)(2,1)S(1)}, u32[]{:S(2)}, u32[]{:S(2)}) async-start(bf16[64,8,512]{2,1,0:T(8,128)(2,1)} %bitcast.6), calls=%async_computation.2 | async-start | bytes 1048576 | tf_op jit(solution)/shard_map/all_to_all | solution.py:350
  99.8 0.7 pick_first.1
  100.4 0.1 collective-permute-start.7
  100.5 2.0 %collective-permute-start.6 = (bf16[32,8,512]{2,1,0:T(8,128)(2,1)S(1)}, bf16[32,8,512]{2,1,0:T(8,128)(2,1)S(1)}, u32[]{:S(2)}, u32[]{:S(2)}) collective-permute-start(bf16[32,8,512]{2,1,0:T(8,128)(2,1)S(1)} %get-tuple-element.39.refs_0_), channel_id=1, source_target_pairs={{0,192},{64,128},{128,64},{192,0},{1,193},{65,129},{129,65},{193,1... | collective-permute-start | bytes 786440 | tf_op jit(solution)/shard_map/ppermute | solution.py:349
  103.2 0.9 collective-permute-start.9
  104.1 0.3 collective-permute-start.8
  104.3 1.6 %copy-done.3 = f32[2,512,512]{2,1,0:T(8,128)S(1)} copy-done((f32[2,512,512]{2,1,0:T(8,128)S(1)}, f32[2,512,512]{2,1,0:T(8,128)}, u32[]{:S(2)}) %copy-start.3) | copy-done | bytes 2097176
  105.9 1.6 %copy-done.4 = f32[2,512,512]{2,1,0:T(8,128)S(1)} copy-done((f32[2,512,512]{2,1,0:T(8,128)S(1)}, f32[2,512,512]{2,1,0:T(8,128)}, u32[]{:S(2)}) %copy-start.4) | copy-done | bytes 2097176
  107.5 3.5 %statistics.1 = (f32[2,512,512]{2,1,0:T(8,128)}, f32[2,512,512]{2,1,0:T(8,128)}) custom-call(s32[1]{0:T(128)} %bitcast.7.counts_ref, bf16[512,512]{1,0:T(8,128)(2,1)S(1)} %bitcast.13, bf16[512,1024]{1,0:T(8,128)(2,1)S(1)} %bitcast.9, f32[2,512,512]{2,1,0:T(8,128)S(1)} %copy-done.3, f32[2,512,512]{2,1,0:T(8,128)S(1)} %copy-done.4), custom_call_target="tpu_custom_call" | custom-call | flops 1073741824 | bytes 8388608 | tf_op jit(solution)/shard_map/statistics/pallas_call | solution.py:328
  111.0 0.0 collective-permute-done.7.refs_3_
  111.0 1.9 %collective-permute-start.11 = (bf16[32,8,512]{2,1,0:T(8,128)(2,1)S(1)}, bf16[32,8,512]{2,1,0:T(8,128)(2,1)S(1)}, u32[]{:S(2)}, u32[]{:S(2)}) collective-permute-start(bf16[32,8,512]{2,1,0:T(8,128)(2,1)S(1)} %collective-permute-done.7.refs_3_), channel_id=1, source_target_pairs={{0,192},{64,128},{128,64},{192,0},{1,193},{65,129},{129,65},{193,1... | collective-permute-start | bytes 786440 | tf_op jit(solution)/shard_map/ppermute | solution.py:349
  112.9 0.7 collective-permute-start.10
  113.6 3.5 %all-to-all-done.2.pieces_ref = bf16[64,8,512]{2,1,0:T(8,128)(2,1)S(1)} async-done(((bf16[64,8,512]{2,1,0:T(8,128)(2,1)}), bf16[64,8,512]{2,1,0:T(8,128)(2,1)S(1)}, u32[]{:S(2)}, u32[]{:S(2)}) %all-to-all-start.2) | async-done | bytes 524320 | tf_op jit(solution)/shard_map/all_to_all | solution.py:350
  117.1 0.7 pick_second.1.refs_0_
  117.8 1.5 %collective-permute-start.14 = (bf16[8,8,512]{2,1,0:T(8,128)(2,1)S(1)}, bf16[8,8,512]{2,1,0:T(8,128)(2,1)S(1)}, u32[]{:S(2)}, u32[]{:S(2)}) collective-permute-start(bf16[8,8,512]{2,1,0:T(8,128)(2,1)S(1)} %pick_second.1.refs_0_), channel_id=1, source_target_pairs={{0,128},{64,192},{128,0},{192,64},{1,129},{65,193},{129,1},{193,65... | collective-permute-start | bytes 196616 | tf_op jit(solution)/shard_map/ppermute | solution.py:349
  119.3 0.6 collective-permute-start.13
  119.9 0.0 collective-permute-done.8.refs_2_
  119.9 0.6 collective-permute-start.12
  120.6 2.1 %lay_near.1._ = bf16[256,8,512]{2,1,0:T(8,128)(2,1)} custom-call(bf16[32,8,512]{2,1,0:T(8,128)(2,1)S(1)} %get-tuple-element.39.refs_0_, bf16[32,8,512]{2,1,0:T(8,128)(2,1)S(1)} %get-tuple-element.40.refs_1_, bf16[32,8,512]{2,1,0:T(8,128)(2,1)} %collective-permute-done.8.refs_2_, bf16[32,8,512]{2,1,0:T(8,128)(2,1)S(1)} %collective-permute-done.7.refs_3_, ...), custom_call_target="tpu_custom_call" | custom-call | tf_op jit(solution)/shard_map/lay_near/pallas_call | solution.py:30
  122.7 0.0 collective-permute-done.11.high
  122.7 0.0 collective-permute-done.10.low
  122.7 1.3 %collective-permute-done.13.refs_2_ = bf16[8,8,512]{2,1,0:T(8,128)(2,1)S(1)} collective-permute-done((bf16[8,8,512]{2,1,0:T(8,128)(2,1)S(1)}, bf16[8,8,512]{2,1,0:T(8,128)(2,1)S(1)}, u32[]{:S(2)}, u32[]{:S(2)}) %collective-permute-start.13) | collective-permute-done | bytes 65568 | tf_op jit(solution)/shard_map/ppermute | solution.py:349
  124.0 0.0 collective-permute-done.12.refs_1_
  124.0 2.0 %lay_rest.1 = bf16[256,8,512]{2,1,0:T(8,128)(2,1)} custom-call(s32[64]{0:T(128)S(1)} %second_places.1.at_ref, bf16[256,8,512]{2,1,0:T(8,128)(2,1)} %lay_near.1._, bf16[32,8,512]{2,1,0:T(8,128)(2,1)S(1)} %collective-permute-done.10.low, bf16[32,8,512]{2,1,0:T(8,128)(2,1)S(1)} %collective-permute-done.11.high, ...), custom_call_target="tpu_custom_call", output_to_operand_aliasing={{}: (1, {})} | custom-call | tf_op jit(solution)/shard_map/lay_rest/pallas_call | solution.py:288
  (10 shorter events, 0.0 us)
Async XLA Ops:
  0.6 1.6 %copy-start = (bf16[1,256,8,512]{3,2,1,0:T(8,128)(2,1)S(1)}, bf16[1,256,8,512]{3,2,1,0:T(8,128)(2,1)}, u32[]{:S(2)}) copy-start(bf16[1,256,8,512]{3,2,1,0:T(8,128)(2,1)} %param.7) | copy-start | bytes 6291460
  2.2 5.4 %copy-start.5 = (s32[256]{0:T(256)S(1)}, s32[256]{0:T(256)}, u32[]{:S(2)}) copy-start(s32[256]{0:T(256)} %table_ref.7) | copy-start | bytes 3076
  2.3 7.0 %collective-permute-start.2 = (bf16[64,8,256]{2,1,0:T(8,128)(2,1)S(1)}, bf16[64,8,256]{2,1,0:T(8,128)(2,1)S(1)}, u32[]{:S(2)}, u32[]{:S(2)}) collective-permute-start(bf16[64,8,256]{2,1,0:T(8,128)(2,1)S(1)} %get-tuple-element.33), channel_id=1, source_target_pairs={{0,64},{64,0},{128,192},{192,128},{1,65},{65,1},{129,193},{193,129... | collective-permute-start | bytes 786440 | tf_op jit(solution)/shard_map/ppermute | solution.py:349
  4.6 7.8 %collective-permute-start.3 = (bf16[64,8,256]{2,1,0:T(8,128)(2,1)S(1)}, bf16[64,8,256]{2,1,0:T(8,128)(2,1)S(1)}, u32[]{:S(2)}, u32[]{:S(2)}) collective-permute-start(bf16[64,8,256]{2,1,0:T(8,128)(2,1)S(1)} %get-tuple-element.34), channel_id=1, source_target_pairs={{0,192},{64,128},{128,64},{192,0},{1,193},{65,129},{129,65},{193,1... | collective-permute-start | bytes 786440 | tf_op jit(solution)/shard_map/ppermute | solution.py:349
  6.5 8.5 %collective-permute-start = (bf16[64,8,256]{2,1,0:T(8,128)(2,1)S(1)}, bf16[64,8,256]{2,1,0:T(8,128)(2,1)S(1)}, u32[]{:S(2)}, u32[]{:S(2)}) collective-permute-start(bf16[64,8,256]{2,1,0:T(8,128)(2,1)S(1)} %get-tuple-element.27), channel_id=1, source_target_pairs={{0,64},{64,0},{128,192},{192,128},{1,65},{65,1},{129,193},{193,129... | collective-permute-start | bytes 786440 | tf_op jit(solution)/shard_map/ppermute | solution.py:349
  6.9 11.1 %collective-permute-start.1 = (bf16[64,8,256]{2,1,0:T(8,128)(2,1)S(1)}, bf16[64,8,256]{2,1,0:T(8,128)(2,1)S(1)}, u32[]{:S(2)}, u32[]{:S(2)}) collective-permute-start(bf16[64,8,256]{2,1,0:T(8,128)(2,1)S(1)} %get-tuple-element.28), channel_id=1, source_target_pairs={{0,192},{64,128},{128,64},{192,0},{1,193},{65,129},{129,65},{193,1... | collective-permute-start | bytes 786440 | tf_op jit(solution)/shard_map/ppermute | solution.py:349
  7.6 48.3 %copy-start.1 = (bf16[2,512,512]{2,1,0:T(8,128)(2,1)S(1)}, bf16[2,512,512]{2,1,0:T(8,128)(2,1)}, u32[]{:S(2)}) copy-start(bf16[2,512,512]{2,1,0:T(8,128)(2,1)} %left_ref.5) | copy-start | bytes 3145732
  7.6 48.3 %copy-start.2 = (bf16[2,512,512]{2,1,0:T(8,128)(2,1)S(1)}, bf16[2,512,512]{2,1,0:T(8,128)(2,1)}, u32[]{:S(2)}) copy-start(bf16[2,512,512]{2,1,0:T(8,128)(2,1)} %right_ref.5) | copy-start | bytes 3145732
  12.5 11.1 %collective-permute-start.4 = (bf16[64,8,256]{2,1,0:T(8,128)(2,1)S(1)}, bf16[64,8,256]{2,1,0:T(8,128)(2,1)S(1)}, u32[]{:S(2)}, u32[]{:S(2)}) collective-permute-start(bf16[64,8,256]{2,1,0:T(8,128)(2,1)S(1)} %get-tuple-element.35), channel_id=1, source_target_pairs={{0,192},{64,128},{128,64},{192,0},{1,193},{65,129},{129,65},{193,1... | collective-permute-start | bytes 786440 | tf_op jit(solution)/shard_map/ppermute | solution.py:349
  14.8 8.8 %collective-permute-start.5 = (bf16[64,8,256]{2,1,0:T(8,128)(2,1)S(1)}, bf16[64,8,256]{2,1,0:T(8,128)(2,1)S(1)}, u32[]{:S(2)}, u32[]{:S(2)}) collective-permute-start(bf16[64,8,256]{2,1,0:T(8,128)(2,1)S(1)} %get-tuple-element.36), channel_id=1, source_target_pairs={{0,64},{64,0},{128,192},{192,128},{1,65},{65,1},{129,193},{193,129... | collective-permute-start | bytes 786440 | tf_op jit(solution)/shard_map/ppermute | solution.py:349
  93.6 23.5 %all-to-all-start.2 = ((bf16[64,8,512]{2,1,0:T(8,128)(2,1)}), bf16[64,8,512]{2,1,0:T(8,128)(2,1)S(1)}, u32[]{:S(2)}, u32[]{:S(2)}) async-start(bf16[64,8,512]{2,1,0:T(8,128)(2,1)} %bitcast.6), calls=%async_computation.2 | async-start | bytes 1048576 | tf_op jit(solution)/shard_map/all_to_all | solution.py:350
  100.4 10.6 %collective-permute-start.7 = (bf16[32,8,512]{2,1,0:T(8,128)(2,1)S(1)}, bf16[32,8,512]{2,1,0:T(8,128)(2,1)S(1)}, u32[]{:S(2)}, u32[]{:S(2)}) collective-permute-start(bf16[32,8,512]{2,1,0:T(8,128)(2,1)S(1)} %get-tuple-element.40.refs_1_), channel_id=1, source_target_pairs={{0,64},{64,0},{128,192},{192,128},{1,65},{65,1},{129,193},{193,129... | collective-permute-start | bytes 786440 | tf_op jit(solution)/shard_map/ppermute | solution.py:349
  100.5 10.5 %collective-permute-start.6 = (bf16[32,8,512]{2,1,0:T(8,128)(2,1)S(1)}, bf16[32,8,512]{2,1,0:T(8,128)(2,1)S(1)}, u32[]{:S(2)}, u32[]{:S(2)}) collective-permute-start(bf16[32,8,512]{2,1,0:T(8,128)(2,1)S(1)} %get-tuple-element.39.refs_0_), channel_id=1, source_target_pairs={{0,192},{64,128},{128,64},{192,0},{1,193},{65,129},{129,65},{193,1... | collective-permute-start | bytes 786440 | tf_op jit(solution)/shard_map/ppermute | solution.py:349
  103.2 16.1 %collective-permute-start.9 = (bf16[32,8,512]{2,1,0:T(8,128)(2,1)S(1)}, bf16[32,8,512]{2,1,0:T(8,128)(2,1)S(1)}, u32[]{:S(2)}, u32[]{:S(2)}) collective-permute-start(bf16[32,8,512]{2,1,0:T(8,128)(2,1)S(1)} %get-tuple-element.40.refs_1_), channel_id=1, source_target_pairs={{0,192},{64,128},{128,64},{192,0},{1,193},{65,129},{129,65},{193,1... | collective-permute-start | bytes 786440 | tf_op jit(solution)/shard_map/ppermute | solution.py:349
  104.1 15.9 %collective-permute-start.8 = (bf16[32,8,512]{2,1,0:T(8,128)(2,1)S(1)}, bf16[32,8,512]{2,1,0:T(8,128)(2,1)}, u32[]{:S(2)}, u32[]{:S(2)}) collective-permute-start(bf16[32,8,512]{2,1,0:T(8,128)(2,1)S(1)} %get-tuple-element.39.refs_0_), channel_id=1, source_target_pairs={{0,64},{64,0},{128,192},{192,128},{1,65},{65,1},{129,193},{193,129... | collective-permute-start | bytes 786440 | tf_op jit(solution)/shard_map/ppermute | solution.py:349
  104.3 1.6 %copy-start.3 = (f32[2,512,512]{2,1,0:T(8,128)S(1)}, f32[2,512,512]{2,1,0:T(8,128)}, u32[]{:S(2)}) copy-start(f32[2,512,512]{2,1,0:T(8,128)} %left_ref.4) | copy-start | bytes 6291460
  105.9 1.6 %copy-start.4 = (f32[2,512,512]{2,1,0:T(8,128)S(1)}, f32[2,512,512]{2,1,0:T(8,128)}, u32[]{:S(2)}) copy-start(f32[2,512,512]{2,1,0:T(8,128)} %right_ref.4) | copy-start | bytes 6291460
  111.0 11.7 %collective-permute-start.11 = (bf16[32,8,512]{2,1,0:T(8,128)(2,1)S(1)}, bf16[32,8,512]{2,1,0:T(8,128)(2,1)S(1)}, u32[]{:S(2)}, u32[]{:S(2)}) collective-permute-start(bf16[32,8,512]{2,1,0:T(8,128)(2,1)S(1)} %collective-permute-done.7.refs_3_), channel_id=1, source_target_pairs={{0,192},{64,128},{128,64},{192,0},{1,193},{65,129},{129,65},{193,1... | collective-permute-start | bytes 786440 | tf_op jit(solution)/shard_map/ppermute | solution.py:349
  112.9 9.8 %collective-permute-start.10 = (bf16[32,8,512]{2,1,0:T(8,128)(2,1)S(1)}, bf16[32,8,512]{2,1,0:T(8,128)(2,1)S(1)}, u32[]{:S(2)}, u32[]{:S(2)}) collective-permute-start(bf16[32,8,512]{2,1,0:T(8,128)(2,1)S(1)} %collective-permute-done.6.refs_4_), channel_id=1, source_target_pairs={{0,64},{64,0},{128,192},{192,128},{1,65},{65,1},{129,193},{193,129... | collective-permute-start | bytes 786440 | tf_op jit(solution)/shard_map/ppermute | solution.py:349
  117.8 4.9 %collective-permute-start.14 = (bf16[8,8,512]{2,1,0:T(8,128)(2,1)S(1)}, bf16[8,8,512]{2,1,0:T(8,128)(2,1)S(1)}, u32[]{:S(2)}, u32[]{:S(2)}) collective-permute-start(bf16[8,8,512]{2,1,0:T(8,128)(2,1)S(1)} %pick_second.1.refs_0_), channel_id=1, source_target_pairs={{0,128},{64,192},{128,0},{192,64},{1,129},{65,193},{129,1},{193,65... | collective-permute-start | bytes 196616 | tf_op jit(solution)/shard_map/ppermute | solution.py:349
  119.3 4.7 %collective-permute-start.13 = (bf16[8,8,512]{2,1,0:T(8,128)(2,1)S(1)}, bf16[8,8,512]{2,1,0:T(8,128)(2,1)S(1)}, u32[]{:S(2)}, u32[]{:S(2)}) collective-permute-start(bf16[8,8,512]{2,1,0:T(8,128)(2,1)S(1)} %pick_second.1.refs_0_), channel_id=1, source_target_pairs={{0,192},{64,128},{128,64},{192,0},{1,193},{65,129},{129,65},{193,1... | collective-permute-start | bytes 196616 | tf_op jit(solution)/shard_map/ppermute | solution.py:349
  119.9 4.1 %collective-permute-start.12 = (bf16[8,8,512]{2,1,0:T(8,128)(2,1)S(1)}, bf16[8,8,512]{2,1,0:T(8,128)(2,1)S(1)}, u32[]{:S(2)}, u32[]{:S(2)}) collective-permute-start(bf16[8,8,512]{2,1,0:T(8,128)(2,1)S(1)} %pick_second.1.refs_0_), channel_id=1, source_target_pairs={{0,64},{64,0},{128,192},{192,128},{1,65},{65,1},{129,193},{193,129... | collective-permute-start | bytes 196616 | tf_op jit(solution)/shard_map/ppermute | solution.py:349

commit v4 on v3

--- a/solution.py
+++ b/solution.py
@@ -56,50 +56,44 @@
 
 def first_sends(grads, group):
     rows, width = grads.shape[1:]
-    half = width // 2
+    half = group // 2
 
     def kernel(grads_ref, far_next, far_last, near_next, near_last, sems):
         _, after, before, opposite = around()
-        part = lambda g, column: grads_ref.at[pl.ds(g * group, group), :, pl.ds(column, half)]
+        part = lambda g, i: grads_ref.at[pl.ds(g * group + i * half, half)]
         pairs = [
             (part(opposite, 0), far_next),
-            (part(opposite, half), far_last),
+            (part(opposite, 1), far_last),
             (part(after, 0), near_next),
-            (part(before, half), near_last),
+            (part(before, 1), near_last),
         ]
         copy_all(pairs, sems)
 
-    outs = [shape(group, rows, half)] * 4
-    scratch = [pltpu.SemaphoreType.DMA((4,))]
-    return call(kernel, outs, [HBM], [grads], "sends", scratch)
+    outs = [shape(half, rows, width)] * 4
+    return call(kernel, outs, [HBM], [grads], "sends", [pltpu.SemaphoreType.DMA((4,))])
 
 
 def kept(grads, group):
     rows, width = grads.shape[1:]
-    half = width // 2
-
-    def kernel(grads_ref, own, left, right, sems):
+    half = group // 2
+
+    def kernel(grads_ref, own, low, high, sems):
         me, after, before, _ = around()
-        part = lambda g, column: grads_ref.at[pl.ds(g * group, group), :, pl.ds(column, half)]
-        pairs = [
-            (grads_ref.at[pl.ds(me * group, group)], own),
-            (part(before, 0), left),
-            (part(after, half), right),
-        ]
+        part = lambda g, i, count: grads_ref.at[pl.ds(g * group + i * half, count)]
+        pairs = [(part(me, 0, group), own), (part(before, 0, half), low), (part(after, 1, half), high)]
         copy_all(pairs, sems)
 
-    outs = [shape(group, rows, width)] + [shape(group, rows, half)] * 2
-    scratch = [pltpu.SemaphoreType.DMA((3,))]
-    return call(kernel, outs, [HBM], [grads], "kept", scratch)
+    outs = [shape(group, rows, width)] + [shape(half, rows, width)] * 2
+    return call(kernel, outs, [HBM], [grads], "kept", [pltpu.SemaphoreType.DMA((3,))])
 
 
 def partial_sums(kept_halves, arrived):
     dims = arrived[0].shape
 
-    def kernel(left_kept, right_kept, left_got, right_got, left, right):
+    def kernel(low_kept, high_kept, low_got, high_got, low, high):
         def step(j, _):
-            left[j] = (left_kept[j].astype(F32) + left_got[j].astype(F32)).astype(BF16)
-            right[j] = (right_kept[j].astype(F32) + right_got[j].astype(F32)).astype(BF16)
+            low[j] = (low_kept[j].astype(F32) + low_got[j].astype(F32)).astype(BF16)
+            high[j] = (high_kept[j].astype(F32) + high_got[j].astype(F32)).astype(BF16)
             return 0
 
         lax.fori_loop(0, dims[0], step, 0, unroll=8)
@@ -109,44 +103,37 @@
 
 def place_mean(table, own, near, passed, devices, replicas):
     group, rows, width = own.shape
-    half = width // 2
+    half = group // 2
     scale = 1.0 / replicas
 
     def kernel(table_ref, own_ref, *refs):
-        first, second = refs[-2:]
-        first[...] = jnp.zeros(first.shape, BF16)
-        second[...] = jnp.zeros(second.shape, BF16)
+        halves, (first, second, room) = refs[:4], refs[4:]
+        room[...] = jnp.zeros(room.shape, BF16)
         me = lax.axis_index("dp")
 
         def step(j, _):
-            entry = table_ref[me * group + j]
-            own = own_ref[j].astype(F32)
-            halves = []
-            for c in range(2):
-                total = own[:, c * half : (c + 1) * half]
-                total = total + refs[c][j].astype(F32) + refs[2 + c][j].astype(F32)
-                halves.append((total * scale).astype(BF16))
-            for slot, out in enumerate((first, second)):
-
-                @pl.when((entry & 1) == slot)
-                def _(out=out):
-                    for c in range(2):
-                        out[entry >> 1, :, c * half : (c + 1) * half] = halves[c]
-
+            for i in range(2):
+                entry = table_ref[me * group + i * half + j]
+                total = own_ref[i * half + j].astype(F32) + halves[i][j].astype(F32)
+                total = total + halves[2 + i][j].astype(F32)
+                room[(entry & 1) * devices + (entry >> 1)] = (total * scale).astype(BF16)
             return 0
 
-        lax.fori_loop(0, group, step, 0, unroll=8)
+        lax.fori_loop(0, half, step, 0, unroll=8)
+        first[...] = room[:devices]
+        second[...] = room[devices:]
 
     outs = [shape(devices, rows, width)] * 2
     args = [table, own, *near, *passed]
-    return call(kernel, outs, [SMEM] + [VMEM] * 5, args, "mean")
-
-
-def scaled_update(grad, left, right):
+    scratch = [pltpu.VMEM((2 * devices, rows, width), BF16)]
+    return call(kernel, outs, [SMEM] + [VMEM] * 5, args, "mean", scratch)
+
+
+def direction_and_scale(grad, left, right):
     part = jnp.dot(left, grad, preferred_element_type=F32).astype(BF16)
     direction = jnp.dot(part, right, preferred_element_type=F32)
     power = jnp.sum(direction * direction) * (1.0 / (direction.shape[0] * direction.shape[1]))
-    return (direction * lax.rsqrt(power + EPS)).astype(BF16)
+    return direction, lax.rsqrt(power + EPS)
 
 
 def direction_first(grad, left, right, passenger):
@@ -154,7 +141,8 @@
 
     def kernel(grad_ref, left_ref, right_ref, passenger_ref, out):
         out[:, size:] = passenger_ref[...]
-        out[:, :size] = scaled_update(grad_ref[...], left_ref[0], right_ref[0])
+        direction, scale = direction_and_scale(grad_ref[...], left_ref[0], right_ref[0])
+        out[:, :size] = (direction * scale).astype(BF16)
 
     whole = pl.BlockSpec((size, size), lambda i: (0, 0))
     slot = pl.BlockSpec((1, size, size), lambda i: (0, 0, 0))
@@ -169,11 +157,20 @@
     )(grad, left, right, passenger)
 
 
-def direction_second(mixed, left, right):
+def direction_second(mixed, left, right, parts=2):
     size = mixed.shape[0]
-
-    def kernel(grad_ref, left_ref, right_ref, out):
-        out[...] = scaled_update(grad_ref[...], left_ref[0], right_ref[0])
+    tile = size // parts
+
+    def kernel(grad_ref, left_ref, right_ref, out, room, sems):
+        direction, scale = direction_and_scale(grad_ref[...], left_ref[0], right_ref[0])
+        copies = []
+        for p in range(parts):
+            span = pl.ds(p * tile, tile)
+            room[span] = (direction[p * tile : (p + 1) * tile] * scale).astype(BF16)
+            copies.append(pltpu.make_async_copy(room.at[span], out.at[span], sems.at[p]))
+            copies[-1].start()
+        for copy in copies:
+            copy.wait()
 
     slot = pl.BlockSpec((1, size, size), lambda i: (1, 0, 0))
     return pl.pallas_call(
@@ -181,7 +178,8 @@
         out_shape=shape(size, size),
         grid=(1,),
         in_specs=[pl.BlockSpec((size, size), lambda i: (0, 1)), slot, slot],
-        out_specs=pl.BlockSpec((size, size), lambda i: (0, 0)),
+        out_specs=HBM,
+        scratch_shapes=[pltpu.VMEM((size, size), BF16), pltpu.SemaphoreType.DMA((parts,))],
         compiler_params=PARAMS,
         name="direction_second",
     )(mixed, left, right)
@@ -212,22 +210,20 @@
     )(table, pieces)
 
 
-def pick_second(table, pieces, group):
+def pick_second(table, at, pieces):
     rows, width = pieces.shape[1:]
 
-    def kernel(table_ref, pieces_ref, out, room):
+    def kernel(table_ref, at_ref, pieces_ref, out, sem):
         me = lax.axis_index("dp")
-        count = jnp.int32(0)
-        for j in range(group):
-            entry = table_ref[me * group + j]
-            room[count] = pieces_ref[entry >> 1]
-            count = count + (entry & 1)
         for i in range(SECOND):
-            out[i] = room[i]
+            owner = table_ref[at_ref[me * LIST + i]] >> 1
+            pltpu.make_async_copy(pieces_ref.at[owner], out.at[i], sem).start()
+        pltpu.make_async_copy(pieces_ref.at[pl.ds(0, SECOND)], out, sem).wait()
 
     outs = [shape(SECOND, rows, width)]
-    scratch = [pltpu.VMEM((SECOND + 1, rows, width), BF16)]
-    return call(kernel, outs, [SMEM, VMEM], [table, pieces], "pick_second", scratch)[0]
+    scratch = [pltpu.SemaphoreType.DMA]
+    args = [table, at, pieces]
+    return call(kernel, outs, [SMEM, SMEM, HBM], args, "pick_second", scratch)[0]
 
 
 def second_places(table, group, replicas):
@@ -259,42 +255,50 @@
     return call(kernel, outs, [VMEM] * len(near), near, "lay_near", scratch, [HBM])[0]
 
 
-def lay_rest(update, at, across, seconds, group):
-    replicas = len(seconds)
-
-    def kernel(at_ref, _, low, high, *refs):
-        sources, (out, sems, second_sems) = refs[:replicas], refs[replicas:]
-        groups = around()
-        start = groups[-1] * group
-        copies = [
-            pltpu.make_async_copy(ref, out.at[pl.ds(start + i * (group // 2), group // 2)], sems.at[i])
+def lay_across(update, across, group):
+    def kernel(_, low, high, out, sems):
+        start = around()[-1] * group
+        pairs = [
+            (ref, out.at[pl.ds(start + i * (group // 2), group // 2)])
             for i, ref in enumerate((low, high))
         ]
-        for copy in copies:
-            copy.start()
-        for k, g in enumerate(groups):
-            if k == replicas - 1:
-                for copy in copies:
-                    copy.wait()
+        copy_all(pairs, sems)
+
+    return pl.pallas_call(
+        kernel,
+        out_shape=shape(*update.shape),
+        in_specs=[HBM, VMEM, VMEM],
+        out_specs=HBM,
+        scratch_shapes=[pltpu.SemaphoreType.DMA((2,))],
+        input_output_aliases={0: 0},
+        compiler_params=PARAMS,
+        name="lay_across",
+    )(update, *across)
+
+
+def lay_second(update, at, seconds):
+    replicas = len(seconds)
+
+    def kernel(at_ref, _, *refs):
+        sources, (out, sems) = refs[:replicas], refs[replicas:]
+        for k, g in enumerate(around()):
             for i in range(SECOND):
                 pltpu.make_async_copy(
-                    sources[k].at[i], out.at[at_ref[g * LIST + i]], second_sems.at[k]
+                    sources[k].at[i], out.at[at_ref[g * LIST + i]], sems.at[k]
                 ).start()
         for k in range(replicas):
-            pltpu.make_async_copy(
-                sources[k], out.at[pl.ds(0, SECOND)], second_sems.at[k]
-            ).wait()
+            pltpu.make_async_copy(sources[k], out.at[pl.ds(0, SECOND)], sems.at[k]).wait()
 
     return pl.pallas_call(
         kernel,
         out_shape=shape(*update.shape),
-        in_specs=[SMEM, HBM] + [VMEM] * (2 + replicas),
+        in_specs=[SMEM, HBM] + [VMEM] * replicas,
         out_specs=HBM,
-        scratch_shapes=[pltpu.SemaphoreType.DMA((2,)), pltpu.SemaphoreType.DMA((replicas,))],
+        scratch_shapes=[pltpu.SemaphoreType.DMA((replicas,))],
         input_output_aliases={1: 0},
         compiler_params=PARAMS,
-        name="lay_rest",
-    )(at, update, *across, *seconds)
+        name="lay_second",
+    )(at, update, *seconds)
 
 
 def new_statistics(counts, grad, mixed, stats_left, stats_right, parts=2):
@@ -345,7 +349,7 @@
     blocks, rows, width = grads.shape[1:]
     slots, size = stats_left.shape[:2]
     group = blocks // replicas
-    mine = grads[0]
+    mine = pltpu.with_memory_space_constraint(grads[0], pltpu.HBM)
     send = lambda pieces, pairs: lax.ppermute(pieces, "dp", pairs)
     exchange = lambda pieces: lax.all_to_all(pieces, "fsdp", 0, 0, tiled=True)
 
@@ -355,8 +359,8 @@
     near = [send(near_next, NEXT), send(near_last, LAST)]
     at = second_places(owner_table, group, replicas)
     kept_halves, at = lax.optimization_barrier((kept_halves, at))
-    left, right = partial_sums(kept_halves, arrived)
-    passed = [send(left, LAST), send(right, NEXT)]
+    low, high = partial_sums(kept_halves, arrived)
+    passed = [send(low, LAST), send(high, NEXT)]
     first_out, second_out = place_mean(owner_table, own, near, passed, devices, replicas)
     grad_first = exchange(first_out).reshape(size, width)
     outgoing = direction_first(
@@ -376,10 +380,11 @@
     )
     last_low, next_high, stats = lax.optimization_barrier((last_low, next_high, stats))
     across = [send(last_low, NEXT), send(next_high, LAST)]
-    second_rows = pick_second(owner_table, second_back, group)
+    second_rows = pick_second(owner_table, at, second_back)
     seconds = [second_rows] + [send(second_rows, p) for p in (NEXT, LAST, OPPOSITE)]
     update = lay_near([low, high, next_low, next_high, last_low, last_high], group, replicas)
-    update = lay_rest(update, at, across, seconds, group)
+    update = lay_across(update, across, group)
+    update = lay_second(update, at, seconds)
     return (*stats, update)
 
 

time: 127 us -> 125 us (0.984)
  waiting for transfers between devices: 16.7 us -> 14.8 us
  Pallas kernels: 15.6 us -> 17.3 us
  local copies, waits for them, and re-layouts: 4.78 us -> 3.2 us
    ppermute x15, waiting for transfers between devices: 13.2 us -> 11.3 us  [local(): send = lambda pieces, pairs: lax.ppermute(pieces, 'dp', pairs)]
    pallas_call x7, Pallas kernels: 6.37 us -> 7.97 us  [call(): pl.pallas_call(kernel, out_shape=outs, in_specs=in_specs, out_specs=[VMEM...]
    unnamed x12 -> x10, local copies, waits for them, and re-layouts: 4.78 us -> 3.2 us
  transfers between devices with their start and end apart: 16 -> 16, of which waited for: 7 -> 6; matrix products, arithmetic and copies ran while one was open for 0% -> 0% of each run, Pallas kernels for 7% -> 9%
where the time goes in v4:
time: 125 us; the launch traced here: 124 us
  blocking collectives  65.4 us (52%)
  starting transfers between devices  22.1 us (18%)
  Pallas kernels  17.3 us (14%)
  waiting for transfers between devices  14.8 us (12%)
  local copies, waits for them, and re-layouts  3.2 us (3%)
  between operations  1.62 us (1%)
    all_to_all x2, blocking collectives, local(): exchange = lambda pieces: lax.all_to_all(pieces, 'fsdp', 0, 0, tiled=True)  65.4 us
    ppermute x15, starting transfers between devices, local(): send = lambda pieces, pairs: lax.ppermute(pieces, 'dp', pairs)  15.9 us
    ppermute x15, waiting for transfers between devices, local(): send = lambda pieces, pairs: lax.ppermute(pieces, 'dp', pairs)  11.3 us
    pallas_call x7, Pallas kernels, call(): pl.pallas_call(kernel, out_shape=outs, in_specs=in_specs, out_specs=[VMEM...  7.97 us
    all_to_all x1, starting transfers between devices, local(): exchange = lambda pieces: lax.all_to_all(pieces, 'fsdp', 0, 0, tiled=True)  6.21 us
    pallas_call x1, Pallas kernels, new_statistics(): pl.pallas_call(kernel, out_shape=[shape(*stats_left.shape, dtype=F32)] *...  3.53 us
    all_to_all x1, waiting for transfers between devices, local(): exchange = lambda pieces: lax.all_to_all(pieces, 'fsdp', 0, 0, tiled=True)  3.49 us
    unnamed x10, local copies, waits for them, and re-layouts  3.2 us
  transfers between devices with their start and end apart: 16, of which 6 were waited for; matrix products, arithmetic and copies ran while one was open for 0% of the time, Pallas kernels for 9%

profile of v4, /device:TPU:1, one launch (start us, length us, event | category | flops | bytes accessed | tf_op | source)
XLA Modules:
  0.0 124.4 jit_solution(5868241601525142579)
XLA Ops:
  0.6 1.2 sends.1
  1.9 2.2 %collective-permute-start.2 = (bf16[32,8,512]{2,1,0:T(8,128)(2,1)S(1)}, bf16[32,8,512]{2,1,0:T(8,128)(2,1)S(1)}, u32[]{:S(2)}, u32[]{:S(2)}) collective-permute-start(bf16[32,8,512]{2,1,0:T(8,128)(2,1)S(1)} %get-tuple-element.33), channel_id=1, source_target_pairs={{0,64},{64,0},{128,192},{192,128},{1,65},{65,1},{129,193},{193,129... | collective-permute-start | bytes 786440 | tf_op jit(solution)/shard_map/ppermute | solution.py:353
  4.1 1.9 %collective-permute-start.3 = (bf16[32,8,512]{2,1,0:T(8,128)(2,1)S(1)}, bf16[32,8,512]{2,1,0:T(8,128)(2,1)S(1)}, u32[]{:S(2)}, u32[]{:S(2)}) collective-permute-start(bf16[32,8,512]{2,1,0:T(8,128)(2,1)S(1)} %get-tuple-element.34), channel_id=1, source_target_pairs={{0,192},{64,128},{128,64},{192,0},{1,193},{65,129},{129,65},{193,1... | collective-permute-start | bytes 786440 | tf_op jit(solution)/shard_map/ppermute | solution.py:353
  6.0 0.4 collective-permute-start
  6.4 0.6 collective-permute-start.1
  7.0 1.2 kept.1
  8.2 0.0 copy-start
  8.2 0.0 copy-start.1
  8.3 1.6 %second_places.1.at_ref = s32[64]{0:T(128)S(1)} custom-call(s32[256]{0:T(256)S(1)} %copy-done.4), custom_call_target="tpu_custom_call" | custom-call | tf_op jit(solution)/shard_map/second_places/pallas_call | solution.py:30
  9.9 0.0 collective-permute-done.2.low_got
  9.9 2.0 %collective-permute-done.3.high_got = bf16[32,8,512]{2,1,0:T(8,128)(2,1)S(1)} collective-permute-done((bf16[32,8,512]{2,1,0:T(8,128)(2,1)S(1)}, bf16[32,8,512]{2,1,0:T(8,128)(2,1)S(1)}, u32[]{:S(2)}, u32[]{:S(2)}) %collective-permute-start.3) | collective-permute-done | bytes 262176 | tf_op jit(solution)/shard_map/ppermute | solution.py:353
  11.9 0.1 partial.1
  12.0 2.3 %collective-permute-start.4 = (bf16[32,8,512]{2,1,0:T(8,128)(2,1)S(1)}, bf16[32,8,512]{2,1,0:T(8,128)(2,1)S(1)}, u32[]{:S(2)}, u32[]{:S(2)}) collective-permute-start(bf16[32,8,512]{2,1,0:T(8,128)(2,1)S(1)} %get-tuple-element.35), channel_id=1, source_target_pairs={{0,192},{64,128},{128,64},{192,0},{1,193},{65,129},{129,65},{193,1... | collective-permute-start | bytes 786440 | tf_op jit(solution)/shard_map/ppermute | solution.py:353
  14.3 0.0 collective-permute-start.5
  14.3 0.2 collective-permute-done.refs_0_
  14.5 3.0 %collective-permute-done.1.refs_1_ = bf16[32,8,512]{2,1,0:T(8,128)(2,1)S(1)} collective-permute-done((bf16[32,8,512]{2,1,0:T(8,128)(2,1)S(1)}, bf16[32,8,512]{2,1,0:T(8,128)(2,1)S(1)}, u32[]{:S(2)}, u32[]{:S(2)}) %collective-permute-start.1) | collective-permute-done | bytes 262176 | tf_op jit(solution)/shard_map/ppermute | solution.py:353
  17.5 5.6 %collective-permute-done.4.refs_2_ = bf16[32,8,512]{2,1,0:T(8,128)(2,1)S(1)} collective-permute-done((bf16[32,8,512]{2,1,0:T(8,128)(2,1)S(1)}, bf16[32,8,512]{2,1,0:T(8,128)(2,1)S(1)}, u32[]{:S(2)}, u32[]{:S(2)}) %collective-permute-start.4) | collective-permute-done | bytes 262176 | tf_op jit(solution)/shard_map/ppermute | solution.py:353
  23.1 0.0 collective-permute-done.5.refs_3_
  23.1 0.9 mean.1
  24.1 30.7 %all_to_all.15 = bf16[64,8,512]{2,1,0:T(8,128)(2,1)S(1)} all-to-all(bf16[64,8,512]{2,1,0:T(8,128)(2,1)S(1)} %get-tuple-element.37), channel_id=1, replica_groups=mesh['dp'=4,'fsdp'=64] {'fsdp'}, dimensions={0} | all-to-all | bytes 1048576 | tf_op jit(solution)/shard_map/all_to_all | solution.py:354
  54.8 1.1 direction_first.1
  55.9 34.6 %all_to_all.16.pieces_ref = bf16[64,8,1024]{2,1,0:T(8,128)(2,1)S(1)} all-to-all(bf16[64,8,1024]{2,1,0:T(8,128)(2,1)S(1)} %bitcast.12), channel_id=1, replica_groups=mesh['dp'=4,'fsdp'=64] {'fsdp'}, dimensions={0} | all-to-all | bytes 2097152 | tf_op jit(solution)/shard_map/all_to_all | solution.py:354
  90.6 1.9 %direction_second.1 = bf16[512,512]{1,0:T(8,128)(2,1)} custom-call(bf16[512,1024]{1,0:T(8,128)(2,1)S(1)} %bitcast.8, bf16[2,512,512]{2,1,0:T(8,128)(2,1)S(1)} %copy-done, bf16[2,512,512]{2,1,0:T(8,128)(2,1)S(1)} %copy-done.1), custom_call_target="tpu_custom_call" | custom-call | tf_op jit(solution)/shard_map/direction_second/pallas_call | solution.py:176
  92.5 6.2 %all-to-all-start.2 = ((bf16[64,8,512]{2,1,0:T(8,128)(2,1)}), bf16[64,8,512]{2,1,0:T(8,128)(2,1)S(1)}, u32[]{:S(2)}, u32[]{:S(2)}) async-start(bf16[64,8,512]{2,1,0:T(8,128)(2,1)} %bitcast.6), calls=%async_computation.2 | async-start | bytes 1048576 | tf_op jit(solution)/shard_map/all_to_all | solution.py:354
  98.7 0.7 pick_first.1
  99.4 0.1 collective-permute-start.7
  99.5 2.0 %collective-permute-start.6 = (bf16[32,8,512]{2,1,0:T(8,128)(2,1)S(1)}, bf16[32,8,512]{2,1,0:T(8,128)(2,1)S(1)}, u32[]{:S(2)}, u32[]{:S(2)}) collective-permute-start(bf16[32,8,512]{2,1,0:T(8,128)(2,1)S(1)} %get-tuple-element.39.refs_0_), channel_id=1, source_target_pairs={{0,192},{64,128},{128,64},{192,0},{1,193},{65,129},{129,65},{193,1... | collective-permute-start | bytes 786440 | tf_op jit(solution)/shard_map/ppermute | solution.py:353
  102.1 0.9 collective-permute-start.9
  103.0 0.3 collective-permute-start.8
  103.2 1.6 %copy-done.2 = f32[2,512,512]{2,1,0:T(8,128)S(1)} copy-done((f32[2,512,512]{2,1,0:T(8,128)S(1)}, f32[2,512,512]{2,1,0:T(8,128)}, u32[]{:S(2)}) %copy-start.2) | copy-done | bytes 2097176
  104.8 1.6 %copy-done.3 = f32[2,512,512]{2,1,0:T(8,128)S(1)} copy-done((f32[2,512,512]{2,1,0:T(8,128)S(1)}, f32[2,512,512]{2,1,0:T(8,128)}, u32[]{:S(2)}) %copy-start.3) | copy-done | bytes 2097176
  106.4 3.5 %statistics.1 = (f32[2,512,512]{2,1,0:T(8,128)}, f32[2,512,512]{2,1,0:T(8,128)}) custom-call(s32[1]{0:T(128)} %bitcast.7.counts_ref, bf16[512,512]{1,0:T(8,128)(2,1)S(1)} %bitcast.11, bf16[512,1024]{1,0:T(8,128)(2,1)S(1)} %bitcast.9, f32[2,512,512]{2,1,0:T(8,128)S(1)} %copy-done.2, f32[2,512,512]{2,1,0:T(8,128)S(1)} %copy-done.3), custom_call_target="tpu_custom_call" | custom-call | flops 1073741824 | bytes 8388608 | tf_op jit(solution)/shard_map/statistics/pallas_call | solution.py:332
  110.0 0.0 collective-permute-done.7.refs_3_
  110.0 0.0 collective-permute-done.6.refs_4_
  110.0 1.9 %collective-permute-start.11 = (bf16[32,8,512]{2,1,0:T(8,128)(2,1)S(1)}, bf16[32,8,512]{2,1,0:T(8,128)(2,1)S(1)}, u32[]{:S(2)}, u32[]{:S(2)}) collective-permute-start(bf16[32,8,512]{2,1,0:T(8,128)(2,1)S(1)} %collective-permute-done.7.refs_3_), channel_id=1, source_target_pairs={{0,192},{64,128},{128,64},{192,0},{1,193},{65,129},{129,65},{193,1... | collective-permute-start | bytes 786440 | tf_op jit(solution)/shard_map/ppermute | solution.py:353
  111.8 0.7 collective-permute-start.10
  112.5 3.5 %all-to-all-done.2.pieces_ref = bf16[64,8,512]{2,1,0:T(8,128)(2,1)S(1)} async-done(((bf16[64,8,512]{2,1,0:T(8,128)(2,1)}), bf16[64,8,512]{2,1,0:T(8,128)(2,1)S(1)}, u32[]{:S(2)}, u32[]{:S(2)}) %all-to-all-start.2) | async-done | bytes 524320 | tf_op jit(solution)/shard_map/all_to_all | solution.py:354
  116.0 0.7 pick_second.1.refs_0_
  116.7 1.5 %collective-permute-start.14 = (bf16[8,8,512]{2,1,0:T(8,128)(2,1)S(1)}, bf16[8,8,512]{2,1,0:T(8,128)(2,1)S(1)}, u32[]{:S(2)}, u32[]{:S(2)}) collective-permute-start(bf16[8,8,512]{2,1,0:T(8,128)(2,1)S(1)} %pick_second.1.refs_0_), channel_id=1, source_target_pairs={{0,128},{64,192},{128,0},{192,64},{1,129},{65,193},{129,1},{193,65... | collective-permute-start | bytes 196616 | tf_op jit(solution)/shard_map/ppermute | solution.py:353
  118.2 0.6 collective-permute-start.13
  118.8 0.0 collective-permute-done.8.refs_2_
  118.9 0.6 collective-permute-start.12
  119.5 2.1 %lay_near.1._ = bf16[256,8,512]{2,1,0:T(8,128)(2,1)} custom-call(bf16[32,8,512]{2,1,0:T(8,128)(2,1)S(1)} %get-tuple-element.39.refs_0_, bf16[32,8,512]{2,1,0:T(8,128)(2,1)S(1)} %get-tuple-element.40.refs_1_, bf16[32,8,512]{2,1,0:T(8,128)(2,1)} %collective-permute-done.8.refs_2_, bf16[32,8,512]{2,1,0:T(8,128)(2,1)S(1)} %collective-permute-done.7.refs_3_, ...), custom_call_target="tpu_custom_call" | custom-call | tf_op jit(solution)/shard_map/lay_near/pallas_call | solution.py:30
  121.6 0.0 collective-permute-done.11.high
  121.6 0.8 lay_across.1._
  122.5 0.4 collective-permute-done.13.refs_2_
  122.9 0.0 collective-permute-done.12.refs_1_
  122.9 1.3 %lay_second.1 = bf16[256,8,512]{2,1,0:T(8,128)(2,1)} custom-call(s32[64]{0:T(128)S(1)} %second_places.1.at_ref, bf16[256,8,512]{2,1,0:T(8,128)(2,1)} %lay_across.1._, bf16[8,8,512]{2,1,0:T(8,128)(2,1)S(1)} %pick_second.1.refs_0_, bf16[8,8,512]{2,1,0:T(8,128)(2,1)S(1)} %collective-permute-done.12.refs_1_, ...), custom_call_target="tpu_custom_call", output_to_operand_aliasing={{}: (1, {})} | custom-call | tf_op jit(solution)/shard_map/lay_second/pallas_call | solution.py:292
  (9 shorter events, 0.0 us)
Async XLA Ops:
  0.6 7.6 %copy-start.4 = (s32[256]{0:T(256)S(1)}, s32[256]{0:T(256)}, u32[]{:S(2)}) copy-start(s32[256]{0:T(256)} %table_ref.7) | copy-start | bytes 3076
  1.9 8.0 %collective-permute-start.2 = (bf16[32,8,512]{2,1,0:T(8,128)(2,1)S(1)}, bf16[32,8,512]{2,1,0:T(8,128)(2,1)S(1)}, u32[]{:S(2)}, u32[]{:S(2)}) collective-permute-start(bf16[32,8,512]{2,1,0:T(8,128)(2,1)S(1)} %get-tuple-element.33), channel_id=1, source_target_pairs={{0,64},{64,0},{128,192},{192,128},{1,65},{65,1},{129,193},{193,129... | collective-permute-start | bytes 786440 | tf_op jit(solution)/shard_map/ppermute | solution.py:353
  4.1 7.8 %collective-permute-start.3 = (bf16[32,8,512]{2,1,0:T(8,128)(2,1)S(1)}, bf16[32,8,512]{2,1,0:T(8,128)(2,1)S(1)}, u32[]{:S(2)}, u32[]{:S(2)}) collective-permute-start(bf16[32,8,512]{2,1,0:T(8,128)(2,1)S(1)} %get-tuple-element.34), channel_id=1, source_target_pairs={{0,192},{64,128},{128,64},{192,0},{1,193},{65,129},{129,65},{193,1... | collective-permute-start | bytes 786440 | tf_op jit(solution)/shard_map/ppermute | solution.py:353
  6.0 8.5 %collective-permute-start = (bf16[32,8,512]{2,1,0:T(8,128)(2,1)S(1)}, bf16[32,8,512]{2,1,0:T(8,128)(2,1)S(1)}, u32[]{:S(2)}, u32[]{:S(2)}) collective-permute-start(bf16[32,8,512]{2,1,0:T(8,128)(2,1)S(1)} %get-tuple-element.27), channel_id=1, source_target_pairs={{0,64},{64,0},{128,192},{192,128},{1,65},{65,1},{129,193},{193,129... | collective-permute-start | bytes 786440 | tf_op jit(solution)/shard_map/ppermute | solution.py:353
  6.4 11.1 %collective-permute-start.1 = (bf16[32,8,512]{2,1,0:T(8,128)(2,1)S(1)}, bf16[32,8,512]{2,1,0:T(8,128)(2,1)S(1)}, u32[]{:S(2)}, u32[]{:S(2)}) collective-permute-start(bf16[32,8,512]{2,1,0:T(8,128)(2,1)S(1)} %get-tuple-element.28), channel_id=1, source_target_pairs={{0,192},{64,128},{128,64},{192,0},{1,193},{65,129},{129,65},{193,1... | collective-permute-start | bytes 786440 | tf_op jit(solution)/shard_map/ppermute | solution.py:353
  8.2 46.6 %copy-start = (bf16[2,512,512]{2,1,0:T(8,128)(2,1)S(1)}, bf16[2,512,512]{2,1,0:T(8,128)(2,1)}, u32[]{:S(2)}) copy-start(bf16[2,512,512]{2,1,0:T(8,128)(2,1)} %left_ref.5) | copy-start | bytes 3145732
  8.2 46.6 %copy-start.1 = (bf16[2,512,512]{2,1,0:T(8,128)(2,1)S(1)}, bf16[2,512,512]{2,1,0:T(8,128)(2,1)}, u32[]{:S(2)}) copy-start(bf16[2,512,512]{2,1,0:T(8,128)(2,1)} %right_ref.5) | copy-start | bytes 3145732
  12.0 11.1 %collective-permute-start.4 = (bf16[32,8,512]{2,1,0:T(8,128)(2,1)S(1)}, bf16[32,8,512]{2,1,0:T(8,128)(2,1)S(1)}, u32[]{:S(2)}, u32[]{:S(2)}) collective-permute-start(bf16[32,8,512]{2,1,0:T(8,128)(2,1)S(1)} %get-tuple-element.35), channel_id=1, source_target_pairs={{0,192},{64,128},{128,64},{192,0},{1,193},{65,129},{129,65},{193,1... | collective-permute-start | bytes 786440 | tf_op jit(solution)/shard_map/ppermute | solution.py:353
  14.3 8.8 %collective-permute-start.5 = (bf16[32,8,512]{2,1,0:T(8,128)(2,1)S(1)}, bf16[32,8,512]{2,1,0:T(8,128)(2,1)S(1)}, u32[]{:S(2)}, u32[]{:S(2)}) collective-permute-start(bf16[32,8,512]{2,1,0:T(8,128)(2,1)S(1)} %get-tuple-element.36), channel_id=1, source_target_pairs={{0,64},{64,0},{128,192},{192,128},{1,65},{65,1},{129,193},{193,129... | collective-permute-start | bytes 786440 | tf_op jit(solution)/shard_map/ppermute | solution.py:353
  92.5 23.5 %all-to-all-start.2 = ((bf16[64,8,512]{2,1,0:T(8,128)(2,1)}), bf16[64,8,512]{2,1,0:T(8,128)(2,1)S(1)}, u32[]{:S(2)}, u32[]{:S(2)}) async-start(bf16[64,8,512]{2,1,0:T(8,128)(2,1)} %bitcast.6), calls=%async_computation.2 | async-start | bytes 1048576 | tf_op jit(solution)/shard_map/all_to_all | solution.py:354
  99.4 10.6 %collective-permute-start.7 = (bf16[32,8,512]{2,1,0:T(8,128)(2,1)S(1)}, bf16[32,8,512]{2,1,0:T(8,128)(2,1)S(1)}, u32[]{:S(2)}, u32[]{:S(2)}) collective-permute-start(bf16[32,8,512]{2,1,0:T(8,128)(2,1)S(1)} %get-tuple-element.40.refs_1_), channel_id=1, source_target_pairs={{0,64},{64,0},{128,192},{192,128},{1,65},{65,1},{129,193},{193,129... | collective-permute-start | bytes 786440 | tf_op jit(solution)/shard_map/ppermute | solution.py:353
  99.5 10.5 %collective-permute-start.6 = (bf16[32,8,512]{2,1,0:T(8,128)(2,1)S(1)}, bf16[32,8,512]{2,1,0:T(8,128)(2,1)S(1)}, u32[]{:S(2)}, u32[]{:S(2)}) collective-permute-start(bf16[32,8,512]{2,1,0:T(8,128)(2,1)S(1)} %get-tuple-element.39.refs_0_), channel_id=1, source_target_pairs={{0,192},{64,128},{128,64},{192,0},{1,193},{65,129},{129,65},{193,1... | collective-permute-start | bytes 786440 | tf_op jit(solution)/shard_map/ppermute | solution.py:353
  102.1 16.1 %collective-permute-start.9 = (bf16[32,8,512]{2,1,0:T(8,128)(2,1)S(1)}, bf16[32,8,512]{2,1,0:T(8,128)(2,1)S(1)}, u32[]{:S(2)}, u32[]{:S(2)}) collective-permute-start(bf16[32,8,512]{2,1,0:T(8,128)(2,1)S(1)} %get-tuple-element.40.refs_1_), channel_id=1, source_target_pairs={{0,192},{64,128},{128,64},{192,0},{1,193},{65,129},{129,65},{193,1... | collective-permute-start | bytes 786440 | tf_op jit(solution)/shard_map/ppermute | solution.py:353
  103.0 15.9 %collective-permute-start.8 = (bf16[32,8,512]{2,1,0:T(8,128)(2,1)S(1)}, bf16[32,8,512]{2,1,0:T(8,128)(2,1)}, u32[]{:S(2)}, u32[]{:S(2)}) collective-permute-start(bf16[32,8,512]{2,1,0:T(8,128)(2,1)S(1)} %get-tuple-element.39.refs_0_), channel_id=1, source_target_pairs={{0,64},{64,0},{128,192},{192,128},{1,65},{65,1},{129,193},{193,129... | collective-permute-start | bytes 786440 | tf_op jit(solution)/shard_map/ppermute | solution.py:353
  103.2 1.6 %copy-start.2 = (f32[2,512,512]{2,1,0:T(8,128)S(1)}, f32[2,512,512]{2,1,0:T(8,128)}, u32[]{:S(2)}) copy-start(f32[2,512,512]{2,1,0:T(8,128)} %left_ref.4) | copy-start | bytes 6291460
  104.8 1.6 %copy-start.3 = (f32[2,512,512]{2,1,0:T(8,128)S(1)}, f32[2,512,512]{2,1,0:T(8,128)}, u32[]{:S(2)}) copy-start(f32[2,512,512]{2,1,0:T(8,128)} %right_ref.4) | copy-start | bytes 6291460
  110.0 11.7 %collective-permute-start.11 = (bf16[32,8,512]{2,1,0:T(8,128)(2,1)S(1)}, bf16[32,8,512]{2,1,0:T(8,128)(2,1)S(1)}, u32[]{:S(2)}, u32[]{:S(2)}) collective-permute-start(bf16[32,8,512]{2,1,0:T(8,128)(2,1)S(1)} %collective-permute-done.7.refs_3_), channel_id=1, source_target_pairs={{0,192},{64,128},{128,64},{192,0},{1,193},{65,129},{129,65},{193,1... | collective-permute-start | bytes 786440 | tf_op jit(solution)/shard_map/ppermute | solution.py:353
  111.8 9.8 %collective-permute-start.10 = (bf16[32,8,512]{2,1,0:T(8,128)(2,1)S(1)}, bf16[32,8,512]{2,1,0:T(8,128)(2,1)S(1)}, u32[]{:S(2)}, u32[]{:S(2)}) collective-permute-start(bf16[32,8,512]{2,1,0:T(8,128)(2,1)S(1)} %collective-permute-done.6.refs_4_), channel_id=1, source_target_pairs={{0,64},{64,0},{128,192},{192,128},{1,65},{65,1},{129,193},{193,129... | collective-permute-start | bytes 786440 | tf_op jit(solution)/shard_map/ppermute | solution.py:353
  116.7 5.7 %collective-permute-start.14 = (bf16[8,8,512]{2,1,0:T(8,128)(2,1)S(1)}, bf16[8,8,512]{2,1,0:T(8,128)(2,1)S(1)}, u32[]{:S(2)}, u32[]{:S(2)}) collective-permute-start(bf16[8,8,512]{2,1,0:T(8,128)(2,1)S(1)} %pick_second.1.refs_0_), channel_id=1, source_target_pairs={{0,128},{64,192},{128,0},{192,64},{1,129},{65,193},{129,1},{193,65... | collective-permute-start | bytes 196616 | tf_op jit(solution)/shard_map/ppermute | solution.py:353
  118.2 4.7 %collective-permute-start.13 = (bf16[8,8,512]{2,1,0:T(8,128)(2,1)S(1)}, bf16[8,8,512]{2,1,0:T(8,128)(2,1)S(1)}, u32[]{:S(2)}, u32[]{:S(2)}) collective-permute-start(bf16[8,8,512]{2,1,0:T(8,128)(2,1)S(1)} %pick_second.1.refs_0_), channel_id=1, source_target_pairs={{0,192},{64,128},{128,64},{192,0},{1,193},{65,129},{129,65},{193,1... | collective-permute-start | bytes 196616 | tf_op jit(solution)/shard_map/ppermute | solution.py:353
  118.9 4.1 %collective-permute-start.12 = (bf16[8,8,512]{2,1,0:T(8,128)(2,1)S(1)}, bf16[8,8,512]{2,1,0:T(8,128)(2,1)S(1)}, u32[]{:S(2)}, u32[]{:S(2)}) collective-permute-start(bf16[8,8,512]{2,1,0:T(8,128)(2,1)S(1)} %pick_second.1.refs_0_), channel_id=1, source_target_pairs={{0,64},{64,0},{128,192},{192,128},{1,65},{65,1},{129,193},{193,129... | collective-permute-start | bytes 196616 | tf_op jit(solution)/shard_map/ppermute | solution.py:353

commit v5 on v4

v5 whole, which is shorter than its diff:
```python
import jax
import jax.numpy as jnp
from jax import lax
from jax.experimental import pallas as pl
from jax.experimental.pallas import tpu as pltpu
from jax.sharding import PartitionSpec as P

BETA = 0.9
EPS = 1e-06
BF16 = jnp.bfloat16
F32 = jnp.float32

NEXT = [(i, i ^ 1) for i in range(4)]
LAST = [(i, 3 - i) for i in range(4)]
OPPOSITE = [(i, i ^ 2) for i in range(4)]
SECOND = 8
LIST = 16

VMEM = pl.BlockSpec(memory_space=pltpu.VMEM)
SMEM = pl.BlockSpec(memory_space=pltpu.SMEM)
HBM = pl.BlockSpec(memory_space=pltpu.HBM)
PARAMS = pltpu.CompilerParams(vmem_limit_bytes=16 * 1024 * 1024)


def shape(*dims, dtype=BF16):
    return jax.ShapeDtypeStruct(dims, dtype)


def call(kernel, outs, in_specs, args, name, scratch=(), out_specs=None):
    return pl.pallas_call(
        kernel,
        out_shape=outs,
        in_specs=in_specs,
        out_specs=[VMEM] * len(outs) if out_specs is None else out_specs,
        scratch_shapes=scratch,
        compiler_params=PARAMS,
        name=name,
    )(*args)


def around():
    me = lax.axis_index("dp")
    return me, me ^ 1, 3 - me, me ^ 2


def copy_all(pairs, sems):
    copies = [
        pltpu.make_async_copy(source, target, sems.at[i])
        for i, (source, target) in enumerate(pairs)
    ]
    for copy in copies:
        copy.start()
    for copy in copies:
        copy.wait()


def first_sends(grads, group, far):
    rows, width = grads.shape[1:]
    half = group // 2

    def kernel(grads_ref, to_next, to_last, sems):
        _, after, before, opposite = around()
        groups = (opposite, opposite) if far else (after, before)
        pairs = [
            (grads_ref.at[pl.ds(g * group + i * half, half)], out)
            for i, (g, out) in enumerate(zip(groups, (to_next, to_last)))
        ]
        copy_all(pairs, sems)

    outs = [shape(half, rows, width)] * 2
    name = "far_sends" if far else "near_sends"
    return call(kernel, outs, [HBM], [grads], name, [pltpu.SemaphoreType.DMA((2,))])


def kept(grads, group):
    rows, width = grads.shape[1:]
    half = group // 2

    def kernel(grads_ref, own, low, high, sems):
        me, after, before, _ = around()
        part = lambda g, i, count: grads_ref.at[pl.ds(g * group + i * half, count)]
        pairs = [(part(me, 0, group), own), (part(before, 0, half), low), (part(after, 1, half), high)]
        copy_all(pairs, sems)

    outs = [shape(group, rows, width)] + [shape(half, rows, width)] * 2
    return call(kernel, outs, [HBM], [grads], "kept", [pltpu.SemaphoreType.DMA((3,))])


def partial_sums(kept_halves, arrived):
    dims = arrived[0].shape

    def kernel(low_kept, high_kept, low_got, high_got, low, high):
        def step(j, _):
            low[j] = (low_kept[j].astype(F32) + low_got[j].astype(F32)).astype(BF16)
            high[j] = (high_kept[j].astype(F32) + high_got[j].astype(F32)).astype(BF16)
            return 0

        lax.fori_loop(0, dims[0], step, 0, unroll=8)

    return call(kernel, [shape(*dims)] * 2, [VMEM] * 4, [*kept_halves, *arrived], "partial")


def place_mean(table, own, near, passed, devices, slots, replicas):
    group, rows, width = own.shape
    half = group // 2
    scale = 1.0 / replicas

    def kernel(table_ref, own_ref, *refs):
        halves, out = refs[:4], refs[4]
        out[...] = jnp.zeros(out.shape, BF16)
        me = lax.axis_index("dp")

        def step(j, _):
            for i in range(2):
                entry = table_ref[me * group + i * half + j]
                total = own_ref[i * half + j].astype(F32) + halves[i][j].astype(F32)
                total = total + halves[2 + i][j].astype(F32)
                column = pl.multiple_of((entry & 1) * width, width)
                out[entry >> 1, :, pl.ds(column, width)] = (total * scale).astype(BF16)
            return 0

        lax.fori_loop(0, half, step, 0, unroll=8)

    outs = [shape(devices, rows, slots * width)]
    args = [table, own, *near, *passed]
    return call(kernel, outs, [SMEM] + [VMEM] * 5, args, "mean")[0]


def precondition(grads, left, right):
    size = left.shape[1]

    def kernel(grads_ref, left_ref, right_ref, first, second, room, sem):
        def scaled(slot):
            grad = grads_ref[:, slot * size : (slot + 1) * size]
            part = jnp.dot(left_ref[slot], grad, preferred_element_type=F32).astype(BF16)
            direction = jnp.dot(part, right_ref[slot], preferred_element_type=F32)
            power = jnp.sum(direction * direction) * (1.0 / (size * size))
            return (direction * lax.rsqrt(power + EPS)).astype(BF16)

        room[...] = scaled(1)
        copy = pltpu.make_async_copy(room, second, sem)
        copy.start()
        first[...] = scaled(0)
        copy.wait()

    outs = [shape(size, size)] * 2
    scratch = [pltpu.VMEM((size, size), BF16), pltpu.SemaphoreType.DMA]
    args = [grads, left, right]
    return call(kernel, outs, [VMEM] * 3, args, "direction", scratch, [VMEM, HBM])


def pick_first(table, first, pieces, group):
    rows, width = pieces.shape[1:]
    half = (group - SECOND) // 2

    def kernel(table_ref, first_ref, pieces_ref, *outs):
        start = lax.axis_index("dp") * group

        def step(j, _):
            for i, out in enumerate(outs):
                block = first_ref[start + i * half + j]
                out[j] = pieces_ref[table_ref[start + block] >> 1]
            return 0

        lax.fori_loop(0, half, step, 0, unroll=4)

    return pl.pallas_call(
        kernel,
        out_shape=[shape(half, rows, width)] * 2,
        grid=(1,),
        in_specs=[SMEM, SMEM, pl.BlockSpec((pieces.shape[0], rows, width), lambda i: (0, 0, 0))],
        out_specs=[pl.BlockSpec((half, rows, width), lambda i: (0, 0, 0))] * 2,
        compiler_params=PARAMS,
        name="pick_first",
    )(table, first, pieces)


def pick_second(table, at, pieces):
    rows, width = pieces.shape[1:]

    def kernel(table_ref, at_ref, pieces_ref, out, sem):
        me = lax.axis_index("dp")
        for i in range(SECOND):
            owner = table_ref[at_ref[me * LIST + i]] >> 1
            pltpu.make_async_copy(pieces_ref.at[owner], out.at[i], sem).start()
        pltpu.make_async_copy(pieces_ref.at[pl.ds(0, SECOND)], out, sem).wait()

    outs = [shape(SECOND, rows, width)]
    scratch = [pltpu.SemaphoreType.DMA]
    args = [table, at, pieces]
    return call(kernel, outs, [SMEM, SMEM, HBM], args, "pick_second", scratch)[0]


def block_lists(table, group, replicas):
    def kernel(table_ref, first, at):
        for g in range(replicas):
            in_first = jnp.int32(0)
            in_second = jnp.int32(0)
            for j in range(group):
                odd = table_ref[g * group + j] & 1
                first[g * group + in_first] = j
                at[g * LIST + in_second] = g * group + j
                in_first = in_first + (1 - odd)
                in_second = in_second + odd

    outs = [shape(replicas * n, dtype=jnp.int32) for n in (group, LIST)]
    return call(kernel, outs, [SMEM], [table], "block_lists", out_specs=[SMEM, SMEM])


def lay(first, groups, halves, group, update_shape, update=None):
    half, rows, width = halves[0].shape
    given = 0 if update is None else 1

    def kernel(first_ref, *refs):
        refs = refs[given:]
        sources, (out, room, sems) = refs[:-3], refs[-3:]
        places = around()
        copies = []
        for k, at in enumerate(groups):
            g = places[at]

            def step(j, _, k=k, g=g):
                for i in range(2):
                    block = first_ref[g * group + i * half + j]
                    room[k * group + block] = sources[2 * k + i][j]
                return 0

            lax.fori_loop(0, half, step, 0, unroll=4)
            source = room.at[pl.ds(k * group, group)]
            copies.append(
                pltpu.make_async_copy(source, out.at[pl.ds(g * group, group)], sems.at[k])
            )
            copies[-1].start()
        for copy in copies:
            copy.wait()

    return pl.pallas_call(
        kernel,
        out_shape=shape(*update_shape),
        in_specs=[SMEM] + [HBM] * given + [VMEM] * len(halves),
        out_specs=HBM,
        scratch_shapes=[
            pltpu.VMEM((len(groups) * group, rows, width), BF16),
            pltpu.SemaphoreType.DMA((len(groups),)),
        ],
        input_output_aliases={1: 0} if given else {},
        compiler_params=PARAMS,
        name="lay",
    )(first, *([update] if given else []), *halves)


def lay_second(update, at, seconds):
    replicas = len(seconds)

    def kernel(at_ref, _, *refs):
        sources, (out, sems) = refs[:replicas], refs[replicas:]
        for k, g in enumerate(around()):
            for i in range(SECOND):
                pltpu.make_async_copy(
                    sources[k].at[i], out.at[at_ref[g * LIST + i]], sems.at[k]
                ).start()
        for k in range(replicas):
            pltpu.make_async_copy(sources[k], out.at[pl.ds(0, SECOND)], sems.at[k]).wait()

    return pl.pallas_call(
        kernel,
        out_shape=shape(*update.shape),
        in_specs=[SMEM, HBM] + [VMEM] * replicas,
        out_specs=HBM,
        scratch_shapes=[pltpu.SemaphoreType.DMA((replicas,))],
        input_output_aliases={1: 0},
        compiler_params=PARAMS,
        name="lay_second",
    )(at, update, *seconds)


def new_statistics(counts, grads, stats_left, stats_right, parts=2):
    slots, size = stats_left.shape[:2]
    tile = size // parts

    def kernel(counts_ref, grads_ref, left_ref, right_ref, new_left_ref, new_right_ref):
        live = counts_ref[0] > pl.program_id(0)
        for p in range(parts):

            @pl.when(pl.program_id(1) == p)
            def _(p=p):
                grad = grads_ref[...]
                span = slice(p * tile, (p + 1) * tile)
                gram_left = lax.dot_general(
                    grad[span], grad, (((1,), (1,)), ((), ())), preferred_element_type=F32
                )
                gram_right = lax.dot_general(
                    grad[:, span], grad, (((0,), (0,)), ((), ())), preferred_element_type=F32
                )
                old_left, old_right = left_ref[0], right_ref[0]
                new_left_ref[0] = jnp.where(
                    live, BETA * old_left + (1.0 - BETA) * gram_left, old_left
                )
                new_right_ref[0] = jnp.where(
                    live, BETA * old_right + (1.0 - BETA) * gram_right, old_right
                )

    block = pl.BlockSpec((size, size), lambda s, t: (0, s))
    part = pl.BlockSpec((1, tile, size), lambda s, t: (s, t, 0))
    return pl.pallas_call(
        kernel,
        out_shape=[shape(*stats_left.shape, dtype=F32)] * 2,
        grid=(slots, parts),
        in_specs=[SMEM, block, part, part],
        out_specs=[part, part],
        compiler_params=PARAMS,
        cost_estimate=pl.CostEstimate(
            flops=8 * size**3, bytes_accessed=16 * 2 * size * size, transcendentals=0
        ),
        name="statistics",
    )(counts, grads, stats_left, stats_right)


def local(grads, stats_left, stats_right, precond_left, precond_right, owner_table, block_counts):
    devices = lax.axis_size("fsdp")
    replicas = lax.axis_size("dp")
    blocks, rows, width = grads.shape[1:]
    slots, size = stats_left.shape[:2]
    group = blocks // replicas
    mine = pltpu.with_memory_space_constraint(grads[0], pltpu.HBM)
    send = lambda pieces, pairs: lax.ppermute(pieces, "dp", pairs)
    exchange = lambda pieces: lax.all_to_all(pieces, "fsdp", 0, 0, tiled=True)

    far_next, far_last = first_sends(mine, group, True)
    near_next, near_last = first_sends(mine, group, False)
    own, *kept_halves = kept(mine, group)
    arrived = [send(far_next, NEXT), send(far_last, LAST)]
    near = [send(near_next, NEXT), send(near_last, LAST)]
    first, at = block_lists(owner_table, group, replicas)
    kept_halves, first, at = lax.optimization_barrier((kept_halves, first, at))
    low, high = partial_sums(kept_halves, arrived)
    passed = [send(low, LAST), send(high, NEXT)]
    outgoing = place_mean(owner_table, own, near, passed, devices, slots, replicas)
    owned = exchange(outgoing).reshape(size, slots * width)
    scaled_first, scaled_second = precondition(owned, precond_left, precond_right)
    first_back = exchange(scaled_first.reshape(devices, rows, width))
    scaled_second, first_back = lax.optimization_barrier((scaled_second, first_back))
    second_back = exchange(scaled_second.reshape(devices, rows, width))

    low, high = pick_first(owner_table, first, first_back, group)
    last_low, next_high = send(low, LAST), send(high, NEXT)
    next_low, last_high = send(low, NEXT), send(high, LAST)
    owned, _ = lax.optimization_barrier((owned, low))
    old_left, old_right = (
        pltpu.with_memory_space_constraint(old, pltpu.HBM) for old in (stats_left, stats_right)
    )
    stats = new_statistics(
        block_counts.reshape(1), owned, old_left, old_right
    )
    last_low, next_high, stats = lax.optimization_barrier((last_low, next_high, stats))
    across = [send(last_low, NEXT), send(next_high, LAST)]
    second_rows = pick_second(owner_table, at, second_back)
    seconds = [second_rows] + [send(second_rows, p) for p in (NEXT, LAST, OPPOSITE)]
    near_rows = [low, high, next_low, next_high, last_low, last_high]
    update = lay(first, (0, 1, 2), near_rows, group, mine.shape)
    update = lay(first, (3,), across, group, mine.shape, update)
    update = lay_second(update, at, seconds)
    return (*stats, update)


def solution(mesh):
    in_specs = (
        P("dp", None, "fsdp", None),
        P(("dp", "fsdp"), None, None),
        P(("dp", "fsdp"), None, None),
        P(("dp", "fsdp"), None, None),
        P(("dp", "fsdp"), None, None),
        P(),
        P("dp", "fsdp"),
    )
    out_specs = (
        P(("dp", "fsdp"), None, None),
        P(("dp", "fsdp"), None, None),
        P(None, "fsdp", None),
    )
    return jax.shard_map(local, mesh=mesh, in_specs=in_specs, out_specs=out_specs, check_vma=False)
```

time: 125 us -> 123 us (0.984)
  local copies, waits for them, and re-layouts: 3.2 us -> 0.01 us
  Pallas kernels: 17.3 us -> 19.9 us
    unnamed x10 -> x6, local copies, waits for them, and re-layouts: 3.2 us -> 0.01 us
    pallas_call x1, Pallas kernels: 3.53 us -> 5.61 us  [new_statistics(): pl.pallas_call(kernel, out_shape=[shape(*stats_left.shape, dtype=F32)] *...]
    ppermute x15, waiting for transfers between devices: 11.3 us -> 9.42 us  [local(): send = lambda pieces, pairs: lax.ppermute(pieces, 'dp', pairs)]
    pallas_call x7 -> x8, Pallas kernels: 7.97 us -> 8.95 us  [call(): pl.pallas_call(kernel, out_shape=outs, in_specs=in_specs, out_specs=[VMEM...]
    pallas_call x3 -> x2, Pallas kernels: 3.83 us -> 3.3 us  [lay(): pl.pallas_call(kernel, out_shape=shape(*update_shape), in_specs=[SMEM] +...]
  transfers between devices with their start and end apart: 16 -> 16, of which waited for: 6 -> 6; matrix products, arithmetic and copies ran while one was open for 0% -> 0% of each run, Pallas kernels for 9% -> 12%
where the time goes in v5:
time: 123 us
  blocking collectives  65.3 us (53%)
  starting transfers between devices  22.5 us (18%)
  Pallas kernels  19.9 us (16%)
  waiting for transfers between devices  13.8 us (11%)
  between operations  1.6 us (1%)
    all_to_all x2, blocking collectives, local(): exchange = lambda pieces: lax.all_to_all(pieces, 'fsdp', 0, 0, tiled=True)  65.3 us
    ppermute x15, starting transfers between devices, local(): send = lambda pieces, pairs: lax.ppermute(pieces, 'dp', pairs)  16.2 us
    ppermute x15, waiting for transfers between devices, local(): send = lambda pieces, pairs: lax.ppermute(pieces, 'dp', pairs)  9.42 us
    pallas_call x8, Pallas kernels, call(): pl.pallas_call(kernel, out_shape=outs, in_specs=in_specs, out_specs=[VMEM...  8.95 us
    all_to_all x1, starting transfers between devices, local(): exchange = lambda pieces: lax.all_to_all(pieces, 'fsdp', 0, 0, tiled=True)  6.28 us
    pallas_call x1, Pallas kernels, new_statistics(): pl.pallas_call(kernel, out_shape=[shape(*stats_left.shape, dtype=F32)] *...  5.61 us
    all_to_all x1, waiting for transfers between devices, local(): exchange = lambda pieces: lax.all_to_all(pieces, 'fsdp', 0, 0, tiled=True)  4.33 us
    pallas_call x2, Pallas kernels, lay(): pl.pallas_call(kernel, out_shape=shape(*update_shape), in_specs=[SMEM] +...  3.3 us
  transfers between devices with their start and end apart: 16, of which 6 were waited for; matrix products, arithmetic and copies ran while one was open for 0% of the time, Pallas kernels for 12%

profile of v5, /device:TPU:1, one launch (start us, length us, event | category | flops | bytes accessed | tf_op | source)
XLA Modules:
  0.0 123.0 jit_solution(9690608463738831350)
XLA Ops:
  0.6 1.1 far_sends.1
  1.7 2.2 %collective-permute-start.2 = (bf16[32,8,512]{2,1,0:T(8,128)(2,1)S(1)}, bf16[32,8,512]{2,1,0:T(8,128)(2,1)S(1)}, u32[]{:S(2)}, u32[]{:S(2)}) collective-permute-start(bf16[32,8,512]{2,1,0:T(8,128)(2,1)S(1)} %get-tuple-element.41), channel_id=1, source_target_pairs={{0,64},{64,0},{128,192},{192,128},{1,65},{65,1},{129,193},{193,129... | collective-permute-start | bytes 786440 | tf_op jit(solution)/shard_map/ppermute | solution.py:326
  3.9 1.9 %collective-permute-start.3 = (bf16[32,8,512]{2,1,0:T(8,128)(2,1)S(1)}, bf16[32,8,512]{2,1,0:T(8,128)(2,1)S(1)}, u32[]{:S(2)}, u32[]{:S(2)}) collective-permute-start(bf16[32,8,512]{2,1,0:T(8,128)(2,1)S(1)} %get-tuple-element.42), channel_id=1, source_target_pairs={{0,192},{64,128},{128,64},{192,0},{1,193},{65,129},{129,65},{193,1... | collective-permute-start | bytes 786440 | tf_op jit(solution)/shard_map/ppermute | solution.py:326
  5.8 1.0 near_sends.1
  6.9 0.5 collective-permute-start
  7.3 0.6 collective-permute-start.1
  8.0 1.2 kept.1
  9.2 0.0 copy-done.2
  9.2 2.0 %block_lists.1 = (s32[256]{0:T(256)S(1)}, s32[64]{0:T(128)S(1)}) custom-call(s32[256]{0:T(256)S(1)} %copy-done.2), custom_call_target="tpu_custom_call" | custom-call | tf_op jit(solution)/shard_map/block_lists/pallas_call | solution.py:30
  11.2 0.0 collective-permute-done.2.low_got
  11.2 0.5 collective-permute-done.3.high_got
  11.7 0.1 partial.1
  11.8 2.3 %collective-permute-start.4 = (bf16[32,8,512]{2,1,0:T(8,128)(2,1)S(1)}, bf16[32,8,512]{2,1,0:T(8,128)(2,1)S(1)}, u32[]{:S(2)}, u32[]{:S(2)}) collective-permute-start(bf16[32,8,512]{2,1,0:T(8,128)(2,1)S(1)} %get-tuple-element.43), channel_id=1, source_target_pairs={{0,192},{64,128},{128,64},{192,0},{1,193},{65,129},{129,65},{193,1... | collective-permute-start | bytes 786440 | tf_op jit(solution)/shard_map/ppermute | solution.py:326
  14.1 0.0 collective-permute-start.5
  14.1 1.2 %collective-permute-done.refs_0_ = bf16[32,8,512]{2,1,0:T(8,128)(2,1)S(1)} collective-permute-done((bf16[32,8,512]{2,1,0:T(8,128)(2,1)S(1)}, bf16[32,8,512]{2,1,0:T(8,128)(2,1)S(1)}, u32[]{:S(2)}, u32[]{:S(2)}) %collective-permute-start) | collective-permute-done | bytes 262176 | tf_op jit(solution)/shard_map/ppermute | solution.py:326
  15.3 2.0 %collective-permute-done.1.refs_1_ = bf16[32,8,512]{2,1,0:T(8,128)(2,1)S(1)} collective-permute-done((bf16[32,8,512]{2,1,0:T(8,128)(2,1)S(1)}, bf16[32,8,512]{2,1,0:T(8,128)(2,1)S(1)}, u32[]{:S(2)}, u32[]{:S(2)}) %collective-permute-start.1) | collective-permute-done | bytes 262176 | tf_op jit(solution)/shard_map/ppermute | solution.py:326
  17.3 5.6 %collective-permute-done.4.refs_2_ = bf16[32,8,512]{2,1,0:T(8,128)(2,1)S(1)} collective-permute-done((bf16[32,8,512]{2,1,0:T(8,128)(2,1)S(1)}, bf16[32,8,512]{2,1,0:T(8,128)(2,1)S(1)}, u32[]{:S(2)}, u32[]{:S(2)}) %collective-permute-start.4) | collective-permute-done | bytes 262176 | tf_op jit(solution)/shard_map/ppermute | solution.py:326
  22.9 0.0 collective-permute-done.5.refs_3_
  22.9 0.9 mean.1
  23.8 42.0 %all_to_all.15 = bf16[64,8,1024]{2,1,0:T(8,128)(2,1)S(1)} all-to-all(bf16[64,8,1024]{2,1,0:T(8,128)(2,1)S(1)} %mean.1), channel_id=1, replica_groups=mesh['dp'=4,'fsdp'=64] {'fsdp'}, dimensions={0} | all-to-all | bytes 2097152 | tf_op jit(solution)/shard_map/all_to_all | solution.py:327
  65.8 1.9 %direction.1 = (bf16[512,512]{1,0:T(8,128)(2,1)S(1)}, bf16[512,512]{1,0:T(8,128)(2,1)}) custom-call(bf16[512,1024]{1,0:T(8,128)(2,1)S(1)} %bitcast.6, bf16[2,512,512]{2,1,0:T(8,128)(2,1)S(1)} %copy-done, bf16[2,512,512]{2,1,0:T(8,128)(2,1)S(1)} %copy-done.1), custom_call_target="tpu_custom_call" | custom-call | tf_op jit(solution)/shard_map/direction/pallas_call | solution.py:30
  67.7 23.3 %all_to_all.16.pieces_ref = bf16[64,8,512]{2,1,0:T(8,128)(2,1)S(1)} all-to-all(bf16[64,8,512]{2,1,0:T(8,128)(2,1)S(1)} %bitcast.8), channel_id=1, replica_groups=mesh['dp'=4,'fsdp'=64] {'fsdp'}, dimensions={0} | all-to-all | bytes 1048576 | tf_op jit(solution)/shard_map/all_to_all | solution.py:327
  91.0 6.3 %all-to-all-start.2 = ((bf16[64,8,512]{2,1,0:T(8,128)(2,1)}), bf16[64,8,512]{2,1,0:T(8,128)(2,1)S(1)}, u32[]{:S(2)}, u32[]{:S(2)}) async-start(bf16[64,8,512]{2,1,0:T(8,128)(2,1)} %bitcast.4), calls=%async_computation.2 | async-start | bytes 1048576 | tf_op jit(solution)/shard_map/all_to_all | solution.py:327
  97.3 0.7 pick_first.1
  98.1 0.1 collective-permute-start.7
  98.2 2.0 %collective-permute-start.6 = (bf16[28,8,512]{2,1,0:T(8,128)(2,1)S(1)}, bf16[28,8,512]{2,1,0:T(8,128)(2,1)S(1)}, u32[]{:S(2)}, u32[]{:S(2)}) collective-permute-start(bf16[28,8,512]{2,1,0:T(8,128)(2,1)S(1)} %get-tuple-element.48.refs_0_), channel_id=1, source_target_pairs={{0,192},{64,128},{128,64},{192,0},{1,193},{65,129},{129,65},{193,1... | collective-permute-start | bytes 688136 | tf_op jit(solution)/shard_map/ppermute | solution.py:326
  100.8 0.9 collective-permute-start.9
  101.7 0.2 collective-permute-start.8
  101.8 5.6 %statistics.1 = (f32[2,512,512]{2,1,0:T(8,128)}, f32[2,512,512]{2,1,0:T(8,128)}) custom-call(s32[1]{0:T(128)} %bitcast.5.counts_ref, bf16[512,1024]{1,0:T(8,128)(2,1)S(1)} %bitcast.7, f32[2,512,512]{2,1,0:T(8,128)} %left_ref.3, f32[2,512,512]{2,1,0:T(8,128)} %right_ref.3), custom_call_target="tpu_custom_call" | custom-call | flops 1073741824 | bytes 8388608 | tf_op jit(solution)/shard_map/statistics/pallas_call | solution.py:305
  107.4 0.0 collective-permute-done.7.refs_3_
  107.4 0.0 collective-permute-done.6.refs_4_
  107.4 2.2 %collective-permute-start.11 = (bf16[28,8,512]{2,1,0:T(8,128)(2,1)S(1)}, bf16[28,8,512]{2,1,0:T(8,128)(2,1)S(1)}, u32[]{:S(2)}, u32[]{:S(2)}) collective-permute-start(bf16[28,8,512]{2,1,0:T(8,128)(2,1)S(1)} %collective-permute-done.7.refs_3_), channel_id=1, source_target_pairs={{0,192},{64,128},{128,64},{192,0},{1,193},{65,129},{129,65},{193,1... | collective-permute-start | bytes 688136 | tf_op jit(solution)/shard_map/ppermute | solution.py:326
  109.6 0.7 collective-permute-start.10
  110.3 4.3 %all-to-all-done.2.pieces_ref = bf16[64,8,512]{2,1,0:T(8,128)(2,1)S(1)} async-done(((bf16[64,8,512]{2,1,0:T(8,128)(2,1)}), bf16[64,8,512]{2,1,0:T(8,128)(2,1)S(1)}, u32[]{:S(2)}, u32[]{:S(2)}) %all-to-all-start.2) | async-done | bytes 524320 | tf_op jit(solution)/shard_map/all_to_all | solution.py:327
  114.7 0.7 pick_second.1.refs_0_
  115.4 1.5 %collective-permute-start.14 = (bf16[8,8,512]{2,1,0:T(8,128)(2,1)S(1)}, bf16[8,8,512]{2,1,0:T(8,128)(2,1)S(1)}, u32[]{:S(2)}, u32[]{:S(2)}) collective-permute-start(bf16[8,8,512]{2,1,0:T(8,128)(2,1)S(1)} %pick_second.1.refs_0_), channel_id=1, source_target_pairs={{0,128},{64,192},{128,0},{192,64},{1,129},{65,193},{129,1},{193,65... | collective-permute-start | bytes 196616 | tf_op jit(solution)/shard_map/ppermute | solution.py:326
  116.9 0.0 collective-permute-done.9.refs_5_
  116.9 0.6 collective-permute-start.13
  117.5 0.0 collective-permute-done.8.refs_2_
  117.5 0.6 collective-permute-start.12
  118.1 1.8 %lay.2.refs_0_ = bf16[256,8,512]{2,1,0:T(8,128)(2,1)} custom-call(s32[256]{0:T(256)S(1)} %get-tuple-element.35.first_ref, bf16[28,8,512]{2,1,0:T(8,128)(2,1)S(1)} %get-tuple-element.48.refs_0_, bf16[28,8,512]{2,1,0:T(8,128)(2,1)S(1)} %get-tuple-element.49.refs_1_, bf16[28,8,512]{2,1,0:T(8,128)(2,1)S(1)} %collective-permute-done.8.refs_2_, ...), custom_call_target="tpu_custom_call" | custom-call | tf_op jit(solution)/shard_map/lay/pallas_call | solution.py:237
  120.0 0.0 collective-permute-done.11.refs_2_
  120.0 0.0 collective-permute-done.10.refs_1_
  120.0 1.5 %lay.3._ = bf16[256,8,512]{2,1,0:T(8,128)(2,1)} custom-call(s32[256]{0:T(256)S(1)} %get-tuple-element.35.first_ref, bf16[256,8,512]{2,1,0:T(8,128)(2,1)} %lay.2.refs_0_, bf16[28,8,512]{2,1,0:T(8,128)(2,1)S(1)} %collective-permute-done.10.refs_1_, bf16[28,8,512]{2,1,0:T(8,128)(2,1)S(1)} %collective-permute-done.11.refs_2_), custom_call_target="tpu_custom_call", output_to_operand_aliasing={{}: (1, {})} | custom-call | tf_op jit(solution)/shard_map/lay/pallas_call | solution.py:237
  121.5 0.0 collective-permute-done.14.refs_3_
  121.5 0.1 collective-permute-done.13.refs_2_
  121.6 0.0 collective-permute-done.12.refs_1_
  121.6 1.3 %lay_second.1 = bf16[256,8,512]{2,1,0:T(8,128)(2,1)} custom-call(s32[64]{0:T(128)S(1)} %get-tuple-element.55.at_ref, bf16[256,8,512]{2,1,0:T(8,128)(2,1)} %lay.3._, bf16[8,8,512]{2,1,0:T(8,128)(2,1)S(1)} %pick_second.1.refs_0_, bf16[8,8,512]{2,1,0:T(8,128)(2,1)S(1)} %collective-permute-done.12.refs_1_, ...), custom_call_target="tpu_custom_call", output_to_operand_aliasing={{}: (1, {})} | custom-call | tf_op jit(solution)/shard_map/lay_second/pallas_call | solution.py:265
  (5 shorter events, 0.0 us)
Async XLA Ops:
  1.7 9.5 %collective-permute-start.2 = (bf16[32,8,512]{2,1,0:T(8,128)(2,1)S(1)}, bf16[32,8,512]{2,1,0:T(8,128)(2,1)S(1)}, u32[]{:S(2)}, u32[]{:S(2)}) collective-permute-start(bf16[32,8,512]{2,1,0:T(8,128)(2,1)S(1)} %get-tuple-element.41), channel_id=1, source_target_pairs={{0,64},{64,0},{128,192},{192,128},{1,65},{65,1},{129,193},{193,129... | collective-permute-start | bytes 786440 | tf_op jit(solution)/shard_map/ppermute | solution.py:326
  3.9 5.3 %copy-start.2 = (s32[256]{0:T(256)S(1)}, s32[256]{0:T(256)}, u32[]{:S(2)}) copy-start(s32[256]{0:T(256)} %table_ref.7) | copy-start | bytes 3076
  3.9 7.8 %collective-permute-start.3 = (bf16[32,8,512]{2,1,0:T(8,128)(2,1)S(1)}, bf16[32,8,512]{2,1,0:T(8,128)(2,1)S(1)}, u32[]{:S(2)}, u32[]{:S(2)}) collective-permute-start(bf16[32,8,512]{2,1,0:T(8,128)(2,1)S(1)} %get-tuple-element.42), channel_id=1, source_target_pairs={{0,192},{64,128},{128,64},{192,0},{1,193},{65,129},{129,65},{193,1... | collective-permute-start | bytes 786440 | tf_op jit(solution)/shard_map/ppermute | solution.py:326
  6.9 8.5 %collective-permute-start = (bf16[32,8,512]{2,1,0:T(8,128)(2,1)S(1)}, bf16[32,8,512]{2,1,0:T(8,128)(2,1)S(1)}, u32[]{:S(2)}, u32[]{:S(2)}) collective-permute-start(bf16[32,8,512]{2,1,0:T(8,128)(2,1)S(1)} %get-tuple-element.37), channel_id=1, source_target_pairs={{0,64},{64,0},{128,192},{192,128},{1,65},{65,1},{129,193},{193,129... | collective-permute-start | bytes 786440 | tf_op jit(solution)/shard_map/ppermute | solution.py:326
  7.3 10.0 %collective-permute-start.1 = (bf16[32,8,512]{2,1,0:T(8,128)(2,1)S(1)}, bf16[32,8,512]{2,1,0:T(8,128)(2,1)S(1)}, u32[]{:S(2)}, u32[]{:S(2)}) collective-permute-start(bf16[32,8,512]{2,1,0:T(8,128)(2,1)S(1)} %get-tuple-element.38), channel_id=1, source_target_pairs={{0,192},{64,128},{128,64},{192,0},{1,193},{65,129},{129,65},{193,1... | collective-permute-start | bytes 786440 | tf_op jit(solution)/shard_map/ppermute | solution.py:326
  11.8 11.1 %collective-permute-start.4 = (bf16[32,8,512]{2,1,0:T(8,128)(2,1)S(1)}, bf16[32,8,512]{2,1,0:T(8,128)(2,1)S(1)}, u32[]{:S(2)}, u32[]{:S(2)}) collective-permute-start(bf16[32,8,512]{2,1,0:T(8,128)(2,1)S(1)} %get-tuple-element.43), channel_id=1, source_target_pairs={{0,192},{64,128},{128,64},{192,0},{1,193},{65,129},{129,65},{193,1... | collective-permute-start | bytes 786440 | tf_op jit(solution)/shard_map/ppermute | solution.py:326
  14.1 8.8 %collective-permute-start.5 = (bf16[32,8,512]{2,1,0:T(8,128)(2,1)S(1)}, bf16[32,8,512]{2,1,0:T(8,128)(2,1)S(1)}, u32[]{:S(2)}, u32[]{:S(2)}) collective-permute-start(bf16[32,8,512]{2,1,0:T(8,128)(2,1)S(1)} %get-tuple-element.44), channel_id=1, source_target_pairs={{0,64},{64,0},{128,192},{192,128},{1,65},{65,1},{129,193},{193,129... | collective-permute-start | bytes 786440 | tf_op jit(solution)/shard_map/ppermute | solution.py:326
  22.9 42.9 %copy-start = (bf16[2,512,512]{2,1,0:T(8,128)(2,1)S(1)}, bf16[2,512,512]{2,1,0:T(8,128)(2,1)}, u32[]{:S(2)}) copy-start(bf16[2,512,512]{2,1,0:T(8,128)(2,1)} %left_ref.2) | copy-start | bytes 3145732
  22.9 42.9 %copy-start.1 = (bf16[2,512,512]{2,1,0:T(8,128)(2,1)S(1)}, bf16[2,512,512]{2,1,0:T(8,128)(2,1)}, u32[]{:S(2)}) copy-start(bf16[2,512,512]{2,1,0:T(8,128)(2,1)} %right_ref.2) | copy-start | bytes 3145732
  91.0 23.6 %all-to-all-start.2 = ((bf16[64,8,512]{2,1,0:T(8,128)(2,1)}), bf16[64,8,512]{2,1,0:T(8,128)(2,1)S(1)}, u32[]{:S(2)}, u32[]{:S(2)}) async-start(bf16[64,8,512]{2,1,0:T(8,128)(2,1)} %bitcast.4), calls=%async_computation.2 | async-start | bytes 1048576 | tf_op jit(solution)/shard_map/all_to_all | solution.py:327
  98.1 9.4 %collective-permute-start.7 = (bf16[28,8,512]{2,1,0:T(8,128)(2,1)S(1)}, bf16[28,8,512]{2,1,0:T(8,128)(2,1)S(1)}, u32[]{:S(2)}, u32[]{:S(2)}) collective-permute-start(bf16[28,8,512]{2,1,0:T(8,128)(2,1)S(1)} %get-tuple-element.49.refs_1_), channel_id=1, source_target_pairs={{0,64},{64,0},{128,192},{192,128},{1,65},{65,1},{129,193},{193,129... | collective-permute-start | bytes 688136 | tf_op jit(solution)/shard_map/ppermute | solution.py:326
  98.2 9.3 %collective-permute-start.6 = (bf16[28,8,512]{2,1,0:T(8,128)(2,1)S(1)}, bf16[28,8,512]{2,1,0:T(8,128)(2,1)S(1)}, u32[]{:S(2)}, u32[]{:S(2)}) collective-permute-start(bf16[28,8,512]{2,1,0:T(8,128)(2,1)S(1)} %get-tuple-element.48.refs_0_), channel_id=1, source_target_pairs={{0,192},{64,128},{128,64},{192,0},{1,193},{65,129},{129,65},{193,1... | collective-permute-start | bytes 688136 | tf_op jit(solution)/shard_map/ppermute | solution.py:326
  100.8 16.1 %collective-permute-start.9 = (bf16[28,8,512]{2,1,0:T(8,128)(2,1)S(1)}, bf16[28,8,512]{2,1,0:T(8,128)(2,1)S(1)}, u32[]{:S(2)}, u32[]{:S(2)}) collective-permute-start(bf16[28,8,512]{2,1,0:T(8,128)(2,1)S(1)} %get-tuple-element.49.refs_1_), channel_id=1, source_target_pairs={{0,192},{64,128},{128,64},{192,0},{1,193},{65,129},{129,65},{193,1... | collective-permute-start | bytes 688136 | tf_op jit(solution)/shard_map/ppermute | solution.py:326
  101.7 15.8 %collective-permute-start.8 = (bf16[28,8,512]{2,1,0:T(8,128)(2,1)S(1)}, bf16[28,8,512]{2,1,0:T(8,128)(2,1)S(1)}, u32[]{:S(2)}, u32[]{:S(2)}) collective-permute-start(bf16[28,8,512]{2,1,0:T(8,128)(2,1)S(1)} %get-tuple-element.48.refs_0_), channel_id=1, source_target_pairs={{0,64},{64,0},{128,192},{192,128},{1,65},{65,1},{129,193},{193,129... | collective-permute-start | bytes 688136 | tf_op jit(solution)/shard_map/ppermute | solution.py:326
  107.4 12.5 %collective-permute-start.11 = (bf16[28,8,512]{2,1,0:T(8,128)(2,1)S(1)}, bf16[28,8,512]{2,1,0:T(8,128)(2,1)S(1)}, u32[]{:S(2)}, u32[]{:S(2)}) collective-permute-start(bf16[28,8,512]{2,1,0:T(8,128)(2,1)S(1)} %collective-permute-done.7.refs_3_), channel_id=1, source_target_pairs={{0,192},{64,128},{128,64},{192,0},{1,193},{65,129},{129,65},{193,1... | collective-permute-start | bytes 688136 | tf_op jit(solution)/shard_map/ppermute | solution.py:326
  109.6 10.3 %collective-permute-start.10 = (bf16[28,8,512]{2,1,0:T(8,128)(2,1)S(1)}, bf16[28,8,512]{2,1,0:T(8,128)(2,1)S(1)}, u32[]{:S(2)}, u32[]{:S(2)}) collective-permute-start(bf16[28,8,512]{2,1,0:T(8,128)(2,1)S(1)} %collective-permute-done.6.refs_4_), channel_id=1, source_target_pairs={{0,64},{64,0},{128,192},{192,128},{1,65},{65,1},{129,193},{193,129... | collective-permute-start | bytes 688136 | tf_op jit(solution)/shard_map/ppermute | solution.py:326
  115.4 6.1 %collective-permute-start.14 = (bf16[8,8,512]{2,1,0:T(8,128)(2,1)S(1)}, bf16[8,8,512]{2,1,0:T(8,128)(2,1)S(1)}, u32[]{:S(2)}, u32[]{:S(2)}) collective-permute-start(bf16[8,8,512]{2,1,0:T(8,128)(2,1)S(1)} %pick_second.1.refs_0_), channel_id=1, source_target_pairs={{0,128},{64,192},{128,0},{192,64},{1,129},{65,193},{129,1},{193,65... | collective-permute-start | bytes 196616 | tf_op jit(solution)/shard_map/ppermute | solution.py:326
  116.9 4.7 %collective-permute-start.13 = (bf16[8,8,512]{2,1,0:T(8,128)(2,1)S(1)}, bf16[8,8,512]{2,1,0:T(8,128)(2,1)S(1)}, u32[]{:S(2)}, u32[]{:S(2)}) collective-permute-start(bf16[8,8,512]{2,1,0:T(8,128)(2,1)S(1)} %pick_second.1.refs_0_), channel_id=1, source_target_pairs={{0,192},{64,128},{128,64},{192,0},{1,193},{65,129},{129,65},{193,1... | collective-permute-start | bytes 196616 | tf_op jit(solution)/shard_map/ppermute | solution.py:326
  117.5 4.1 %collective-permute-start.12 = (bf16[8,8,512]{2,1,0:T(8,128)(2,1)S(1)}, bf16[8,8,512]{2,1,0:T(8,128)(2,1)S(1)}, u32[]{:S(2)}, u32[]{:S(2)}) collective-permute-start(bf16[8,8,512]{2,1,0:T(8,128)(2,1)S(1)} %pick_second.1.refs_0_), channel_id=1, source_target_pairs={{0,64},{64,0},{128,192},{192,128},{1,65},{65,1},{129,193},{193,129... | collective-permute-start | bytes 196616 | tf_op jit(solution)/shard_map/ppermute | solution.py:326

commit v6 on v5

--- a/solution.py
+++ b/solution.py
@@ -130,17 +130,20 @@
     size = left.shape[1]
 
     def kernel(grads_ref, left_ref, right_ref, first, second, room, sem):
-        def scaled(slot):
+        def direction(slot):
             grad = grads_ref[:, slot * size : (slot + 1) * size]
             part = jnp.dot(left_ref[slot], grad, preferred_element_type=F32).astype(BF16)
-            direction = jnp.dot(part, right_ref[slot], preferred_element_type=F32)
-            power = jnp.sum(direction * direction) * (1.0 / (size * size))
-            return (direction * lax.rsqrt(power + EPS)).astype(BF16)
-
-        room[...] = scaled(1)
+            return jnp.dot(part, right_ref[slot], preferred_element_type=F32)
+
+        def scaled(value):
+            power = jnp.sum(value * value) * (1.0 / (size * size))
+            return (value * lax.rsqrt(power + EPS)).astype(BF16)
+
+        of_second, of_first = direction(1), direction(0)
+        room[...] = scaled(of_second)
         copy = pltpu.make_async_copy(room, second, sem)
         copy.start()
-        first[...] = scaled(0)
+        first[...] = scaled(of_first)
         copy.wait()
 
     outs = [shape(size, size)] * 2

time: 123 us -> 123 us (level)
  no operation moved by 1% of the time
where the time goes in v6:
time: 123 us
  blocking collectives  65.3 us (53%)
  starting transfers between devices  22.5 us (18%)
  Pallas kernels  19.9 us (16%)
  waiting for transfers between devices  13.8 us (11%)
  between operations  1.6 us (1%)
    all_to_all x2, blocking collectives, local(): exchange = lambda pieces: lax.all_to_all(pieces, 'fsdp', 0, 0, tiled=True)  65.3 us
    ppermute x15, starting transfers between devices, local(): send = lambda pieces, pairs: lax.ppermute(pieces, 'dp', pairs)  16.2 us
    ppermute x15, waiting for transfers between devices, local(): send = lambda pieces, pairs: lax.ppermute(pieces, 'dp', pairs)  9.42 us
    pallas_call x8, Pallas kernels, call(): pl.pallas_call(kernel, out_shape=outs, in_specs=in_specs, out_specs=[VMEM...  8.95 us
    all_to_all x1, starting transfers between devices, local(): exchange = lambda pieces: lax.all_to_all(pieces, 'fsdp', 0, 0, tiled=True)  6.28 us
    pallas_call x1, Pallas kernels, new_statistics(): pl.pallas_call(kernel, out_shape=[shape(*stats_left.shape, dtype=F32)] *...  5.61 us
    all_to_all x1, waiting for transfers between devices, local(): exchange = lambda pieces: lax.all_to_all(pieces, 'fsdp', 0, 0, tiled=True)  4.33 us
    pallas_call x2, Pallas kernels, lay(): pl.pallas_call(kernel, out_shape=shape(*update_shape), in_specs=[SMEM] +...  3.3 us
  transfers between devices with their start and end apart: 16, of which 6 were waited for; matrix products, arithmetic and copies ran while one was open for 0% of the time, Pallas kernels for 12%

profile of v6, /device:TPU:1, one launch (start us, length us, event | category | flops | bytes accessed | tf_op | source)
XLA Modules:
  0.0 123.0 jit_solution(4683796411839165274)
XLA Ops:
  0.6 1.1 far_sends.1
  1.7 2.2 %collective-permute-start.2 = (bf16[32,8,512]{2,1,0:T(8,128)(2,1)S(1)}, bf16[32,8,512]{2,1,0:T(8,128)(2,1)S(1)}, u32[]{:S(2)}, u32[]{:S(2)}) collective-permute-start(bf16[32,8,512]{2,1,0:T(8,128)(2,1)S(1)} %get-tuple-element.41), channel_id=1, source_target_pairs={{0,64},{64,0},{128,192},{192,128},{1,65},{65,1},{129,193},{193,129... | collective-permute-start | bytes 786440 | tf_op jit(solution)/shard_map/ppermute | solution.py:329
  3.9 1.9 %collective-permute-start.3 = (bf16[32,8,512]{2,1,0:T(8,128)(2,1)S(1)}, bf16[32,8,512]{2,1,0:T(8,128)(2,1)S(1)}, u32[]{:S(2)}, u32[]{:S(2)}) collective-permute-start(bf16[32,8,512]{2,1,0:T(8,128)(2,1)S(1)} %get-tuple-element.42), channel_id=1, source_target_pairs={{0,192},{64,128},{128,64},{192,0},{1,193},{65,129},{129,65},{193,1... | collective-permute-start | bytes 786440 | tf_op jit(solution)/shard_map/ppermute | solution.py:329
  5.8 1.0 near_sends.1
  6.9 0.5 collective-permute-start
  7.3 0.6 collective-permute-start.1
  8.0 1.2 kept.1
  9.2 0.0 copy-done.2
  9.2 2.0 %block_lists.1 = (s32[256]{0:T(256)S(1)}, s32[64]{0:T(128)S(1)}) custom-call(s32[256]{0:T(256)S(1)} %copy-done.2), custom_call_target="tpu_custom_call" | custom-call | tf_op jit(solution)/shard_map/block_lists/pallas_call | solution.py:30
  11.2 0.0 collective-permute-done.2.low_got
  11.2 0.5 collective-permute-done.3.high_got
  11.7 0.1 partial.1
  11.8 2.3 %collective-permute-start.4 = (bf16[32,8,512]{2,1,0:T(8,128)(2,1)S(1)}, bf16[32,8,512]{2,1,0:T(8,128)(2,1)S(1)}, u32[]{:S(2)}, u32[]{:S(2)}) collective-permute-start(bf16[32,8,512]{2,1,0:T(8,128)(2,1)S(1)} %get-tuple-element.43), channel_id=1, source_target_pairs={{0,192},{64,128},{128,64},{192,0},{1,193},{65,129},{129,65},{193,1... | collective-permute-start | bytes 786440 | tf_op jit(solution)/shard_map/ppermute | solution.py:329
  14.1 0.0 collective-permute-start.5
  14.1 1.2 %collective-permute-done.refs_0_ = bf16[32,8,512]{2,1,0:T(8,128)(2,1)S(1)} collective-permute-done((bf16[32,8,512]{2,1,0:T(8,128)(2,1)S(1)}, bf16[32,8,512]{2,1,0:T(8,128)(2,1)S(1)}, u32[]{:S(2)}, u32[]{:S(2)}) %collective-permute-start) | collective-permute-done | bytes 262176 | tf_op jit(solution)/shard_map/ppermute | solution.py:329
  15.3 2.0 %collective-permute-done.1.refs_1_ = bf16[32,8,512]{2,1,0:T(8,128)(2,1)S(1)} collective-permute-done((bf16[32,8,512]{2,1,0:T(8,128)(2,1)S(1)}, bf16[32,8,512]{2,1,0:T(8,128)(2,1)S(1)}, u32[]{:S(2)}, u32[]{:S(2)}) %collective-permute-start.1) | collective-permute-done | bytes 262176 | tf_op jit(solution)/shard_map/ppermute | solution.py:329
  17.3 5.6 %collective-permute-done.4.refs_2_ = bf16[32,8,512]{2,1,0:T(8,128)(2,1)S(1)} collective-permute-done((bf16[32,8,512]{2,1,0:T(8,128)(2,1)S(1)}, bf16[32,8,512]{2,1,0:T(8,128)(2,1)S(1)}, u32[]{:S(2)}, u32[]{:S(2)}) %collective-permute-start.4) | collective-permute-done | bytes 262176 | tf_op jit(solution)/shard_map/ppermute | solution.py:329
  22.9 0.0 collective-permute-done.5.refs_3_
  22.9 0.9 mean.1
  23.8 42.0 %all_to_all.15 = bf16[64,8,1024]{2,1,0:T(8,128)(2,1)S(1)} all-to-all(bf16[64,8,1024]{2,1,0:T(8,128)(2,1)S(1)} %mean.1), channel_id=1, replica_groups=mesh['dp'=4,'fsdp'=64] {'fsdp'}, dimensions={0} | all-to-all | bytes 2097152 | tf_op jit(solution)/shard_map/all_to_all | solution.py:330
  65.8 1.9 %direction.1 = (bf16[512,512]{1,0:T(8,128)(2,1)S(1)}, bf16[512,512]{1,0:T(8,128)(2,1)}) custom-call(bf16[512,1024]{1,0:T(8,128)(2,1)S(1)} %bitcast.6, bf16[2,512,512]{2,1,0:T(8,128)(2,1)S(1)} %copy-done, bf16[2,512,512]{2,1,0:T(8,128)(2,1)S(1)} %copy-done.1), custom_call_target="tpu_custom_call" | custom-call | tf_op jit(solution)/shard_map/direction/pallas_call | solution.py:30
  67.7 23.3 %all_to_all.16.pieces_ref = bf16[64,8,512]{2,1,0:T(8,128)(2,1)S(1)} all-to-all(bf16[64,8,512]{2,1,0:T(8,128)(2,1)S(1)} %bitcast.8), channel_id=1, replica_groups=mesh['dp'=4,'fsdp'=64] {'fsdp'}, dimensions={0} | all-to-all | bytes 1048576 | tf_op jit(solution)/shard_map/all_to_all | solution.py:330
  91.0 6.3 %all-to-all-start.2 = ((bf16[64,8,512]{2,1,0:T(8,128)(2,1)}), bf16[64,8,512]{2,1,0:T(8,128)(2,1)S(1)}, u32[]{:S(2)}, u32[]{:S(2)}) async-start(bf16[64,8,512]{2,1,0:T(8,128)(2,1)} %bitcast.4), calls=%async_computation.2 | async-start | bytes 1048576 | tf_op jit(solution)/shard_map/all_to_all | solution.py:330
  97.3 0.7 pick_first.1
  98.1 0.1 collective-permute-start.7
  98.2 2.0 %collective-permute-start.6 = (bf16[28,8,512]{2,1,0:T(8,128)(2,1)S(1)}, bf16[28,8,512]{2,1,0:T(8,128)(2,1)S(1)}, u32[]{:S(2)}, u32[]{:S(2)}) collective-permute-start(bf16[28,8,512]{2,1,0:T(8,128)(2,1)S(1)} %get-tuple-element.48.refs_0_), channel_id=1, source_target_pairs={{0,192},{64,128},{128,64},{192,0},{1,193},{65,129},{129,65},{193,1... | collective-permute-start | bytes 688136 | tf_op jit(solution)/shard_map/ppermute | solution.py:329
  100.8 0.9 collective-permute-start.9
  101.7 0.2 collective-permute-start.8
  101.8 5.6 %statistics.1 = (f32[2,512,512]{2,1,0:T(8,128)}, f32[2,512,512]{2,1,0:T(8,128)}) custom-call(s32[1]{0:T(128)} %bitcast.5.counts_ref, bf16[512,1024]{1,0:T(8,128)(2,1)S(1)} %bitcast.7, f32[2,512,512]{2,1,0:T(8,128)} %left_ref.3, f32[2,512,512]{2,1,0:T(8,128)} %right_ref.3), custom_call_target="tpu_custom_call" | custom-call | flops 1073741824 | bytes 8388608 | tf_op jit(solution)/shard_map/statistics/pallas_call | solution.py:308
  107.4 0.0 collective-permute-done.7.refs_3_
  107.4 0.0 collective-permute-done.6.refs_4_
  107.4 2.2 %collective-permute-start.11 = (bf16[28,8,512]{2,1,0:T(8,128)(2,1)S(1)}, bf16[28,8,512]{2,1,0:T(8,128)(2,1)S(1)}, u32[]{:S(2)}, u32[]{:S(2)}) collective-permute-start(bf16[28,8,512]{2,1,0:T(8,128)(2,1)S(1)} %collective-permute-done.7.refs_3_), channel_id=1, source_target_pairs={{0,192},{64,128},{128,64},{192,0},{1,193},{65,129},{129,65},{193,1... | collective-permute-start | bytes 688136 | tf_op jit(solution)/shard_map/ppermute | solution.py:329
  109.6 0.7 collective-permute-start.10
  110.3 4.3 %all-to-all-done.2.pieces_ref = bf16[64,8,512]{2,1,0:T(8,128)(2,1)S(1)} async-done(((bf16[64,8,512]{2,1,0:T(8,128)(2,1)}), bf16[64,8,512]{2,1,0:T(8,128)(2,1)S(1)}, u32[]{:S(2)}, u32[]{:S(2)}) %all-to-all-start.2) | async-done | bytes 524320 | tf_op jit(solution)/shard_map/all_to_all | solution.py:330
  114.7 0.7 pick_second.1.refs_0_
  115.4 1.5 %collective-permute-start.14 = (bf16[8,8,512]{2,1,0:T(8,128)(2,1)S(1)}, bf16[8,8,512]{2,1,0:T(8,128)(2,1)S(1)}, u32[]{:S(2)}, u32[]{:S(2)}) collective-permute-start(bf16[8,8,512]{2,1,0:T(8,128)(2,1)S(1)} %pick_second.1.refs_0_), channel_id=1, source_target_pairs={{0,128},{64,192},{128,0},{192,64},{1,129},{65,193},{129,1},{193,65... | collective-permute-start | bytes 196616 | tf_op jit(solution)/shard_map/ppermute | solution.py:329
  116.9 0.0 collective-permute-done.9.refs_5_
  116.9 0.6 collective-permute-start.13
  117.5 0.0 collective-permute-done.8.refs_2_
  117.5 0.6 collective-permute-start.12
  118.1 1.8 %lay.2.refs_0_ = bf16[256,8,512]{2,1,0:T(8,128)(2,1)} custom-call(s32[256]{0:T(256)S(1)} %get-tuple-element.35.first_ref, bf16[28,8,512]{2,1,0:T(8,128)(2,1)S(1)} %get-tuple-element.48.refs_0_, bf16[28,8,512]{2,1,0:T(8,128)(2,1)S(1)} %get-tuple-element.49.refs_1_, bf16[28,8,512]{2,1,0:T(8,128)(2,1)S(1)} %collective-permute-done.8.refs_2_, ...), custom_call_target="tpu_custom_call" | custom-call | tf_op jit(solution)/shard_map/lay/pallas_call | solution.py:240
  120.0 0.0 collective-permute-done.11.refs_2_
  120.0 0.0 collective-permute-done.10.refs_1_
  120.0 1.5 %lay.3._ = bf16[256,8,512]{2,1,0:T(8,128)(2,1)} custom-call(s32[256]{0:T(256)S(1)} %get-tuple-element.35.first_ref, bf16[256,8,512]{2,1,0:T(8,128)(2,1)} %lay.2.refs_0_, bf16[28,8,512]{2,1,0:T(8,128)(2,1)S(1)} %collective-permute-done.10.refs_1_, bf16[28,8,512]{2,1,0:T(8,128)(2,1)S(1)} %collective-permute-done.11.refs_2_), custom_call_target="tpu_custom_call", output_to_operand_aliasing={{}: (1, {})} | custom-call | tf_op jit(solution)/shard_map/lay/pallas_call | solution.py:240
  121.5 0.0 collective-permute-done.14.refs_3_
  121.5 0.1 collective-permute-done.13.refs_2_
  121.6 0.0 collective-permute-done.12.refs_1_
  121.6 1.3 %lay_second.1 = bf16[256,8,512]{2,1,0:T(8,128)(2,1)} custom-call(s32[64]{0:T(128)S(1)} %get-tuple-element.55.at_ref, bf16[256,8,512]{2,1,0:T(8,128)(2,1)} %lay.3._, bf16[8,8,512]{2,1,0:T(8,128)(2,1)S(1)} %pick_second.1.refs_0_, bf16[8,8,512]{2,1,0:T(8,128)(2,1)S(1)} %collective-permute-done.12.refs_1_, ...), custom_call_target="tpu_custom_call", output_to_operand_aliasing={{}: (1, {})} | custom-call | tf_op jit(solution)/shard_map/lay_second/pallas_call | solution.py:268
  (5 shorter events, 0.0 us)
Async XLA Ops:
  1.7 9.5 %collective-permute-start.2 = (bf16[32,8,512]{2,1,0:T(8,128)(2,1)S(1)}, bf16[32,8,512]{2,1,0:T(8,128)(2,1)S(1)}, u32[]{:S(2)}, u32[]{:S(2)}) collective-permute-start(bf16[32,8,512]{2,1,0:T(8,128)(2,1)S(1)} %get-tuple-element.41), channel_id=1, source_target_pairs={{0,64},{64,0},{128,192},{192,128},{1,65},{65,1},{129,193},{193,129... | collective-permute-start | bytes 786440 | tf_op jit(solution)/shard_map/ppermute | solution.py:329
  3.9 5.3 %copy-start.2 = (s32[256]{0:T(256)S(1)}, s32[256]{0:T(256)}, u32[]{:S(2)}) copy-start(s32[256]{0:T(256)} %table_ref.7) | copy-start | bytes 3076
  3.9 7.8 %collective-permute-start.3 = (bf16[32,8,512]{2,1,0:T(8,128)(2,1)S(1)}, bf16[32,8,512]{2,1,0:T(8,128)(2,1)S(1)}, u32[]{:S(2)}, u32[]{:S(2)}) collective-permute-start(bf16[32,8,512]{2,1,0:T(8,128)(2,1)S(1)} %get-tuple-element.42), channel_id=1, source_target_pairs={{0,192},{64,128},{128,64},{192,0},{1,193},{65,129},{129,65},{193,1... | collective-permute-start | bytes 786440 | tf_op jit(solution)/shard_map/ppermute | solution.py:329
  6.9 8.5 %collective-permute-start = (bf16[32,8,512]{2,1,0:T(8,128)(2,1)S(1)}, bf16[32,8,512]{2,1,0:T(8,128)(2,1)S(1)}, u32[]{:S(2)}, u32[]{:S(2)}) collective-permute-start(bf16[32,8,512]{2,1,0:T(8,128)(2,1)S(1)} %get-tuple-element.37), channel_id=1, source_target_pairs={{0,64},{64,0},{128,192},{192,128},{1,65},{65,1},{129,193},{193,129... | collective-permute-start | bytes 786440 | tf_op jit(solution)/shard_map/ppermute | solution.py:329
  7.3 10.0 %collective-permute-start.1 = (bf16[32,8,512]{2,1,0:T(8,128)(2,1)S(1)}, bf16[32,8,512]{2,1,0:T(8,128)(2,1)S(1)}, u32[]{:S(2)}, u32[]{:S(2)}) collective-permute-start(bf16[32,8,512]{2,1,0:T(8,128)(2,1)S(1)} %get-tuple-element.38), channel_id=1, source_target_pairs={{0,192},{64,128},{128,64},{192,0},{1,193},{65,129},{129,65},{193,1... | collective-permute-start | bytes 786440 | tf_op jit(solution)/shard_map/ppermute | solution.py:329
  11.8 11.1 %collective-permute-start.4 = (bf16[32,8,512]{2,1,0:T(8,128)(2,1)S(1)}, bf16[32,8,512]{2,1,0:T(8,128)(2,1)S(1)}, u32[]{:S(2)}, u32[]{:S(2)}) collective-permute-start(bf16[32,8,512]{2,1,0:T(8,128)(2,1)S(1)} %get-tuple-element.43), channel_id=1, source_target_pairs={{0,192},{64,128},{128,64},{192,0},{1,193},{65,129},{129,65},{193,1... | collective-permute-start | bytes 786440 | tf_op jit(solution)/shard_map/ppermute | solution.py:329
  14.1 8.8 %collective-permute-start.5 = (bf16[32,8,512]{2,1,0:T(8,128)(2,1)S(1)}, bf16[32,8,512]{2,1,0:T(8,128)(2,1)S(1)}, u32[]{:S(2)}, u32[]{:S(2)}) collective-permute-start(bf16[32,8,512]{2,1,0:T(8,128)(2,1)S(1)} %get-tuple-element.44), channel_id=1, source_target_pairs={{0,64},{64,0},{128,192},{192,128},{1,65},{65,1},{129,193},{193,129... | collective-permute-start | bytes 786440 | tf_op jit(solution)/shard_map/ppermute | solution.py:329
  22.9 42.9 %copy-start = (bf16[2,512,512]{2,1,0:T(8,128)(2,1)S(1)}, bf16[2,512,512]{2,1,0:T(8,128)(2,1)}, u32[]{:S(2)}) copy-start(bf16[2,512,512]{2,1,0:T(8,128)(2,1)} %left_ref.2) | copy-start | bytes 3145732
  22.9 42.9 %copy-start.1 = (bf16[2,512,512]{2,1,0:T(8,128)(2,1)S(1)}, bf16[2,512,512]{2,1,0:T(8,128)(2,1)}, u32[]{:S(2)}) copy-start(bf16[2,512,512]{2,1,0:T(8,128)(2,1)} %right_ref.2) | copy-start | bytes 3145732
  91.0 23.6 %all-to-all-start.2 = ((bf16[64,8,512]{2,1,0:T(8,128)(2,1)}), bf16[64,8,512]{2,1,0:T(8,128)(2,1)S(1)}, u32[]{:S(2)}, u32[]{:S(2)}) async-start(bf16[64,8,512]{2,1,0:T(8,128)(2,1)} %bitcast.4), calls=%async_computation.2 | async-start | bytes 1048576 | tf_op jit(solution)/shard_map/all_to_all | solution.py:330
  98.1 9.4 %collective-permute-start.7 = (bf16[28,8,512]{2,1,0:T(8,128)(2,1)S(1)}, bf16[28,8,512]{2,1,0:T(8,128)(2,1)S(1)}, u32[]{:S(2)}, u32[]{:S(2)}) collective-permute-start(bf16[28,8,512]{2,1,0:T(8,128)(2,1)S(1)} %get-tuple-element.49.refs_1_), channel_id=1, source_target_pairs={{0,64},{64,0},{128,192},{192,128},{1,65},{65,1},{129,193},{193,129... | collective-permute-start | bytes 688136 | tf_op jit(solution)/shard_map/ppermute | solution.py:329
  98.2 9.3 %collective-permute-start.6 = (bf16[28,8,512]{2,1,0:T(8,128)(2,1)S(1)}, bf16[28,8,512]{2,1,0:T(8,128)(2,1)S(1)}, u32[]{:S(2)}, u32[]{:S(2)}) collective-permute-start(bf16[28,8,512]{2,1,0:T(8,128)(2,1)S(1)} %get-tuple-element.48.refs_0_), channel_id=1, source_target_pairs={{0,192},{64,128},{128,64},{192,0},{1,193},{65,129},{129,65},{193,1... | collective-permute-start | bytes 688136 | tf_op jit(solution)/shard_map/ppermute | solution.py:329
  100.8 16.1 %collective-permute-start.9 = (bf16[28,8,512]{2,1,0:T(8,128)(2,1)S(1)}, bf16[28,8,512]{2,1,0:T(8,128)(2,1)S(1)}, u32[]{:S(2)}, u32[]{:S(2)}) collective-permute-start(bf16[28,8,512]{2,1,0:T(8,128)(2,1)S(1)} %get-tuple-element.49.refs_1_), channel_id=1, source_target_pairs={{0,192},{64,128},{128,64},{192,0},{1,193},{65,129},{129,65},{193,1... | collective-permute-start | bytes 688136 | tf_op jit(solution)/shard_map/ppermute | solution.py:329
  101.7 15.8 %collective-permute-start.8 = (bf16[28,8,512]{2,1,0:T(8,128)(2,1)S(1)}, bf16[28,8,512]{2,1,0:T(8,128)(2,1)S(1)}, u32[]{:S(2)}, u32[]{:S(2)}) collective-permute-start(bf16[28,8,512]{2,1,0:T(8,128)(2,1)S(1)} %get-tuple-element.48.refs_0_), channel_id=1, source_target_pairs={{0,64},{64,0},{128,192},{192,128},{1,65},{65,1},{129,193},{193,129... | collective-permute-start | bytes 688136 | tf_op jit(solution)/shard_map/ppermute | solution.py:329
  107.4 12.5 %collective-permute-start.11 = (bf16[28,8,512]{2,1,0:T(8,128)(2,1)S(1)}, bf16[28,8,512]{2,1,0:T(8,128)(2,1)S(1)}, u32[]{:S(2)}, u32[]{:S(2)}) collective-permute-start(bf16[28,8,512]{2,1,0:T(8,128)(2,1)S(1)} %collective-permute-done.7.refs_3_), channel_id=1, source_target_pairs={{0,192},{64,128},{128,64},{192,0},{1,193},{65,129},{129,65},{193,1... | collective-permute-start | bytes 688136 | tf_op jit(solution)/shard_map/ppermute | solution.py:329
  109.6 10.3 %collective-permute-start.10 = (bf16[28,8,512]{2,1,0:T(8,128)(2,1)S(1)}, bf16[28,8,512]{2,1,0:T(8,128)(2,1)S(1)}, u32[]{:S(2)}, u32[]{:S(2)}) collective-permute-start(bf16[28,8,512]{2,1,0:T(8,128)(2,1)S(1)} %collective-permute-done.6.refs_4_), channel_id=1, source_target_pairs={{0,64},{64,0},{128,192},{192,128},{1,65},{65,1},{129,193},{193,129... | collective-permute-start | bytes 688136 | tf_op jit(solution)/shard_map/ppermute | solution.py:329
  115.4 6.1 %collective-permute-start.14 = (bf16[8,8,512]{2,1,0:T(8,128)(2,1)S(1)}, bf16[8,8,512]{2,1,0:T(8,128)(2,1)S(1)}, u32[]{:S(2)}, u32[]{:S(2)}) collective-permute-start(bf16[8,8,512]{2,1,0:T(8,128)(2,1)S(1)} %pick_second.1.refs_0_), channel_id=1, source_target_pairs={{0,128},{64,192},{128,0},{192,64},{1,129},{65,193},{129,1},{193,65... | collective-permute-start | bytes 196616 | tf_op jit(solution)/shard_map/ppermute | solution.py:329
  116.9 4.7 %collective-permute-start.13 = (bf16[8,8,512]{2,1,0:T(8,128)(2,1)S(1)}, bf16[8,8,512]{2,1,0:T(8,128)(2,1)S(1)}, u32[]{:S(2)}, u32[]{:S(2)}) collective-permute-start(bf16[8,8,512]{2,1,0:T(8,128)(2,1)S(1)} %pick_second.1.refs_0_), channel_id=1, source_target_pairs={{0,192},{64,128},{128,64},{192,0},{1,193},{65,129},{129,65},{193,1... | collective-permute-start | bytes 196616 | tf_op jit(solution)/shard_map/ppermute | solution.py:329
  117.5 4.1 %collective-permute-start.12 = (bf16[8,8,512]{2,1,0:T(8,128)(2,1)S(1)}, bf16[8,8,512]{2,1,0:T(8,128)(2,1)S(1)}, u32[]{:S(2)}, u32[]{:S(2)}) collective-permute-start(bf16[8,8,512]{2,1,0:T(8,128)(2,1)S(1)} %pick_second.1.refs_0_), channel_id=1, source_target_pairs={{0,64},{64,0},{128,192},{192,128},{1,65},{65,1},{129,193},{193,129... | collective-permute-start | bytes 196616 | tf_op jit(solution)/shard_map/ppermute | solution.py:329
